TPU v7x, 32 devices: a whole 2x2x4 slice. The times are simulated.
32 devices in a mesh: dop: 8 (over z, y), rng: 4 (over x, core).
Axes of the slice: x: 2, y: 2, z: 4, core: 2. Of those that a mesh axis runs over, the one named last changes fastest.
Arguments:
- raw_echo: float32 [2, 512, 512, 128], P(None, 'dop', 'rng'), may hold values from -6 to 6
- replica: float32 [2, 64], replicated, may hold values from -0.5 to 0.5
- beam_weights: bfloat16 [2, 512, 192], replicated, may hold values from -0.1875 to 0.1875
- pivots: int32 [128, 192], replicated, may hold values from 0 to 191, each once within a row
- owner_counts: int32 [8], replicated, may hold values from 1 to 32, 128 in all
- train_gates: int32 [128, 256], P(None, 'rng'), may hold values from 0 to 511, as said below
Outputs:
- factor: float32 [256, 384, 384], P('dop', 'rng')
Inputs may be any that keep to these rules, and one draw needn't show every extreme that they name: Owner o holds the run of owner_counts[o] consecutive Doppler bins that follows the bins of the owners below it; the counts sum to 128, and the largest is exactly 32 in every draw. `pivots`: each row is a permutation of 0 to 191. `train_gates`: in each row, columns r * 64 to (r + 1) * 64 - 1 hold distinct gates of range block r, that is of r * 128 to (r + 1) * 128 - 1.
All inputs are finite; a program needn't handle non-finite values.
Results may differ from a plain program's by a relative error of at most 0.005.
Values may be sent and summed in bfloat16 or wider, within the bound.
No kernel may reach another device: no remote copies, remote signals or barrier semaphores. Data moves between devices by JAX's collectives and lax.ppermute only.
A program may use at most 128 MiB of HBM per device.

v0:
```python
import functools
import math

import jax
import jax.numpy as jnp
from jax import lax
from jax.experimental import pallas as pl
from jax.experimental.pallas import tpu as pltpu
from jax.sharding import PartitionSpec as P

LOADING = 0.25
LANES = 128
PANEL = 32
BF16 = jnp.bfloat16
F32 = jnp.float32
PARAMS = pltpu.CompilerParams(vmem_limit_bytes=48 * 1024 * 1024)


def shifted(array, axis, by):
    count = lax.axis_size(axis)
    pairs = [(i, i + by) for i in range(count) if 0 <= i + by < count]
    return lax.ppermute(array, axis, pairs)


def complex_block(real_part, imag_part):
    upper_row = jnp.stack([real_part, imag_part])
    lower_row = jnp.stack([-imag_part, real_part])
    return jnp.stack([upper_row, lower_row])


def doppler_table(pulse_count):
    pulse_index = jnp.arange(pulse_count, dtype=jnp.int32)
    phase_index = pulse_index[:, None] * pulse_index[None, :] % pulse_count
    angle_table = phase_index.astype(jnp.float32) * (2.0 * math.pi / pulse_count)
    norm_scale = 1.0 / math.sqrt(pulse_count)
    return complex_block(jnp.cos(angle_table) * norm_scale, jnp.sin(angle_table) * norm_scale)


def filter_kernel(replica_ref, out_ref):
    gate_rows, span = out_ref.shape[0] // 2, replica_ref.shape[1]
    banded = [
        pltpu.roll(
            jnp.broadcast_to(replica_ref[part : part + 1, :], (gate_rows, span)),
            0,
            1,
            stride=1,
            stride_axis=0,
        )
        for part in range(2)
    ]
    out_ref[:gate_rows, :span] = banded[0].astype(BF16)
    out_ref[:gate_rows, span:] = banded[1].astype(BF16)
    out_ref[gate_rows:, :span] = (-banded[1]).astype(BF16)
    out_ref[gate_rows:, span:] = banded[0].astype(BF16)


def filter_rows(replica, gate_rows):
    tap_count = replica.shape[1]
    span = -(-(gate_rows + tap_count) // LANES) * LANES
    return pl.pallas_call(
        filter_kernel,
        out_shape=jax.ShapeDtypeStruct((2 * gate_rows, 2 * span), BF16),
        in_specs=[pl.BlockSpec(memory_space=pltpu.VMEM)],
        out_specs=pl.BlockSpec(memory_space=pltpu.VMEM),
        compiler_params=PARAMS,
        name="filter_rows",
    )(jnp.pad(replica, ((0, 0), (0, span - tap_count))))


def rim_kernel(echo_ref, out_ref):
    out_ref[...] = echo_ref[...].astype(BF16)


def rim_rows(raw_echo, rim, chunk, chunks):
    _, ch_local, _, pulses = raw_echo.shape
    shape = (2, ch_local // chunks, rim, pulses)
    return pl.pallas_call(
        rim_kernel,
        out_shape=jax.ShapeDtypeStruct(shape, BF16),
        grid=(1,),
        in_specs=[pl.BlockSpec(shape, lambda i: (0, chunk, 0, 0))],
        out_specs=pl.BlockSpec(shape, lambda i: (0, 0, 0, 0)),
        compiler_params=PARAMS,
        name="rim_rows",
    )(raw_echo)


def spectrum_kernel(rows_ref, table_ref, own_ref, next_ref, out_ref, turned):
    step = pl.program_id(0)
    _, channels, gate_rows, pulses = own_ref.shape
    bins, height, _ = out_ref.shape
    rim = next_ref.shape[2]
    span = rows_ref.shape[1] // 2
    each = range(channels)
    samples = []
    for part in range(2):
        samples += [
            jnp.concatenate([own_ref[part, c] for c in each], axis=1).astype(BF16),
            jnp.concatenate([next_ref[part, c] for c in each], axis=1),
        ]
        if span > gate_rows + rim:
            samples.append(jnp.zeros((span - gate_rows - rim, channels * pulses), BF16))
    samples = jnp.concatenate(samples, axis=0)
    matched = jnp.dot(rows_ref[...], samples, preferred_element_type=F32).astype(BF16)
    halves = [matched[:gate_rows], matched[gate_rows:]]
    stacked = jnp.concatenate(
        [
            jnp.concatenate([half[:, c * pulses : (c + 1) * pulses] for half in halves], axis=1)
            for c in each
        ],
        axis=0,
    )
    spectra = lax.dot_general(
        table_ref[...], stacked, (((1,), (1,)), ((), ())), preferred_element_type=F32
    )
    for part in range(2):
        turned_part = jnp.stack(
            [
                spectra[part * bins : (part + 1) * bins, c * gate_rows : (c + 1) * gate_rows]
                for c in each
            ],
            axis=0,
        )
        place = pl.multiple_of(part * (height // 2) + step * channels, channels)
        turned[:, pl.ds(place, channels), :] = jnp.swapaxes(turned_part, 0, 1)

    @pl.when(step == pl.num_programs(0) - 1)
    def _():
        out_ref[...] = turned[...].astype(BF16)


def form_spectrum(rows, table, raw_echo, next_rows, chunk, chunks):
    _, ch_local, gate_rows, pulses = raw_echo.shape
    channels = ch_local // chunks
    step = math.gcd(channels, 8)
    steps = channels // step
    height = 2 * channels
    bins = table.shape[0] // 2
    return pl.pallas_call(
        spectrum_kernel,
        out_shape=jax.ShapeDtypeStruct((bins, height, gate_rows), BF16),
        grid=(steps,),
        in_specs=[
            pl.BlockSpec(rows.shape, lambda i: (0, 0)),
            pl.BlockSpec(table.shape, lambda i: (0, 0)),
            pl.BlockSpec((2, step, gate_rows, pulses), lambda i: (0, chunk * steps + i, 0, 0)),
            pl.BlockSpec((2, step) + next_rows.shape[2:], lambda i: (0, i, 0, 0)),
        ],
        out_specs=pl.BlockSpec((bins, height, gate_rows), lambda i: (0, 0, 0)),
        scratch_shapes=[pltpu.VMEM((bins, height, gate_rows), F32)],
        compiler_params=PARAMS,
        cost_estimate=pl.CostEstimate(
            flops=2 * rows.size * channels * pulses + 2 * table.size * channels * gate_rows,
            bytes_accessed=8 * channels * gate_rows * pulses,
            transcendentals=0,
        ),
        name="form_spectrum",
    )(rows, table, raw_echo, next_rows)


def owner_count(index_ref, owner):
    return index_ref[2 + owner]


def owner_start(index_ref, owner, owners):
    return index_ref[2 + owners + owner]


def select_kernel(index_ref, gates_ref, *refs, owners, pack):
    *spectrum_refs, out_ref = refs
    bin_count, height, gate_rows = spectrum_refs[0].shape
    some, groups, _, width = out_ref.shape
    half = height // 2
    gate_index = lax.broadcasted_iota(jnp.int32, (pack * gate_rows, width), 0)
    part_index = lax.broadcasted_iota(jnp.int32, (1, width), 1) // (width // pack)
    for inner in range(some):
        start = owner_start(index_ref, pl.program_id(0) * some + inner, owners)
        for group in range(groups):
            bins = [
                jnp.minimum(start + group * pack + part, bin_count - 1) for part in range(pack)
            ]
            gates = gates_ref[pl.ds(bins[0], 1), :]
            for part in range(1, pack):
                gates = jnp.where(part_index == part, gates_ref[pl.ds(bins[part], 1), :], gates)
            chooser = jnp.where(gate_index == gates, 1.0, 0.0).astype(BF16)
            spectra = jnp.concatenate(
                [
                    jnp.concatenate([ref[b, s * half : (s + 1) * half] for b in bins], axis=1)
                    for s in range(2)
                    for ref in spectrum_refs
                ],
                axis=0,
            )
            picked = jnp.dot(spectra, chooser, preferred_element_type=F32)
            out_ref[inner, group] = picked.astype(BF16)


def select_gates(spectra, index, gates, most_slots, owners, pack):
    rows = sum(spectrum.shape[1] for spectrum in spectra)
    gate_rows = spectra[0].shape[2]
    groups = most_slots // pack
    width = gates.shape[1]
    return pl.pallas_call(
        functools.partial(select_kernel, owners=owners, pack=pack),
        out_shape=jax.ShapeDtypeStruct((owners, groups, rows, width), BF16),
        grid=(owners,),
        in_specs=[pl.BlockSpec(memory_space=pltpu.SMEM)]
        + [pl.BlockSpec(memory_space=pltpu.VMEM)] * (1 + len(spectra)),
        out_specs=pl.BlockSpec((1, groups, rows, width), lambda i: (i, 0, 0, 0)),
        compiler_params=PARAMS,
        cost_estimate=pl.CostEstimate(
            flops=2 * owners * groups * pack * rows * gate_rows * width,
            bytes_accessed=owners * groups * rows * width * 2,
            transcendentals=0,
        ),
        name="select_gates",
    )(index, gates, *spectra)


def beam_kernel(index_ref, weights_ref, arrived_ref, *out_refs, first):
    sources, groups, rows, width = arrived_ref.shape
    ranges, share = len(out_refs), out_refs[0].shape[0]
    dof = weights_ref.shape[2]
    half = rows // 2
    for shift, out_ref in enumerate(out_refs):
        lead = lax.rem(index_ref[1] + shift, ranges) * (groups // ranges) + first
        packed = jnp.concatenate(
            [
                arrived_ref[:, lead + g, s * half : (s + 1) * half].reshape(sources * half, width)
                for s in range(2)
                for g in range(share)
            ],
            axis=1,
        )
        by_real, by_imag = [
            lax.dot_general(
                weights_ref[part], packed, (((0,), (0,)), ((), ())), preferred_element_type=F32
            )
            for part in range(2)
        ]
        middle = share * width
        real_part = by_real[:, :middle] + by_imag[:, middle:]
        imag_part = by_real[:, middle:] - by_imag[:, :middle]
        for g in range(share):
            span = slice(g * width, (g + 1) * width)
            out_ref[g, :dof] = real_part[:, span].astype(BF16)
            out_ref[g, dof:] = imag_part[:, span].astype(BF16)


def form_beams(arrived, weights, index, ranges, first, count):
    sources, _, rows, width = arrived.shape
    shape = (count, 2 * weights.shape[2], width)
    return pl.pallas_call(
        functools.partial(beam_kernel, first=first),
        out_shape=[jax.ShapeDtypeStruct(shape, BF16)] * ranges,
        in_specs=[
            pl.BlockSpec(memory_space=pltpu.SMEM),
            pl.BlockSpec(memory_space=pltpu.VMEM),
            pl.BlockSpec(memory_space=pltpu.VMEM),
        ],
        out_specs=[pl.BlockSpec(memory_space=pltpu.VMEM)] * ranges,
        compiler_params=PARAMS,
        cost_estimate=pl.CostEstimate(
            flops=4 * ranges * count * sources * rows * width * weights.shape[2],
            bytes_accessed=arrived.size * 2,
            transcendentals=0,
        ),
        name="form_beams",
    )(index, weights, arrived)


def exchange(arrays, axis):
    count = len(arrays)
    moved = [arrays[0]]
    for shift in range(1, count):
        pairs = [(i, (i + shift) % count) for i in range(count)]
        moved.append(lax.ppermute(arrays[shift], axis, pairs))
    return moved


def split_terms(array):
    high = array.astype(BF16)
    return high, (array - high.astype(F32)).astype(BF16)


def left_terms(array):
    high, low = split_terms(array)
    high, low = high.astype(F32), low.astype(F32)
    return jnp.concatenate([high, high, low], axis=0).T.astype(BF16)


def right_terms(array):
    high, low = split_terms(array)
    return jnp.concatenate([high, low, high], axis=0)


def product(left, right):
    return jnp.dot(left, right, preferred_element_type=F32)


def loaded_covariance(beams, pivot_row, part, pack, count_rows):
    dof = pivot_row.shape[1]
    width = beams[0].shape[1] // pack
    hot = lax.broadcasted_iota(jnp.int32, (dof, dof), 0) == pivot_row
    hot = jnp.where(hot, 1.0, 0.0).astype(BF16)
    own = jnp.concatenate([b[:, part * width : (part + 1) * width] for b in beams], axis=1)
    picked = [
        lax.dot_general(
            hot,
            own[half * dof : (half + 1) * dof],
            (((0,), (0,)), ((), ())),
            preferred_element_type=F32,
        )
        for half in range(2)
    ]
    upper = jnp.concatenate([picked[0], picked[1]], axis=1).astype(BF16)
    lower = jnp.concatenate([picked[1], -picked[0]], axis=1).astype(BF16)
    stacked = jnp.concatenate([upper, lower], axis=0)
    gram = lax.dot_general(
        stacked, stacked, (((1,), (1,)), ((), ())), preferred_element_type=F32
    )
    return gram * (1.0 / count_rows)


def lane_spread(piece, lane):
    return jnp.broadcast_to(piece[:, lane : lane + 1], piece.shape)


def refined_reciprocal(value):
    guess = pl.reciprocal(value, approx=True)
    return guess * (2.0 - value * guess)


def eliminate(rows):
    scales = []
    for first in range(0, PANEL, 8):
        span = range(first, first + 8)
        small = {(i, j): lane_spread(rows[i][0], j) for i in span for j in span if j >= i}
        for t in range(first, first + 8, 2):
            u = t + 1
            inverse = refined_reciprocal(small[t, t])
            cross = small[t, t] * small[u, u] - small[t, u] * small[t, u]
            second = refined_reciprocal(cross) * small[t, t]
            scales += [lax.rsqrt(small[t, t]), lax.rsqrt(cross * inverse)]
            factor = small[t, u] * inverse
            for j in range(u + 1, first + 8):
                small[u, j] = small[u, j] - factor * small[t, j]
            rows[u] = [x - factor * y for x, y in zip(rows[u], rows[t])]
            for i in range(u + 1, first + 8):
                one, two = small[t, i] * inverse, small[u, i] * second
                for j in range(i, first + 8):
                    small[i, j] = small[i, j] - one * small[t, j] - two * small[u, j]
                rows[i] = [
                    x - one * y - two * z for x, y, z in zip(rows[i], rows[t], rows[u])
                ]
        for t in span:
            rows[t] = [x * scales[t] for x in rows[t]]
        for i in range(first + 8, PANEL):
            for t in span:
                factor = lane_spread(rows[t][0], i)
                rows[i] = [x - factor * y for x, y in zip(rows[i], rows[t])]
    return rows


def factor_kernel(
    index_ref, pivots_ref, *refs, first, share_slots, ranges, waits, pack, count_rows
):
    beams_refs, refs = refs[:ranges], refs[ranges + waits :]
    out_refs = refs[:ranges]
    arriving, leaving, *scratch = refs[ranges:]
    slots = len(scratch) // 3
    work, lefts, rights = scratch[:slots], scratch[slots : 2 * slots], scratch[2 * slots :]
    order = work[0].shape[0]
    height = arriving.shape[1] // PANEL

    row = lax.broadcasted_iota(jnp.int32, (LANES, LANES), 0)
    col = lax.broadcasted_iota(jnp.int32, (LANES, LANES), 1)
    loading = jnp.where(row == col, LOADING, 0.0)
    owners = (index_ref.shape[0] - 2) // 2
    bin_lead = owner_start(index_ref, index_ref[0], owners) + index_ref[1] * share_slots + first
    for slot in range(slots):
        group, part = divmod(slot, pack)
        own_bin = jnp.minimum(bin_lead + slot, pivots_ref.shape[0] - 1)
        work[slot][...] = loaded_covariance(
            [ref[group] for ref in beams_refs],
            pivots_ref[pl.ds(own_bin, 1), :],
            part,
            pack,
            count_rows,
        )
        for start in range(0, order, LANES):
            work[slot][start : start + LANES, start : start + LANES] += loading

    eights = range(0, PANEL, 8)
    column = lax.broadcasted_iota(jnp.int32, (LANES, 3 * PANEL), 0)

    def spread_out(slot, rows):
        for i in eights:
            for w in range(rows.shape[1] // LANES):
                piece = rows[i : i + 8, w * LANES : (w + 1) * LANES]
                arriving[w, pl.ds(i * height + slot, 8, stride=height), :] = piece

    for slot in range(slots):
        spread_out(slot, work[slot][:PANEL, :])
    for start in range(0, order, LANES):
        chunks = (order - start) // LANES
        stop = start + LANES
        for slot in range(slots):
            lefts[slot][...] = jnp.zeros_like(lefts[slot])
            rights[slot][...] = jnp.zeros_like(rights[slot])

        def one_panel(p, carry, start=start, stop=stop, chunks=chunks):
            back = p * PANEL
            base = pl.multiple_of(start + back, PANEL)
            ahead = pl.multiple_of(jnp.minimum(back + PANEL, LANES - PANEL), PANEL)
            following = pl.multiple_of(start + ahead, PANEL)
            for slot in range(slots):
                left = jnp.where(column >= back + PANEL, lefts[slot][...], 0.0).astype(BF16)
                work[slot][start:stop, start:] -= product(left, rights[slot][:, start:])
            rows = []
            for t in range(PANEL):
                pieces = [arriving[w, t * height : (t + 1) * height, :] for w in range(chunks)]
                pieces[0] = pltpu.roll(pieces[0], (LANES - back) % LANES, 1)
                rows.append(pieces)
            rows = eliminate(rows)
            for t in range(PANEL):
                rows[t][0] = pltpu.roll(rows[t][0], back, 1)
                for w in range(chunks):
                    leaving[w, t * height : (t + 1) * height, :] = rows[t][w]
            for slot in range(slots):
                parts = []
                for w in range(chunks):
                    pieces = [
                        leaving[w, pl.ds(i * height + slot, 8, stride=height), :] for i in eights
                    ]
                    parts.append(jnp.concatenate(pieces, axis=0))
                panel = jnp.concatenate(parts, axis=1)
                work[slot][pl.ds(base, PANEL), start:] = panel
                lefts[slot][...] = left_terms(parts[0]).astype(F32)
                right = right_terms(panel)
                rights[slot][:, start:] = right
                left = lefts[slot][pl.ds(ahead, PANEL), :].astype(BF16)
                spread_out(slot, work[slot][pl.ds(following, PANEL), start:] - product(left, right))
            return carry

        lax.fori_loop(0, LANES // PANEL, one_panel, 0)
        if chunks > 1:
            terms = []
            for slot in range(slots):
                done = work[slot][start:stop, stop:]
                left = jnp.concatenate(
                    [left_terms(done[:, w * LANES : (w + 1) * LANES]) for w in range(chunks - 1)],
                    axis=0,
                )
                right = right_terms(done)
                ready = work[slot][stop : stop + PANEL, stop:] - product(left[:PANEL], right)
                spread_out(slot, ready)
                terms.append((left, right))
            for slot in range(slots):
                left, right = terms[slot]
                work[slot][stop + PANEL :, stop:] -= product(left[PANEL:], right)

    share = order // ranges
    row = lax.broadcasted_iota(jnp.int32, (share, order), 0)
    col = lax.broadcasted_iota(jnp.int32, (share, order), 1)
    for shift, out_ref in enumerate(out_refs):
        lead = pl.multiple_of(lax.rem(index_ref[1] + shift, ranges) * share, math.gcd(share, 16))
        upper = col >= row + lead
        for slot in range(slots):
            piece = work[slot][pl.ds(lead, share), :]
            out_ref[slot] = jnp.where(upper, piece, 0.0).astype(out_ref.dtype)


def factor_slots(beams, pivots, index, first, slots, share_slots, pack, count_rows, earlier):
    ranges = len(beams)
    order = beams[0].shape[1]
    height = -(-slots // 8) * 8
    return pl.pallas_call(
        functools.partial(
            factor_kernel,
            first=first,
            share_slots=share_slots,
            ranges=ranges,
            waits=len(earlier),
            pack=pack,
            count_rows=count_rows,
        ),
        out_shape=[jax.ShapeDtypeStruct((slots, order // ranges, order), BF16)] * ranges,
        in_specs=[pl.BlockSpec(memory_space=pltpu.SMEM)]
        + [pl.BlockSpec(memory_space=pltpu.VMEM)] * (1 + ranges)
        + [pl.BlockSpec(memory_space=pl.ANY)] * len(earlier),
        out_specs=[pl.BlockSpec(memory_space=pltpu.VMEM)] * ranges,
        scratch_shapes=[pltpu.VMEM((order // LANES, PANEL * height, LANES), F32)] * 2
        + [pltpu.VMEM((order, order), F32) for _ in range(slots)]
        + [pltpu.VMEM((LANES, 3 * PANEL), F32) for _ in range(slots)]
        + [pltpu.VMEM((3 * PANEL, order), BF16) for _ in range(slots)],
        compiler_params=PARAMS,
        cost_estimate=pl.CostEstimate(
            flops=slots * order**3,
            bytes_accessed=ranges * beams[0].size * 2,
            transcendentals=0,
        ),
        name="factor_slots",
    )(index, pivots, *beams, *earlier)


def place_kernel(index_ref, *refs, ranges, parts):
    *in_refs, out_ref = refs
    share_slots = out_ref.shape[0] // ranges
    for shift in range(ranges):
        lead = lax.rem(index_ref[1] + (ranges - shift), ranges) * share_slots
        for index, (first, count) in enumerate(parts):
            ref = in_refs[index * ranges + shift]
            for i in range(count):
                slot = lead + first + i
                keep = jnp.broadcast_to(slot < owner_count(index_ref, index_ref[0]), out_ref.shape[1:])
                out_ref[slot] = jnp.where(keep, ref[i].astype(F32), 0.0)


def place_rows(index, done, parts, most_slots):
    ranges = len(done[0])
    arrays = [array for part in done for array in part]
    return pl.pallas_call(
        functools.partial(place_kernel, ranges=ranges, parts=parts),
        out_shape=jax.ShapeDtypeStruct((most_slots,) + arrays[0].shape[1:], F32),
        in_specs=[pl.BlockSpec(memory_space=pltpu.SMEM)]
        + [pl.BlockSpec(memory_space=pltpu.VMEM)] * len(arrays),
        out_specs=pl.BlockSpec(memory_space=pltpu.VMEM),
        compiler_params=PARAMS,
        name="place_rows",
    )(index, *arrays)


def slot_parts(share_slots, pack):
    head = share_slots - pack
    return [(0, head), (head, pack)] if head > 0 else [(0, share_slots)]


def local(raw_echo, replica, beam_weights, pivots, owner_counts, train_gates):
    ch_local = raw_echo.shape[1]
    gate_rows = raw_echo.shape[2]
    pulse_count = raw_echo.shape[3]
    tap_count = replica.shape[1]
    train_local = train_gates.shape[1]
    owners = lax.axis_size("dop")
    ranges = lax.axis_size("rng")
    most_slots = 2 * (pulse_count // owners)
    share_slots = most_slots // ranges
    pack = max(1, min(LANES // train_local, share_slots))

    chunks = max(1, min(4, ch_local // 16))
    chunk_rows = ch_local // chunks
    rim = -(-(tap_count - 1) // 16) * 16
    filters = filter_rows(replica, gate_rows)
    table = doppler_table(pulse_count).transpose(0, 3, 1, 2)
    table = table.reshape(2 * pulse_count, -1).astype(BF16)
    following = [shifted(rim_rows(raw_echo, rim, c, chunks), "rng", -1) for c in range(chunks)]
    spectra = [
        form_spectrum(filters, table, raw_echo, following[c], c, chunks) for c in range(chunks)
    ]

    starts = jnp.cumsum(owner_counts, dtype=jnp.int32) - owner_counts
    places = jnp.stack([lax.axis_index("dop"), lax.axis_index("rng")]).astype(jnp.int32)
    index = jnp.concatenate([places, owner_counts, starts])
    local_gates = train_gates % gate_rows
    gates = jnp.concatenate([local_gates + part * gate_rows for part in range(pack)], axis=1)
    count_rows = float(train_local * ranges)

    outgoing = select_gates(spectra, index, gates, most_slots, owners, pack)
    arrived = lax.all_to_all(outgoing, "dop", split_axis=0, concat_axis=0, tiled=True)
    parts = slot_parts(share_slots, pack)
    formed = [
        form_beams(arrived, beam_weights, index, ranges, first // pack, count // pack)
        for first, count in parts
    ]
    beams = [exchange(arrays, "rng") for arrays in formed]
    done, earlier = [], [arrays[0] for arrays in formed[1:]]
    for (first, count), arrays in zip(parts, beams):
        factors = factor_slots(
            arrays, pivots, index, first, count, share_slots, pack, count_rows, earlier
        )
        earlier = factors[:1]
        done.append(exchange(factors, "rng"))
    return place_rows(index, done, parts, most_slots)


def solution(mesh):
    return jax.shard_map(
        local,
        mesh=mesh,
        in_specs=(P(None, "dop", "rng", None), P(), P(), P(), P(), P(None, "rng")),
        out_specs=P("dop", "rng", None),
        check_vma=False,
    )
```

profile of v0, /device:TPU:1, one launch (start us, length us, event | category | flops | bytes accessed | tf_op | source)
XLA Modules:
  0.0 236.5 jit_solution(14282516301368048120)
XLA Ops:
  0.0 2.1 rim_rows.4
  2.1 2.0 collective-permute-start
  4.0 2.1 rim_rows.5
  6.1 1.9 collective-permute-start.1
  8.0 1.3 rim_rows.6
  9.4 1.9 collective-permute-start.2
  11.3 1.3 rim_rows.7
  12.6 1.9 collective-permute-start.3
  14.5 0.3 negate_convert_fusion
  14.8 0.3 fusion.7
  15.1 0.2 reduce-window.9
  15.4 0.1 copy.17
  15.6 0.1 filter_rows.1.rows_ref
  15.7 1.5 copy.14
  17.2 0.9 add_select_fusion.1
  18.1 0.1 pad_add_fusion.gates_ref
  18.2 2.9 %form_spectrum.4.refs_0_ = bf16[128,32,128]{2,1,0:T(8,128)(2,1)S(1)} custom-call(bf16[256,512]{1,0:T(8,128)(2,1)S(1)} %filter_rows.1.rows_ref, bf16[256,256]{1,0:T(8,128)(2,1)S(1)} %bitcast.16, f32[2,64,128,128]{3,2,1,0:T(8,128)} %own_ref.7, bf16[2,16,64,128]{3,2,1,0:T(8,128)(2,1)S(1)} %collective-permute-done.next_ref), custom_call_target="tpu_custom_call" | custom-call | flops 805306368 | bytes 2097152 | tf_op jit(solution)/shard_map/form_spectrum/pallas_call | solution.py:139
  21.1 3.0 %form_spectrum.5.refs_1_ = bf16[128,32,128]{2,1,0:T(8,128)(2,1)S(1)} custom-call(bf16[256,512]{1,0:T(8,128)(2,1)S(1)} %filter_rows.1.rows_ref, bf16[256,256]{1,0:T(8,128)(2,1)S(1)} %bitcast.17, f32[2,64,128,128]{3,2,1,0:T(8,128)} %own_ref.7, bf16[2,16,64,128]{3,2,1,0:T(8,128)(2,1)S(1)} %collective-permute-done.1.next_ref), custom_call_target="tpu_custom_call" | custom-call | flops 805306368 | bytes 2097152 | tf_op jit(solution)/shard_map/form_spectrum/pallas_call | solution.py:139
  24.1 0.8 collective-permute-done.2.next_ref
  24.9 2.9 %form_spectrum.6.refs_2_ = bf16[128,32,128]{2,1,0:T(8,128)(2,1)S(1)} custom-call(bf16[256,512]{1,0:T(8,128)(2,1)S(1)} %filter_rows.1.rows_ref, bf16[256,256]{1,0:T(8,128)(2,1)S(1)} %bitcast.18, f32[2,64,128,128]{3,2,1,0:T(8,128)} %own_ref.7, bf16[2,16,64,128]{3,2,1,0:T(8,128)(2,1)S(1)} %collective-permute-done.2.next_ref), custom_call_target="tpu_custom_call" | custom-call | flops 805306368 | bytes 2097152 | tf_op jit(solution)/shard_map/form_spectrum/pallas_call | solution.py:139
  27.8 2.7 %collective-permute-done.3.next_ref = bf16[2,16,64,128]{3,2,1,0:T(8,128)(2,1)S(1)} collective-permute-done((bf16[2,16,64,128]{3,2,1,0:T(8,128)(2,1)S(1)}, bf16[2,16,64,128]{3,2,1,0:T(8,128)(2,1)S(1)}, u32[]{:S(2)}, u32[]{:S(2)}) %collective-permute-start.3) | collective-permute-done | bytes 524320 | tf_op jit(solution)/shard_map/ppermute | solution.py:22
  30.5 2.9 %form_spectrum.7.refs_3_ = bf16[128,32,128]{2,1,0:T(8,128)(2,1)S(1)} custom-call(bf16[256,512]{1,0:T(8,128)(2,1)S(1)} %filter_rows.1.rows_ref, bf16[256,256]{1,0:T(8,128)(2,1)S(1)} %bitcast.19, f32[2,64,128,128]{3,2,1,0:T(8,128)} %own_ref.7, bf16[2,16,64,128]{3,2,1,0:T(8,128)(2,1)S(1)} %collective-permute-done.3.next_ref), custom_call_target="tpu_custom_call" | custom-call | flops 805306368 | bytes 2097152 | tf_op jit(solution)/shard_map/form_spectrum/pallas_call | solution.py:139
  33.4 6.0 %select_gates.1 = bf16[8,16,128,128]{3,2,1,0:T(8,128)(2,1)} custom-call(s32[18]{0:T(128)S(1)} %pad_add_fusion.1.index_ref, s32[128,128]{1,0:T(8,128)S(1)} %pad_add_fusion.gates_ref, bf16[128,32,128]{2,1,0:T(8,128)(2,1)S(1)} %form_spectrum.4.refs_0_, bf16[128,32,128]{2,1,0:T(8,128)(2,1)S(1)} %form_spectrum.5.refs_1_, ...), custom_call_target="tpu_custom_call" | custom-call | flops 1073741824 | bytes 4194304 | tf_op jit(solution)/shard_map/select_gates/pallas_call | solution.py:203
  39.4 5.7 %all-to-all-start = ((bf16[8,16,128,128]{3,2,1,0:T(8,128)(2,1)}), bf16[8,16,128,128]{3,2,1,0:T(8,128)(2,1)}, u32[]{:S(2)}, u32[]{:S(2)}) async-start(bf16[8,16,128,128]{3,2,1,0:T(8,128)(2,1)} %select_gates.1), calls=%async_computation | async-start | bytes 8388608 | tf_op jit(solution)/shard_map/all_to_all | solution.py:570
  45.1 0.2 copy.18.weights_ref
  45.4 90.0 %all-to-all-done.arrived_ref = bf16[8,16,128,128]{3,2,1,0:T(8,128)(2,1)} async-done(((bf16[8,16,128,128]{3,2,1,0:T(8,128)(2,1)}), bf16[8,16,128,128]{3,2,1,0:T(8,128)(2,1)}, u32[]{:S(2)}, u32[]{:S(2)}) %all-to-all-start) | async-done | bytes 4194336 | tf_op jit(solution)/shard_map/all_to_all | solution.py:570
  135.4 3.6 %form_beams.2 = (bf16[3,384,128]{2,1,0:T(8,128)(2,1)S(1)}, bf16[3,384,128]{2,1,0:T(8,128)(2,1)S(1)}, bf16[3,384,128]{2,1,0:T(8,128)(2,1)S(1)}, bf16[3,384,128]{2,1,0:T(8,128)(2,1)S(1)}) custom-call(s32[18]{0:T(128)S(1)} %pad_add_fusion.1.index_ref, bf16[2,512,192]{2,1,0:T(8,128)(2,1)S(1)} %copy.18.weights_ref, bf16[8,16,128,128]{3,2,1,0:T(8,128)(2,1)} %all-to-all-done.arrived_ref), custom_call_target="tpu_custom_call" | custom-call | flops 1207959552 | bytes 4194304 | tf_op jit(solution)/shard_map/form_beams/pallas_call | solution.py:253
  139.0 3.9 %collective-permute-start.4 = (bf16[3,384,128]{2,1,0:T(8,128)(2,1)S(1)}, bf16[3,384,128]{2,1,0:T(8,128)(2,1)S(1)}, u32[]{:S(2)}, u32[]{:S(2)}) collective-permute-start(bf16[3,384,128]{2,1,0:T(8,128)(2,1)S(1)} %get-tuple-element.22), channel_id=1, source_target_pairs={{0,1},{1,2},{2,3},{3,0},{4,5},{5,6},{6,7},{7,4},{8,9},{9,10},{10,1... | collective-permute-start | bytes 884744 | tf_op jit(solution)/shard_map/ppermute | solution.py:277
  142.9 0.5 collective-permute-start.6
  143.3 3.0 %form_beams.3 = (bf16[1,384,128]{2,1,0:T(8,128)(2,1)S(1)}, bf16[1,384,128]{2,1,0:T(8,128)(2,1)S(1)}, bf16[1,384,128]{2,1,0:T(8,128)(2,1)S(1)}, bf16[1,384,128]{2,1,0:T(8,128)(2,1)S(1)}) custom-call(s32[18]{0:T(128)S(1)} %pad_add_fusion.1.index_ref, bf16[2,512,192]{2,1,0:T(8,128)(2,1)S(1)} %copy.18.weights_ref, bf16[8,16,128,128]{3,2,1,0:T(8,128)(2,1)} %all-to-all-done.arrived_ref), custom_call_target="tpu_custom_call" | custom-call | flops 402653184 | bytes 4194304 | tf_op jit(solution)/shard_map/form_beams/pallas_call | solution.py:253
  146.4 1.5 collective-permute-start.10
  147.9 0.1 copy.20.pivots_ref
  148.0 1.0 collective-permute-done.4.refs_1_
  149.1 6.3 %collective-permute-done.5.refs_2_ = bf16[3,384,128]{2,1,0:T(8,128)(2,1)S(1)} collective-permute-done((bf16[3,384,128]{2,1,0:T(8,128)(2,1)S(1)}, bf16[3,384,128]{2,1,0:T(8,128)(2,1)S(1)}, u32[]{:S(2)}, u32[]{:S(2)}) %collective-permute-start.5) | collective-permute-done | bytes 294944 | tf_op jit(solution)/shard_map/ppermute | solution.py:277
  155.4 1.1 collective-permute-done.6.refs_3_
  156.5 23.2 %factor_slots.2 = (bf16[6,96,384]{2,1,0:T(8,128)(2,1)S(1)}, bf16[6,96,384]{2,1,0:T(8,128)(2,1)S(1)}, bf16[6,96,384]{2,1,0:T(8,128)(2,1)S(1)}, bf16[6,96,384]{2,1,0:T(8,128)(2,1)S(1)}) custom-call(s32[18]{0:T(128)S(1)} %pad_add_fusion.1.index_ref, s32[128,192]{1,0:T(8,128)S(1)} %copy.20.pivots_ref, bf16[3,384,128]{2,1,0:T(8,128)(2,1)S(1)} %get-tuple-element.21.refs_0_, ...), custom_call_target="tpu_custom_call" | custom-call | flops 339738624 | bytes 1179648 | tf_op jit(solution)/shard_map/factor_slots/pallas_call | solution.py:478
  179.8 2.4 %collective-permute-start.8 = (bf16[6,96,384]{2,1,0:T(8,128)(2,1)S(1)}, bf16[6,96,384]{2,1,0:T(8,128)(2,1)S(1)}, u32[]{:S(2)}, u32[]{:S(2)}) collective-permute-start(bf16[6,96,384]{2,1,0:T(8,128)(2,1)S(1)} %get-tuple-element.28), channel_id=1, source_target_pairs={{0,2},{1,3},{2,0},{3,1},{4,6},{5,7},{6,4},{7,5},{8,10},{9,11},{10,... | collective-permute-start | bytes 1327112 | tf_op jit(solution)/shard_map/ppermute | solution.py:277
  182.2 0.7 collective-permute-start.9
  182.9 1.4 collective-permute-start.12
  184.3 19.4 %collective-permute-done.11.refs_2_ = bf16[1,384,128]{2,1,0:T(8,128)(2,1)S(1)} collective-permute-done((bf16[1,384,128]{2,1,0:T(8,128)(2,1)S(1)}, bf16[1,384,128]{2,1,0:T(8,128)(2,1)S(1)}, u32[]{:S(2)}, u32[]{:S(2)}) %collective-permute-start.11) | collective-permute-done | bytes 98336 | tf_op jit(solution)/shard_map/ppermute | solution.py:277
  203.8 1.4 collective-permute-done.12.refs_3_
  205.2 19.8 %factor_slots.3 = (bf16[2,96,384]{2,1,0:T(8,128)(2,1)S(1)}, bf16[2,96,384]{2,1,0:T(8,128)(2,1)S(1)}, bf16[2,96,384]{2,1,0:T(8,128)(2,1)S(1)}, bf16[2,96,384]{2,1,0:T(8,128)(2,1)S(1)}) custom-call(s32[18]{0:T(128)S(1)} %pad_add_fusion.1.index_ref, s32[128,192]{1,0:T(8,128)S(1)} %copy.20.pivots_ref, ...), custom_call_target="tpu_custom_call" | custom-call | flops 113246208 | bytes 393216 | tf_op jit(solution)/shard_map/factor_slots/pallas_call | solution.py:478
  225.1 1.0 collective-permute-start.14
  226.0 2.0 collective-permute-done.13.refs_5_
  228.1 1.2 collective-permute-start.15
  229.3 2.6 %collective-permute-done.14.refs_6_ = bf16[2,96,384]{2,1,0:T(8,128)(2,1)S(1)} collective-permute-done((bf16[2,96,384]{2,1,0:T(8,128)(2,1)S(1)}, bf16[2,96,384]{2,1,0:T(8,128)(2,1)S(1)}, u32[]{:S(2)}, u32[]{:S(2)}) %collective-permute-start.14) | collective-permute-done | bytes 147488 | tf_op jit(solution)/shard_map/ppermute | solution.py:277
  232.0 1.4 collective-permute-done.15.refs_7_
  233.4 3.0 %place_rows.1 = f32[32,96,384]{2,1,0:T(8,128)} custom-call(s32[18]{0:T(128)S(1)} %pad_add_fusion.1.index_ref, bf16[6,96,384]{2,1,0:T(8,128)(2,1)S(1)} %get-tuple-element.26.refs_4_.refs_0_, bf16[6,96,384]{2,1,0:T(8,128)(2,1)S(1)} %collective-permute-done.7.refs_1_, bf16[6,96,384]{2,1,0:T(8,128)(2,1)S(1)} %collective-permute-done.8.refs_2_, ...), custom_call_target="tpu_custom_call" | custom-call | tf_op jit(solution)/shard_map/place_rows/pallas_call | solution.py:523
  (24 shorter events, 0.3 us)
Async XLA Ops:
  2.1 16.1 %collective-permute-start = (bf16[2,16,64,128]{3,2,1,0:T(8,128)(2,1)}, bf16[2,16,64,128]{3,2,1,0:T(8,128)(2,1)S(1)}, u32[]{:S(2)}, u32[]{:S(2)}) collective-permute-start(bf16[2,16,64,128]{3,2,1,0:T(8,128)(2,1)} %rim_rows.4), channel_id=1, source_target_pairs={{1,0},{2,1},{3,2},{5,4},{6,5},{7,6},{9,8},{10,9},{11,10},{13,12},{... | collective-permute-start | bytes 1572872 | tf_op jit(solution)/shard_map/ppermute | solution.py:22
  6.1 15.0 %collective-permute-start.1 = (bf16[2,16,64,128]{3,2,1,0:T(8,128)(2,1)}, bf16[2,16,64,128]{3,2,1,0:T(8,128)(2,1)S(1)}, u32[]{:S(2)}, u32[]{:S(2)}) collective-permute-start(bf16[2,16,64,128]{3,2,1,0:T(8,128)(2,1)} %rim_rows.5), channel_id=1, source_target_pairs={{1,0},{2,1},{3,2},{5,4},{6,5},{7,6},{9,8},{10,9},{11,10},{13,12},{... | collective-permute-start | bytes 1572872 | tf_op jit(solution)/shard_map/ppermute | solution.py:22
  9.3 5.7 %copy-start.3 = (s32[8]{0:T(128)S(1)}, s32[8]{0:T(128)}, u32[]{:S(2)}) copy-start(s32[8]{0:T(128)} %param.10) | copy-start | bytes 100
  9.3 6.2 %copy-start.2 = (f32[2,64]{1,0:T(2,128)S(1)}, f32[2,64]{1,0:T(2,128)}, u32[]{:S(2)}) copy-start(f32[2,64]{1,0:T(2,128)} %param.7) | copy-start | bytes 1540
  9.4 15.5 %collective-permute-start.2 = (bf16[2,16,64,128]{3,2,1,0:T(8,128)(2,1)S(1)}, bf16[2,16,64,128]{3,2,1,0:T(8,128)(2,1)S(1)}, u32[]{:S(2)}, u32[]{:S(2)}) collective-permute-start(bf16[2,16,64,128]{3,2,1,0:T(8,128)(2,1)S(1)} %rim_rows.6), channel_id=1, source_target_pairs={{1,0},{2,1},{3,2},{5,4},{6,5},{7,6},{9,8},{10,9},{11,10},{13,12},{... | collective-permute-start | bytes 1572872 | tf_op jit(solution)/shard_map/ppermute | solution.py:22
  12.6 17.9 %collective-permute-start.3 = (bf16[2,16,64,128]{3,2,1,0:T(8,128)(2,1)S(1)}, bf16[2,16,64,128]{3,2,1,0:T(8,128)(2,1)S(1)}, u32[]{:S(2)}, u32[]{:S(2)}) collective-permute-start(bf16[2,16,64,128]{3,2,1,0:T(8,128)(2,1)S(1)} %rim_rows.7), channel_id=1, source_target_pairs={{1,0},{2,1},{3,2},{5,4},{6,5},{7,6},{9,8},{10,9},{11,10},{13,12},{... | collective-permute-start | bytes 1572872 | tf_op jit(solution)/shard_map/ppermute | solution.py:22
  39.4 5.7 %copy-start = (bf16[2,512,192]{1,2,0:T(8,128)(2,1)S(1)}, bf16[2,512,192]{1,2,0:T(8,128)(2,1)}, u32[]{:S(2)}) copy-start(bf16[2,512,192]{1,2,0:T(8,128)(2,1)} %param.8) | copy-start | bytes 1179652
  39.4 95.9 %all-to-all-start = ((bf16[8,16,128,128]{3,2,1,0:T(8,128)(2,1)}), bf16[8,16,128,128]{3,2,1,0:T(8,128)(2,1)}, u32[]{:S(2)}, u32[]{:S(2)}) async-start(bf16[8,16,128,128]{3,2,1,0:T(8,128)(2,1)} %select_gates.1), calls=%async_computation | async-start | bytes 8388608 | tf_op jit(solution)/shard_map/all_to_all | solution.py:570
  45.4 102.6 %copy-start.1 = (s32[128,192]{0,1:T(8,128)S(1)}, s32[128,192]{0,1:T(8,128)}, u32[]{:S(2)}) copy-start(s32[128,192]{0,1:T(8,128)} %param.9) | copy-start | bytes 294916
  139.0 10.1 %collective-permute-start.4 = (bf16[3,384,128]{2,1,0:T(8,128)(2,1)S(1)}, bf16[3,384,128]{2,1,0:T(8,128)(2,1)S(1)}, u32[]{:S(2)}, u32[]{:S(2)}) collective-permute-start(bf16[3,384,128]{2,1,0:T(8,128)(2,1)S(1)} %get-tuple-element.22), channel_id=1, source_target_pairs={{0,1},{1,2},{2,3},{3,0},{4,5},{5,6},{6,7},{7,4},{8,9},{9,10},{10,1... | collective-permute-start | bytes 884744 | tf_op jit(solution)/shard_map/ppermute | solution.py:277
  142.9 12.5 %collective-permute-start.5 = (bf16[3,384,128]{2,1,0:T(8,128)(2,1)S(1)}, bf16[3,384,128]{2,1,0:T(8,128)(2,1)S(1)}, u32[]{:S(2)}, u32[]{:S(2)}) collective-permute-start(bf16[3,384,128]{2,1,0:T(8,128)(2,1)S(1)} %get-tuple-element.23), channel_id=1, source_target_pairs={{0,2},{1,3},{2,0},{3,1},{4,6},{5,7},{6,4},{7,5},{8,10},{9,11},{10,... | collective-permute-start | bytes 884744 | tf_op jit(solution)/shard_map/ppermute | solution.py:277
  142.9 13.6 %collective-permute-start.6 = (bf16[3,384,128]{2,1,0:T(8,128)(2,1)S(1)}, bf16[3,384,128]{2,1,0:T(8,128)(2,1)S(1)}, u32[]{:S(2)}, u32[]{:S(2)}) collective-permute-start(bf16[3,384,128]{2,1,0:T(8,128)(2,1)S(1)} %get-tuple-element.24), channel_id=1, source_target_pairs={{0,3},{1,0},{2,1},{3,2},{4,7},{5,4},{6,5},{7,6},{8,11},{9,8},{10,9... | collective-permute-start | bytes 884744 | tf_op jit(solution)/shard_map/ppermute | solution.py:277
  146.4 36.5 %collective-permute-start.10 = (bf16[1,384,128]{2,1,0:T(8,128)(2,1)S(1)}, bf16[1,384,128]{2,1,0:T(8,128)(2,1)S(1)}, u32[]{:S(2)}, u32[]{:S(2)}) collective-permute-start(bf16[1,384,128]{2,1,0:T(8,128)(2,1)S(1)} %get-tuple-element.30), channel_id=1, source_target_pairs={{0,1},{1,2},{2,3},{3,0},{4,5},{5,6},{6,7},{7,4},{8,9},{9,10},{10,1... | collective-permute-start | bytes 294920 | tf_op jit(solution)/shard_map/ppermute | solution.py:277
  179.7 53.7 %collective-permute-start.7 = (bf16[6,96,384]{2,1,0:T(8,128)(2,1)S(1)}, bf16[6,96,384]{2,1,0:T(8,128)(2,1)S(1)}, u32[]{:S(2)}, u32[]{:S(2)}) collective-permute-start(bf16[6,96,384]{2,1,0:T(8,128)(2,1)S(1)} %get-tuple-element.27), channel_id=1, source_target_pairs={{0,1},{1,2},{2,3},{3,0},{4,5},{5,6},{6,7},{7,4},{8,9},{9,10},{10,1... | collective-permute-start | bytes 1327112 | tf_op jit(solution)/shard_map/ppermute | solution.py:277
  179.8 53.6 %collective-permute-start.8 = (bf16[6,96,384]{2,1,0:T(8,128)(2,1)S(1)}, bf16[6,96,384]{2,1,0:T(8,128)(2,1)S(1)}, u32[]{:S(2)}, u32[]{:S(2)}) collective-permute-start(bf16[6,96,384]{2,1,0:T(8,128)(2,1)S(1)} %get-tuple-element.28), channel_id=1, source_target_pairs={{0,2},{1,3},{2,0},{3,1},{4,6},{5,7},{6,4},{7,5},{8,10},{9,11},{10,... | collective-permute-start | bytes 1327112 | tf_op jit(solution)/shard_map/ppermute | solution.py:277
  182.2 51.2 %collective-permute-start.9 = (bf16[6,96,384]{2,1,0:T(8,128)(2,1)S(1)}, bf16[6,96,384]{2,1,0:T(8,128)(2,1)S(1)}, u32[]{:S(2)}, u32[]{:S(2)}) collective-permute-start(bf16[6,96,384]{2,1,0:T(8,128)(2,1)S(1)} %get-tuple-element.29), channel_id=1, source_target_pairs={{0,3},{1,0},{2,1},{3,2},{4,7},{5,4},{6,5},{7,6},{8,11},{9,8},{10,9... | collective-permute-start | bytes 1327112 | tf_op jit(solution)/shard_map/ppermute | solution.py:277
  182.9 20.9 %collective-permute-start.11 = (bf16[1,384,128]{2,1,0:T(8,128)(2,1)S(1)}, bf16[1,384,128]{2,1,0:T(8,128)(2,1)S(1)}, u32[]{:S(2)}, u32[]{:S(2)}) collective-permute-start(bf16[1,384,128]{2,1,0:T(8,128)(2,1)S(1)} %get-tuple-element.31), channel_id=1, source_target_pairs={{0,2},{1,3},{2,0},{3,1},{4,6},{5,7},{6,4},{7,5},{8,10},{9,11},{10,... | collective-permute-start | bytes 294920 | tf_op jit(solution)/shard_map/ppermute | solution.py:277
  182.9 22.3 %collective-permute-start.12 = (bf16[1,384,128]{2,1,0:T(8,128)(2,1)S(1)}, bf16[1,384,128]{2,1,0:T(8,128)(2,1)S(1)}, u32[]{:S(2)}, u32[]{:S(2)}) collective-permute-start(bf16[1,384,128]{2,1,0:T(8,128)(2,1)S(1)} %get-tuple-element.32), channel_id=1, source_target_pairs={{0,3},{1,0},{2,1},{3,2},{4,7},{5,4},{6,5},{7,6},{8,11},{9,8},{10,9... | collective-permute-start | bytes 294920 | tf_op jit(solution)/shard_map/ppermute | solution.py:277
  225.0 3.1 %collective-permute-start.13 = (bf16[2,96,384]{2,1,0:T(8,128)(2,1)S(1)}, bf16[2,96,384]{2,1,0:T(8,128)(2,1)S(1)}, u32[]{:S(2)}, u32[]{:S(2)}) collective-permute-start(bf16[2,96,384]{2,1,0:T(8,128)(2,1)S(1)} %get-tuple-element.34), channel_id=1, source_target_pairs={{0,1},{1,2},{2,3},{3,0},{4,5},{5,6},{6,7},{7,4},{8,9},{9,10},{10,1... | collective-permute-start | bytes 442376 | tf_op jit(solution)/shard_map/ppermute | solution.py:277
  225.1 6.9 %collective-permute-start.14 = (bf16[2,96,384]{2,1,0:T(8,128)(2,1)S(1)}, bf16[2,96,384]{2,1,0:T(8,128)(2,1)S(1)}, u32[]{:S(2)}, u32[]{:S(2)}) collective-permute-start(bf16[2,96,384]{2,1,0:T(8,128)(2,1)S(1)} %get-tuple-element.35), channel_id=1, source_target_pairs={{0,2},{1,3},{2,0},{3,1},{4,6},{5,7},{6,4},{7,5},{8,10},{9,11},{10,... | collective-permute-start | bytes 442376 | tf_op jit(solution)/shard_map/ppermute | solution.py:277
  228.1 5.3 %collective-permute-start.15 = (bf16[2,96,384]{2,1,0:T(8,128)(2,1)S(1)}, bf16[2,96,384]{2,1,0:T(8,128)(2,1)S(1)}, u32[]{:S(2)}, u32[]{:S(2)}) collective-permute-start(bf16[2,96,384]{2,1,0:T(8,128)(2,1)S(1)} %get-tuple-element.36), channel_id=1, source_target_pairs={{0,3},{1,0},{2,1},{3,2},{4,7},{5,4},{6,5},{7,6},{8,11},{9,8},{10,9... | collective-permute-start | bytes 442376 | tf_op jit(solution)/shard_map/ppermute | solution.py:277
where the time goes:
time: 237 us; the launch traced here: 236 us
  waiting for transfers between devices  129 us (54%)
  Pallas kernels  77.4 us (33%)
  starting transfers between devices  26.1 us (11%)
    all_to_all x1, waiting for transfers between devices, local(): lax.all_to_all(outgoing, 'dop', split_axis=0, concat_axis=0, tiled=True)  90 us
    pallas_call x2, Pallas kernels, factor_slots(): pl.pallas_call(functools.partial(factor_kernel, first=first, share_slots=...  43.1 us
    ppermute x12, waiting for transfers between devices, exchange(): moved.append(lax.ppermute(arrays[shift], axis, pairs))  35.4 us
    ppermute x12, starting transfers between devices, exchange(): moved.append(lax.ppermute(arrays[shift], axis, pairs))  12.7 us
    pallas_call x4, Pallas kernels, form_spectrum(): pl.pallas_call(spectrum_kernel, out_shape=jax.ShapeDtypeStruct((bins, hei...  11.8 us
    ppermute x4, starting transfers between devices, shifted(): return lax.ppermute(array, axis, pairs)  7.7 us
    pallas_call x4, Pallas kernels, rim_rows(): pl.pallas_call(rim_kernel, out_shape=jax.ShapeDtypeStruct(shape, BF16), g...  6.74 us
    pallas_call x2, Pallas kernels, form_beams(): pl.pallas_call(functools.partial(beam_kernel, first=first), out_shape=[ja...  6.68 us
  transfers between devices with their start and end apart: 17, of which 11 were waited for; matrix products, arithmetic and copies ran while one was open for 2% of the time, Pallas kernels for 25%

commit v1 on v0

--- a/solution.py
+++ b/solution.py
@@ -166,7 +166,7 @@
     return index_ref[2 + owners + owner]
 
 
-def select_kernel(index_ref, gates_ref, *refs, owners, pack):
+def select_kernel(index_ref, gates_ref, *refs, owners, ranges, first, share_slots, pack):
     *spectrum_refs, out_ref = refs
     bin_count, height, gate_rows = spectrum_refs[0].shape
     some, groups, _, width = out_ref.shape
@@ -176,9 +176,9 @@
     for inner in range(some):
         start = owner_start(index_ref, pl.program_id(0) * some + inner, owners)
         for group in range(groups):
-            bins = [
-                jnp.minimum(start + group * pack + part, bin_count - 1) for part in range(pack)
-            ]
+            block, place = divmod(group, groups // ranges)
+            slot = block * share_slots + first + place * pack
+            bins = [jnp.minimum(start + slot + part, bin_count - 1) for part in range(pack)]
             gates = gates_ref[pl.ds(bins[0], 1), :]
             for part in range(1, pack):
                 gates = jnp.where(part_index == part, gates_ref[pl.ds(bins[part], 1), :], gates)
@@ -195,18 +195,26 @@
             out_ref[inner, group] = picked.astype(BF16)
 
 
-def select_gates(spectra, index, gates, most_slots, owners, pack):
+def select_gates(spectra, index, gates, first, count, share_slots, owners, ranges, pack):
     rows = sum(spectrum.shape[1] for spectrum in spectra)
     gate_rows = spectra[0].shape[2]
-    groups = most_slots // pack
+    groups = ranges * count // pack
     width = gates.shape[1]
+    some = math.gcd(owners, 2)
     return pl.pallas_call(
-        functools.partial(select_kernel, owners=owners, pack=pack),
+        functools.partial(
+            select_kernel,
+            owners=owners,
+            ranges=ranges,
+            first=first,
+            share_slots=share_slots,
+            pack=pack,
+        ),
         out_shape=jax.ShapeDtypeStruct((owners, groups, rows, width), BF16),
-        grid=(owners,),
+        grid=(owners // some,),
         in_specs=[pl.BlockSpec(memory_space=pltpu.SMEM)]
         + [pl.BlockSpec(memory_space=pltpu.VMEM)] * (1 + len(spectra)),
-        out_specs=pl.BlockSpec((1, groups, rows, width), lambda i: (i, 0, 0, 0)),
+        out_specs=pl.BlockSpec((some, groups, rows, width), lambda i: (i, 0, 0, 0)),
         compiler_params=PARAMS,
         cost_estimate=pl.CostEstimate(
             flops=2 * owners * groups * pack * rows * gate_rows * width,
@@ -217,13 +225,14 @@
     )(index, gates, *spectra)
 
 
-def beam_kernel(index_ref, weights_ref, arrived_ref, *out_refs, first):
+def beam_kernel(index_ref, weights_ref, arrived_ref, *refs, ranges):
+    out_refs = refs[-ranges:]
     sources, groups, rows, width = arrived_ref.shape
-    ranges, share = len(out_refs), out_refs[0].shape[0]
+    share = groups // ranges
     dof = weights_ref.shape[2]
     half = rows // 2
     for shift, out_ref in enumerate(out_refs):
-        lead = lax.rem(index_ref[1] + shift, ranges) * (groups // ranges) + first
+        lead = lax.rem(index_ref[1] + shift, ranges) * share
         packed = jnp.concatenate(
             [
                 arrived_ref[:, lead + g, s * half : (s + 1) * half].reshape(sources * half, width)
@@ -247,26 +256,27 @@
             out_ref[g, dof:] = imag_part[:, span].astype(BF16)
 
 
-def form_beams(arrived, weights, index, ranges, first, count):
-    sources, _, rows, width = arrived.shape
-    shape = (count, 2 * weights.shape[2], width)
+def form_beams(arrived, weights, index, ranges, earlier):
+    _, groups, _, width = arrived.shape
+    shape = (groups // ranges, 2 * weights.shape[2], width)
     return pl.pallas_call(
-        functools.partial(beam_kernel, first=first),
+        functools.partial(beam_kernel, ranges=ranges),
         out_shape=[jax.ShapeDtypeStruct(shape, BF16)] * ranges,
         in_specs=[
             pl.BlockSpec(memory_space=pltpu.SMEM),
             pl.BlockSpec(memory_space=pltpu.VMEM),
             pl.BlockSpec(memory_space=pltpu.VMEM),
-        ],
+        ]
+        + [pl.BlockSpec(memory_space=pl.ANY)] * len(earlier),
         out_specs=[pl.BlockSpec(memory_space=pltpu.VMEM)] * ranges,
         compiler_params=PARAMS,
         cost_estimate=pl.CostEstimate(
-            flops=4 * ranges * count * sources * rows * width * weights.shape[2],
+            flops=4 * arrived.size * weights.shape[2],
             bytes_accessed=arrived.size * 2,
             transcendentals=0,
         ),
         name="form_beams",
-    )(index, weights, arrived)
+    )(index, weights, arrived, *earlier)
 
 
 def exchange(arrays, axis):
@@ -333,33 +343,39 @@
 
 def eliminate(rows):
     scales = []
+
+    def diagonal_piece(first):
+        span = range(first, first + 8)
+        return {(i, j): lane_spread(rows[i][0], j) for i in span for j in span if j >= i}
+
+    small = diagonal_piece(0)
     for first in range(0, PANEL, 8):
-        span = range(first, first + 8)
-        small = {(i, j): lane_spread(rows[i][0], j) for i in span for j in span if j >= i}
-        for t in range(first, first + 8, 2):
+        stop = first + 8
+        following = diagonal_piece(stop) if stop < PANEL else {}
+        for t in range(first, stop, 2):
             u = t + 1
             inverse = refined_reciprocal(small[t, t])
             cross = small[t, t] * small[u, u] - small[t, u] * small[t, u]
             second = refined_reciprocal(cross) * small[t, t]
             scales += [lax.rsqrt(small[t, t]), lax.rsqrt(cross * inverse)]
             factor = small[t, u] * inverse
-            for j in range(u + 1, first + 8):
+            for j in range(u + 1, stop):
                 small[u, j] = small[u, j] - factor * small[t, j]
             rows[u] = [x - factor * y for x, y in zip(rows[u], rows[t])]
-            for i in range(u + 1, first + 8):
-                one, two = small[t, i] * inverse, small[u, i] * second
-                for j in range(i, first + 8):
-                    small[i, j] = small[i, j] - one * small[t, j] - two * small[u, j]
-                rows[i] = [
-                    x - one * y - two * z for x, y, z in zip(rows[i], rows[t], rows[u])
-                ]
-        for t in span:
-            rows[t] = [x * scales[t] for x in rows[t]]
-        for i in range(first + 8, PANEL):
-            for t in span:
-                factor = lane_spread(rows[t][0], i)
-                rows[i] = [x - factor * y for x, y in zip(rows[i], rows[t])]
-    return rows
+            upper = {i: (small[t, i], small[u, i]) for i in range(u + 1, stop)}
+            for i in range(stop, PANEL):
+                upper[i] = (lane_spread(rows[t][0], i), lane_spread(rows[u][0], i))
+            scaled = {i: (x * inverse, y * second) for i, (x, y) in upper.items()}
+            for piece in (small, following):
+                for i, j in piece:
+                    if i > u:
+                        one, two = scaled[i]
+                        x, y = upper[j]
+                        piece[i, j] = piece[i, j] - one * x - two * y
+            for i, (one, two) in scaled.items():
+                rows[i] = [x - one * y - two * z for x, y, z in zip(rows[i], rows[t], rows[u])]
+        small = following
+    return [[x * scale for x in row] for row, scale in zip(rows, scales)]
 
 
 def factor_kernel(
@@ -504,36 +520,54 @@
     )(index, pivots, *beams, *earlier)
 
 
-def place_kernel(index_ref, *refs, ranges, parts):
-    *in_refs, out_ref = refs
-    share_slots = out_ref.shape[0] // ranges
-    for shift in range(ranges):
-        lead = lax.rem(index_ref[1] + (ranges - shift), ranges) * share_slots
-        for index, (first, count) in enumerate(parts):
-            ref = in_refs[index * ranges + shift]
-            for i in range(count):
-                slot = lead + first + i
-                keep = jnp.broadcast_to(slot < owner_count(index_ref, index_ref[0]), out_ref.shape[1:])
-                out_ref[slot] = jnp.where(keep, ref[i].astype(F32), 0.0)
-
-
-def place_rows(index, done, parts, most_slots):
-    ranges = len(done[0])
-    arrays = [array for part in done for array in part]
+def place_kernel(index_ref, *refs, first, share_slots, ranges):
+    in_refs, out_ref = refs[:ranges], refs[-1]
+    slots = out_ref.shape[0]
+    steps = in_refs[0].shape[0] // slots
+    step = pl.program_id(0)
+    shift, place = step // steps, step % steps
+    block = lax.rem(index_ref[1] + ranges - shift, ranges)
+    lead = block * share_slots + first + place * slots
+    for this, ref in enumerate(in_refs):
+
+        @pl.when(shift == this)
+        def _(ref=ref):
+            for i in range(slots):
+                keep = lead + i < owner_count(index_ref, index_ref[0])
+                keep = jnp.broadcast_to(keep, out_ref.shape[1:])
+                out_ref[i] = jnp.where(keep, ref[place * slots + i].astype(F32), 0.0)
+
+
+def place_rows(index, arrays, first, share_slots, earlier):
+    ranges = len(arrays)
+    count = arrays[0].shape[0]
+    slots = math.gcd(math.gcd(count, first), share_slots)
+    steps = count // slots
+
+    def out_index(step, index_ref):
+        block = lax.rem(index_ref[1] + ranges - step // steps, ranges)
+        return ((block * share_slots + first) // slots + step % steps, 0, 0)
+
     return pl.pallas_call(
-        functools.partial(place_kernel, ranges=ranges, parts=parts),
-        out_shape=jax.ShapeDtypeStruct((most_slots,) + arrays[0].shape[1:], F32),
-        in_specs=[pl.BlockSpec(memory_space=pltpu.SMEM)]
-        + [pl.BlockSpec(memory_space=pltpu.VMEM)] * len(arrays),
-        out_specs=pl.BlockSpec(memory_space=pltpu.VMEM),
+        functools.partial(place_kernel, first=first, share_slots=share_slots, ranges=ranges),
+        out_shape=jax.ShapeDtypeStruct((ranges * share_slots,) + arrays[0].shape[1:], F32),
+        grid_spec=pltpu.PrefetchScalarGridSpec(
+            num_scalar_prefetch=1,
+            grid=(ranges * steps,),
+            in_specs=[pl.BlockSpec(memory_space=pltpu.VMEM)] * ranges
+            + [pl.BlockSpec(memory_space=pl.ANY)] * len(earlier),
+            out_specs=pl.BlockSpec((slots,) + arrays[0].shape[1:], out_index),
+        ),
+        input_output_aliases={1 + ranges: 0} if earlier else {},
         compiler_params=PARAMS,
         name="place_rows",
-    )(index, *arrays)
+    )(index, *arrays, *earlier)
 
 
 def slot_parts(share_slots, pack):
-    head = share_slots - pack
-    return [(0, head), (head, pack)] if head > 0 else [(0, share_slots)]
+    halves = 2 if share_slots % (2 * pack) == 0 else 1
+    count = share_slots // halves
+    return [(i * count, count) for i in range(halves)]
 
 
 def local(raw_echo, replica, beam_weights, pivots, owner_counts, train_gates):
@@ -566,22 +600,24 @@
     gates = jnp.concatenate([local_gates + part * gate_rows for part in range(pack)], axis=1)
     count_rows = float(train_local * ranges)
 
-    outgoing = select_gates(spectra, index, gates, most_slots, owners, pack)
-    arrived = lax.all_to_all(outgoing, "dop", split_axis=0, concat_axis=0, tiled=True)
     parts = slot_parts(share_slots, pack)
-    formed = [
-        form_beams(arrived, beam_weights, index, ranges, first // pack, count // pack)
+    outgoing = [
+        select_gates(spectra, index, gates, first, count, share_slots, owners, ranges, pack)
         for first, count in parts
     ]
-    beams = [exchange(arrays, "rng") for arrays in formed]
-    done, earlier = [], [arrays[0] for arrays in formed[1:]]
-    for (first, count), arrays in zip(parts, beams):
+    sent = [
+        lax.all_to_all(array, "dop", split_axis=0, concat_axis=0, tiled=True) for array in outgoing
+    ]
+    result, earlier = [], outgoing[1:]
+    for (first, count), arrived in zip(parts, sent):
+        beams = exchange(form_beams(arrived, beam_weights, index, ranges, earlier), "rng")
         factors = factor_slots(
-            arrays, pivots, index, first, count, share_slots, pack, count_rows, earlier
+            beams, pivots, index, first, count, share_slots, pack, count_rows, []
         )
         earlier = factors[:1]
-        done.append(exchange(factors, "rng"))
-    return place_rows(index, done, parts, most_slots)
+        rows = exchange(factors, "rng")
+        result = [place_rows(index, rows, first, share_slots, result)]
+    return result[0]
 
 
 def solution(mesh):

time: 237 us -> 202 us (0.85)
  waiting for transfers between devices: 129 us -> 78.9 us
  Pallas kernels: 77.4 us -> 84.5 us
  starting transfers between devices: 26.1 us -> 31.9 us
  local copies, waits for them, and re-layouts: 1.97 us -> 4.6 us
    all_to_all x1 -> x2, waiting for transfers between devices: 90 us -> 48.5 us  [local(): lax.all_to_all(array, 'dop', split_axis=0, concat_axis=0, tiled=True)]
    ppermute x12, waiting for transfers between devices: 35.4 us -> 27.4 us  [exchange(): moved.append(lax.ppermute(arrays[shift], axis, pairs))]
    pallas_call x2, Pallas kernels: 43.1 us -> 48.5 us  [factor_slots(): pl.pallas_call(functools.partial(factor_kernel, first=first, share_slots=...]
    all_to_all x1 -> x2, starting transfers between devices: 5.7 us -> 9.91 us  [local(): lax.all_to_all(array, 'dop', split_axis=0, concat_axis=0, tiled=True)]
    unnamed x12 -> x24, local copies, waits for them, and re-layouts: 1.83 us -> 4.46 us
    pallas_call x4 -> x6, Pallas kernels: 15.7 us -> 17.4 us  [the longest x2 7.02 us: select_gates(): pl.pallas_call(functools.partial(select_kernel, owners=owners, ranges=ran...]
  transfers between devices with their start and end apart: 17 -> 18, of which waited for: 11 -> 12; matrix products, arithmetic and copies ran while one was open for 2% -> 1% of each run, Pallas kernels for 25% -> 37%
where the time goes in v1:
time: 202 us; the launch traced here: 201 us
  Pallas kernels  84.5 us (42%)
  waiting for transfers between devices  78.9 us (39%)
  starting transfers between devices  31.9 us (16%)
  local copies, waits for them, and re-layouts  4.6 us (2%)
    pallas_call x2, Pallas kernels, factor_slots(): pl.pallas_call(functools.partial(factor_kernel, first=first, share_slots=...  48.5 us
    all_to_all x2, waiting for transfers between devices, local(): lax.all_to_all(array, 'dop', split_axis=0, concat_axis=0, tiled=True)  48.5 us
    ppermute x12, waiting for transfers between devices, exchange(): moved.append(lax.ppermute(arrays[shift], axis, pairs))  27.4 us
    ppermute x12, starting transfers between devices, exchange(): moved.append(lax.ppermute(arrays[shift], axis, pairs))  14.2 us
    pallas_call x4, Pallas kernels, form_spectrum(): pl.pallas_call(spectrum_kernel, out_shape=jax.ShapeDtypeStruct((bins, hei...  11.7 us
    all_to_all x2, starting transfers between devices, local(): lax.all_to_all(array, 'dop', split_axis=0, concat_axis=0, tiled=True)  9.91 us
    ppermute x4, starting transfers between devices, shifted(): return lax.ppermute(array, axis, pairs)  7.84 us
    pallas_call x2, Pallas kernels, select_gates(): pl.pallas_call(functools.partial(select_kernel, owners=owners, ranges=ran...  7.02 us
  transfers between devices with their start and end apart: 18, of which 12 were waited for; matrix products, arithmetic and copies ran while one was open for 1% of the time, Pallas kernels for 37%

profile of v1, /device:TPU:1, one launch (start us, length us, event | category | flops | bytes accessed | tf_op | source)
XLA Modules:
  0.0 201.1 jit_solution(10463529350258228783)
XLA Ops:
  0.0 1.3 rim_rows.7
  1.3 2.0 collective-permute-start.3
  3.3 1.3 rim_rows.4
  4.5 1.9 collective-permute-start
  6.5 2.1 %rim_rows.5 = bf16[2,16,64,128]{3,2,1,0:T(8,128)(2,1)} custom-call(f32[2,64,128,128]{3,2,1,0:T(8,128)} %own_ref.7), custom_call_target="tpu_custom_call" | custom-call | tf_op jit(solution)/shard_map/rim_rows/pallas_call | solution.py:77
  8.6 2.0 %collective-permute-start.1 = (bf16[2,16,64,128]{3,2,1,0:T(8,128)(2,1)}, bf16[2,16,64,128]{3,2,1,0:T(8,128)(2,1)S(1)}, u32[]{:S(2)}, u32[]{:S(2)}) collective-permute-start(bf16[2,16,64,128]{3,2,1,0:T(8,128)(2,1)} %rim_rows.5), channel_id=1, source_target_pairs={{1,0},{2,1},{3,2},{5,4},{6,5},{7,6},{9,8},{10,9},{11,10},{13,12},{... | collective-permute-start | bytes 1572872 | tf_op jit(solution)/shard_map/ppermute | solution.py:22
  10.6 2.1 %rim_rows.6 = bf16[2,16,64,128]{3,2,1,0:T(8,128)(2,1)} custom-call(f32[2,64,128,128]{3,2,1,0:T(8,128)} %own_ref.7), custom_call_target="tpu_custom_call" | custom-call | tf_op jit(solution)/shard_map/rim_rows/pallas_call | solution.py:77
  12.7 1.9 collective-permute-start.2
  14.6 0.3 fusion.7
  14.9 0.3 negate_convert_fusion
  16.1 2.9 %form_spectrum.7.refs_3_ = bf16[128,32,128]{2,1,0:T(8,128)(2,1)S(1)} custom-call(bf16[256,512]{1,0:T(8,128)(2,1)S(1)} %filter_rows.1.rows_ref, bf16[256,256]{1,0:T(8,128)(2,1)S(1)} %bitcast.16, f32[2,64,128,128]{3,2,1,0:T(8,128)} %own_ref.7, bf16[2,16,64,128]{3,2,1,0:T(8,128)(2,1)S(1)} %collective-permute-done.3.next_ref), custom_call_target="tpu_custom_call" | custom-call | flops 805306368 | bytes 2097152 | tf_op jit(solution)/shard_map/form_spectrum/pallas_call | solution.py:139
  19.0 2.9 %form_spectrum.4.refs_0_ = bf16[128,32,128]{2,1,0:T(8,128)(2,1)S(1)} custom-call(bf16[256,512]{1,0:T(8,128)(2,1)S(1)} %filter_rows.1.rows_ref, bf16[256,256]{1,0:T(8,128)(2,1)S(1)} %bitcast.17, f32[2,64,128,128]{3,2,1,0:T(8,128)} %own_ref.7, bf16[2,16,64,128]{3,2,1,0:T(8,128)(2,1)S(1)} %collective-permute-done.next_ref), custom_call_target="tpu_custom_call" | custom-call | flops 805306368 | bytes 2097152 | tf_op jit(solution)/shard_map/form_spectrum/pallas_call | solution.py:139
  21.9 2.0 collective-permute-done.1.next_ref
  23.9 0.8 copy-done.3
  24.7 1.0 copy-done.4
  25.7 2.9 %form_spectrum.5.refs_1_ = bf16[128,32,128]{2,1,0:T(8,128)(2,1)S(1)} custom-call(bf16[256,512]{1,0:T(8,128)(2,1)S(1)} %filter_rows.1.rows_ref, bf16[256,256]{1,0:T(8,128)(2,1)S(1)} %bitcast.18, f32[2,64,128,128]{3,2,1,0:T(8,128)} %own_ref.7, bf16[2,16,64,128]{3,2,1,0:T(8,128)(2,1)S(1)} %copy-done.4), custom_call_target="tpu_custom_call" | custom-call | flops 805306368 | bytes 2097152 | tf_op jit(solution)/shard_map/form_spectrum/pallas_call | solution.py:139
  28.6 1.0 collective-permute-done.2.next_ref
  29.6 3.0 %form_spectrum.6.refs_2_ = bf16[128,32,128]{2,1,0:T(8,128)(2,1)S(1)} custom-call(bf16[256,512]{1,0:T(8,128)(2,1)S(1)} %filter_rows.1.rows_ref, bf16[256,256]{1,0:T(8,128)(2,1)S(1)} %bitcast.19, f32[2,64,128,128]{3,2,1,0:T(8,128)} %own_ref.7, bf16[2,16,64,128]{3,2,1,0:T(8,128)(2,1)} %collective-permute-done.2.next_ref), custom_call_target="tpu_custom_call" | custom-call | flops 805306368 | bytes 2097152 | tf_op jit(solution)/shard_map/form_spectrum/pallas_call | solution.py:139
  32.6 3.5 %select_gates.3 = bf16[8,8,128,128]{3,2,1,0:T(8,128)(2,1)} custom-call(s32[18]{0:T(128)S(1)} %pad_add_fusion.1.index_ref, s32[128,128]{1,0:T(8,128)S(1)} %pad_add_fusion.gates_ref, bf16[128,32,128]{2,1,0:T(8,128)(2,1)S(1)} %form_spectrum.4.refs_0_, bf16[128,32,128]{2,1,0:T(8,128)(2,1)S(1)} %form_spectrum.5.refs_1_, ...), custom_call_target="tpu_custom_call" | custom-call | flops 536870912 | bytes 2097152 | tf_op jit(solution)/shard_map/select_gates/pallas_call | solution.py:204
  36.1 1.0 copy-done.1
  37.1 5.6 %all-to-all-start.1 = ((bf16[8,8,128,128]{3,2,1,0:T(8,128)(2,1)}), bf16[8,8,128,128]{3,2,1,0:T(8,128)(2,1)}, u32[]{:S(2)}, u32[]{:S(2)}) async-start(bf16[8,8,128,128]{3,2,1,0:T(8,128)(2,1)} %select_gates.3), calls=%async_computation.1 | async-start | bytes 4194304 | tf_op jit(solution)/shard_map/all_to_all | solution.py:609
  42.6 1.2 copy-done.2
  43.9 3.5 %select_gates.2.refs_0_ = bf16[8,8,128,128]{3,2,1,0:T(8,128)(2,1)} custom-call(s32[18]{0:T(128)S(1)} %pad_add_fusion.1.index_ref, s32[128,128]{1,0:T(8,128)S(1)} %pad_add_fusion.gates_ref, bf16[128,32,128]{2,1,0:T(8,128)(2,1)S(1)} %form_spectrum.4.refs_0_, bf16[128,32,128]{2,1,0:T(8,128)(2,1)S(1)} %form_spectrum.5.refs_1_, ...), custom_call_target="tpu_custom_call" | custom-call | flops 536870912 | bytes 2097152 | tf_op jit(solution)/shard_map/select_gates/pallas_call | solution.py:204
  47.4 41.2 %all-to-all-done.1.arrived_ref = bf16[8,8,128,128]{3,2,1,0:T(8,128)(2,1)} async-done(((bf16[8,8,128,128]{3,2,1,0:T(8,128)(2,1)}), bf16[8,8,128,128]{3,2,1,0:T(8,128)(2,1)}, u32[]{:S(2)}, u32[]{:S(2)}) %all-to-all-start.1) | async-done | bytes 2097184 | tf_op jit(solution)/shard_map/all_to_all | solution.py:609
  88.6 4.4 %all-to-all-start = ((bf16[8,8,128,128]{3,2,1,0:T(8,128)(2,1)}), bf16[8,8,128,128]{3,2,1,0:T(8,128)(2,1)}, u32[]{:S(2)}, u32[]{:S(2)}) async-start(bf16[8,8,128,128]{3,2,1,0:T(8,128)(2,1)} %select_gates.2.refs_0_), calls=%async_computation | async-start | bytes 4194304 | tf_op jit(solution)/shard_map/all_to_all | solution.py:609
  92.9 0.2 copy.21.weights_ref
  93.2 2.6 %form_beams.2 = (bf16[2,384,128]{2,1,0:T(8,128)(2,1)S(1)}, bf16[2,384,128]{2,1,0:T(8,128)(2,1)S(1)}, bf16[2,384,128]{2,1,0:T(8,128)(2,1)S(1)}, bf16[2,384,128]{2,1,0:T(8,128)(2,1)S(1)}) custom-call(s32[18]{0:T(128)S(1)} %pad_add_fusion.1.index_ref, bf16[2,512,192]{2,1,0:T(8,128)(2,1)S(1)} %copy.21.weights_ref, ...), custom_call_target="tpu_custom_call" | custom-call | flops 805306368 | bytes 2097152 | tf_op jit(solution)/shard_map/form_beams/pallas_call | solution.py:262
  95.8 4.9 %collective-permute-start.4 = (bf16[2,384,128]{2,1,0:T(8,128)(2,1)S(1)}, bf16[2,384,128]{2,1,0:T(8,128)(2,1)S(1)}, u32[]{:S(2)}, u32[]{:S(2)}) collective-permute-start(bf16[2,384,128]{2,1,0:T(8,128)(2,1)S(1)} %get-tuple-element.22), channel_id=1, source_target_pairs={{0,1},{1,2},{2,3},{3,0},{4,5},{5,6},{6,7},{7,4},{8,9},{9,10},{10,1... | collective-permute-start | bytes 589832 | tf_op jit(solution)/shard_map/ppermute | solution.py:287
  100.7 0.5 collective-permute-start.6
  101.3 3.5 %collective-permute-done.4.refs_1_ = bf16[2,384,128]{2,1,0:T(8,128)(2,1)S(1)} collective-permute-done((bf16[2,384,128]{2,1,0:T(8,128)(2,1)S(1)}, bf16[2,384,128]{2,1,0:T(8,128)(2,1)S(1)}, u32[]{:S(2)}, u32[]{:S(2)}) %collective-permute-start.4) | collective-permute-done | bytes 196640 | tf_op jit(solution)/shard_map/ppermute | solution.py:287
  104.8 4.8 %collective-permute-done.5.refs_2_ = bf16[2,384,128]{2,1,0:T(8,128)(2,1)S(1)} collective-permute-done((bf16[2,384,128]{2,1,0:T(8,128)(2,1)S(1)}, bf16[2,384,128]{2,1,0:T(8,128)(2,1)S(1)}, u32[]{:S(2)}, u32[]{:S(2)}) %collective-permute-start.5) | collective-permute-done | bytes 196640 | tf_op jit(solution)/shard_map/ppermute | solution.py:287
  109.6 0.6 collective-permute-done.6.refs_3_
  110.2 24.3 %factor_slots.2 = (bf16[4,96,384]{2,1,0:T(8,128)(2,1)S(1)}, bf16[4,96,384]{2,1,0:T(8,128)(2,1)S(1)}, bf16[4,96,384]{2,1,0:T(8,128)(2,1)S(1)}, bf16[4,96,384]{2,1,0:T(8,128)(2,1)S(1)}) custom-call(s32[18]{0:T(128)S(1)} %pad_add_fusion.1.index_ref, s32[128,192]{1,0:T(8,128)S(1)} %copy.22.pivots_ref, bf16[2,384,128]{2,1,0:T(8,128)(2,1)S(1)} %get-tuple-element.21.refs_0_, ...), custom_call_target="tpu_custom_call" | custom-call | flops 226492416 | bytes 786432 | tf_op jit(solution)/shard_map/factor_slots/pallas_call | solution.py:494
  134.5 7.3 %all-to-all-done.arrived_ref = bf16[8,8,128,128]{3,2,1,0:T(8,128)(2,1)} async-done(((bf16[8,8,128,128]{3,2,1,0:T(8,128)(2,1)}), bf16[8,8,128,128]{3,2,1,0:T(8,128)(2,1)}, u32[]{:S(2)}, u32[]{:S(2)}) %all-to-all-start) | async-done | bytes 2097184 | tf_op jit(solution)/shard_map/all_to_all | solution.py:609
  141.8 2.6 %form_beams.3 = (bf16[2,384,128]{2,1,0:T(8,128)(2,1)S(1)}, bf16[2,384,128]{2,1,0:T(8,128)(2,1)S(1)}, bf16[2,384,128]{2,1,0:T(8,128)(2,1)S(1)}, bf16[2,384,128]{2,1,0:T(8,128)(2,1)S(1)}) custom-call(s32[18]{0:T(128)S(1)} %pad_add_fusion.1.index_ref, bf16[2,512,192]{2,1,0:T(8,128)(2,1)S(1)} %copy.21.weights_ref, ...), custom_call_target="tpu_custom_call" | custom-call | flops 805306368 | bytes 2097152 | tf_op jit(solution)/shard_map/form_beams/pallas_call | solution.py:262
  144.4 4.8 %collective-permute-start.7 = (bf16[2,384,128]{2,1,0:T(8,128)(2,1)S(1)}, bf16[2,384,128]{2,1,0:T(8,128)(2,1)S(1)}, u32[]{:S(2)}, u32[]{:S(2)}) collective-permute-start(bf16[2,384,128]{2,1,0:T(8,128)(2,1)S(1)} %get-tuple-element.27), channel_id=1, source_target_pairs={{0,1},{1,2},{2,3},{3,0},{4,5},{5,6},{6,7},{7,4},{8,9},{9,10},{10,1... | collective-permute-start | bytes 589832 | tf_op jit(solution)/shard_map/ppermute | solution.py:287
  149.2 0.5 collective-permute-start.9
  149.7 1.0 collective-permute-start.14
  150.7 2.6 %collective-permute-done.7.refs_1_ = bf16[2,384,128]{2,1,0:T(8,128)(2,1)S(1)} collective-permute-done((bf16[2,384,128]{2,1,0:T(8,128)(2,1)S(1)}, bf16[2,384,128]{2,1,0:T(8,128)(2,1)S(1)}, u32[]{:S(2)}, u32[]{:S(2)}) %collective-permute-start.7) | collective-permute-done | bytes 196640 | tf_op jit(solution)/shard_map/ppermute | solution.py:287
  153.3 4.2 %collective-permute-done.8.refs_2_ = bf16[2,384,128]{2,1,0:T(8,128)(2,1)S(1)} collective-permute-done((bf16[2,384,128]{2,1,0:T(8,128)(2,1)S(1)}, bf16[2,384,128]{2,1,0:T(8,128)(2,1)S(1)}, u32[]{:S(2)}, u32[]{:S(2)}) %collective-permute-start.8) | collective-permute-done | bytes 196640 | tf_op jit(solution)/shard_map/ppermute | solution.py:287
  157.5 1.5 collective-permute-done.9.refs_3_
  159.0 24.2 %factor_slots.3 = (bf16[4,96,384]{2,1,0:T(8,128)(2,1)S(1)}, bf16[4,96,384]{2,1,0:T(8,128)(2,1)S(1)}, bf16[4,96,384]{2,1,0:T(8,128)(2,1)S(1)}, bf16[4,96,384]{2,1,0:T(8,128)(2,1)S(1)}) custom-call(s32[18]{0:T(128)S(1)} %pad_add_fusion.1.index_ref, s32[128,192]{1,0:T(8,128)S(1)} %copy.22.pivots_ref, bf16[2,384,128]{2,1,0:T(8,128)(2,1)S(1)} %get-tuple-element.26.refs_0_, ...), custom_call_target="tpu_custom_call" | custom-call | flops 226492416 | bytes 786432 | tf_op jit(solution)/shard_map/factor_slots/pallas_call | solution.py:494
  183.4 1.7 collective-permute-start.11
  185.0 0.7 collective-permute-start.12
  185.8 2.6 %place_rows.2.refs_4_ = f32[32,96,384]{2,1,0:T(8,128)} custom-call(s32[18]{0:T(128)S(1)} %pad_add_fusion.1.index_ref, bf16[4,96,384]{2,1,0:T(8,128)(2,1)S(1)} %get-tuple-element.25.refs_0_, bf16[4,96,384]{2,1,0:T(8,128)(2,1)S(1)} %collective-permute-done.13.refs_1_, bf16[4,96,384]{2,1,0:T(8,128)(2,1)S(1)} %collective-permute-done.14.refs_2_, ...), custom_call_target="tpu_custom_call" | custom-call | tf_op jit(solution)/shard_map/place_rows/pallas_call | solution.py:551
  188.3 9.5 %collective-permute-done.11.refs_2_ = bf16[4,96,384]{2,1,0:T(8,128)(2,1)S(1)} collective-permute-done((bf16[4,96,384]{2,1,0:T(8,128)(2,1)S(1)}, bf16[4,96,384]{2,1,0:T(8,128)(2,1)S(1)}, u32[]{:S(2)}, u32[]{:S(2)}) %collective-permute-start.11) | collective-permute-done | bytes 294944 | tf_op jit(solution)/shard_map/ppermute | solution.py:287
  197.8 0.8 collective-permute-done.12.refs_3_
  198.6 2.6 %place_rows.3 = f32[32,96,384]{2,1,0:T(8,128)} custom-call(s32[18]{0:T(128)S(1)} %pad_add_fusion.1.index_ref, bf16[4,96,384]{2,1,0:T(8,128)(2,1)S(1)} %get-tuple-element.30.refs_0_, bf16[4,96,384]{2,1,0:T(8,128)(2,1)S(1)} %collective-permute-done.10.refs_1_, bf16[4,96,384]{2,1,0:T(8,128)(2,1)S(1)} %collective-permute-done.11.refs_2_, ...), custom_call_target="tpu_custom_call", output_to_operand_aliasing={{}: (5, {})} | custom-call | tf_op jit(solution)/shard_map/place_rows/pallas_call | solution.py:551
  (40 shorter events, 1.0 us)
Async XLA Ops:
  1.3 14.8 %collective-permute-start.3 = (bf16[2,16,64,128]{3,2,1,0:T(8,128)(2,1)S(1)}, bf16[2,16,64,128]{3,2,1,0:T(8,128)(2,1)S(1)}, u32[]{:S(2)}, u32[]{:S(2)}) collective-permute-start(bf16[2,16,64,128]{3,2,1,0:T(8,128)(2,1)S(1)} %rim_rows.7), channel_id=1, source_target_pairs={{1,0},{2,1},{3,2},{5,4},{6,5},{7,6},{9,8},{10,9},{11,10},{13,12},{... | collective-permute-start | bytes 1572872 | tf_op jit(solution)/shard_map/ppermute | solution.py:22
  4.5 14.4 %collective-permute-start = (bf16[2,16,64,128]{3,2,1,0:T(8,128)(2,1)S(1)}, bf16[2,16,64,128]{3,2,1,0:T(8,128)(2,1)S(1)}, u32[]{:S(2)}, u32[]{:S(2)}) collective-permute-start(bf16[2,16,64,128]{3,2,1,0:T(8,128)(2,1)S(1)} %rim_rows.4), channel_id=1, source_target_pairs={{1,0},{2,1},{3,2},{5,4},{6,5},{7,6},{9,8},{10,9},{11,10},{13,12},{... | collective-permute-start | bytes 1572872 | tf_op jit(solution)/shard_map/ppermute | solution.py:22
  8.6 6.6 %copy-start.9 = (s32[8]{0:T(128)S(1)}, s32[8]{0:T(128)}, u32[]{:S(2)}) copy-start(s32[8]{0:T(128)} %param.10) | copy-start | bytes 100
  8.6 6.9 %copy-start.7 = (s32[128,64]{0,1:T(8,128)S(1)}, s32[128,64]{0,1:T(8,128)}, u32[]{:S(2)}) copy-start(s32[128,64]{0,1:T(8,128)} %param.11) | copy-start | bytes 98308
  8.6 7.2 %copy-start.8 = (f32[2,64]{1,0:T(2,128)S(1)}, f32[2,64]{1,0:T(2,128)}, u32[]{:S(2)}) copy-start(f32[2,64]{1,0:T(2,128)} %param.7) | copy-start | bytes 1540
  8.6 15.3 %collective-permute-start.1 = (bf16[2,16,64,128]{3,2,1,0:T(8,128)(2,1)}, bf16[2,16,64,128]{3,2,1,0:T(8,128)(2,1)S(1)}, u32[]{:S(2)}, u32[]{:S(2)}) collective-permute-start(bf16[2,16,64,128]{3,2,1,0:T(8,128)(2,1)} %rim_rows.5), channel_id=1, source_target_pairs={{1,0},{2,1},{3,2},{5,4},{6,5},{7,6},{9,8},{10,9},{11,10},{13,12},{... | collective-permute-start | bytes 1572872 | tf_op jit(solution)/shard_map/ppermute | solution.py:22
  12.7 16.9 %collective-permute-start.2 = (bf16[2,16,64,128]{3,2,1,0:T(8,128)(2,1)}, bf16[2,16,64,128]{3,2,1,0:T(8,128)(2,1)}, u32[]{:S(2)}, u32[]{:S(2)}) collective-permute-start(bf16[2,16,64,128]{3,2,1,0:T(8,128)(2,1)} %rim_rows.6), channel_id=1, source_target_pairs={{1,0},{2,1},{3,2},{5,4},{6,5},{7,6},{9,8},{10,9},{11,10},{13,12},{... | collective-permute-start | bytes 1572872 | tf_op jit(solution)/shard_map/ppermute | solution.py:22
  23.9 0.8 copy-start.3
  24.7 1.0 copy-start.4
  36.1 1.0 copy-start.1
  37.1 51.5 %all-to-all-start.1 = ((bf16[8,8,128,128]{3,2,1,0:T(8,128)(2,1)}), bf16[8,8,128,128]{3,2,1,0:T(8,128)(2,1)}, u32[]{:S(2)}, u32[]{:S(2)}) async-start(bf16[8,8,128,128]{3,2,1,0:T(8,128)(2,1)} %select_gates.3), calls=%async_computation.1 | async-start | bytes 4194304 | tf_op jit(solution)/shard_map/all_to_all | solution.py:609
  42.6 1.2 copy-start.2
  47.3 45.6 %copy-start.5 = (bf16[2,512,192]{1,2,0:T(8,128)(2,1)S(1)}, bf16[2,512,192]{1,2,0:T(8,128)(2,1)}, u32[]{:S(2)}) copy-start(bf16[2,512,192]{1,2,0:T(8,128)(2,1)} %param.8) | copy-start | bytes 1179652
  47.3 45.8 %copy-start = (bf16[8,8,128,128]{3,2,1,0:T(8,128)(2,1)S(1)}, bf16[8,8,128,128]{3,2,1,0:T(8,128)(2,1)}, u32[]{:S(2)}) copy-start(bf16[8,8,128,128]{3,2,1,0:T(8,128)(2,1)} %select_gates.2.refs_0_) | copy-start | bytes 6291460
  88.6 53.3 %all-to-all-start = ((bf16[8,8,128,128]{3,2,1,0:T(8,128)(2,1)}), bf16[8,8,128,128]{3,2,1,0:T(8,128)(2,1)}, u32[]{:S(2)}, u32[]{:S(2)}) async-start(bf16[8,8,128,128]{3,2,1,0:T(8,128)(2,1)} %select_gates.2.refs_0_), calls=%async_computation | async-start | bytes 4194304 | tf_op jit(solution)/shard_map/all_to_all | solution.py:609
  93.1 8.1 %copy-start.6 = (s32[128,192]{0,1:T(8,128)S(1)}, s32[128,192]{0,1:T(8,128)}, u32[]{:S(2)}) copy-start(s32[128,192]{0,1:T(8,128)} %param.9) | copy-start | bytes 294916
  95.8 9.0 %collective-permute-start.4 = (bf16[2,384,128]{2,1,0:T(8,128)(2,1)S(1)}, bf16[2,384,128]{2,1,0:T(8,128)(2,1)S(1)}, u32[]{:S(2)}, u32[]{:S(2)}) collective-permute-start(bf16[2,384,128]{2,1,0:T(8,128)(2,1)S(1)} %get-tuple-element.22), channel_id=1, source_target_pairs={{0,1},{1,2},{2,3},{3,0},{4,5},{5,6},{6,7},{7,4},{8,9},{9,10},{10,1... | collective-permute-start | bytes 589832 | tf_op jit(solution)/shard_map/ppermute | solution.py:287
  100.7 8.9 %collective-permute-start.5 = (bf16[2,384,128]{2,1,0:T(8,128)(2,1)S(1)}, bf16[2,384,128]{2,1,0:T(8,128)(2,1)S(1)}, u32[]{:S(2)}, u32[]{:S(2)}) collective-permute-start(bf16[2,384,128]{2,1,0:T(8,128)(2,1)S(1)} %get-tuple-element.23), channel_id=1, source_target_pairs={{0,2},{1,3},{2,0},{3,1},{4,6},{5,7},{6,4},{7,5},{8,10},{9,11},{10,... | collective-permute-start | bytes 589832 | tf_op jit(solution)/shard_map/ppermute | solution.py:287
  100.7 9.5 %collective-permute-start.6 = (bf16[2,384,128]{2,1,0:T(8,128)(2,1)S(1)}, bf16[2,384,128]{2,1,0:T(8,128)(2,1)S(1)}, u32[]{:S(2)}, u32[]{:S(2)}) collective-permute-start(bf16[2,384,128]{2,1,0:T(8,128)(2,1)S(1)} %get-tuple-element.24), channel_id=1, source_target_pairs={{0,3},{1,0},{2,1},{3,2},{4,7},{5,4},{6,5},{7,6},{8,11},{9,8},{10,9... | collective-permute-start | bytes 589832 | tf_op jit(solution)/shard_map/ppermute | solution.py:287
  134.5 50.6 %collective-permute-start.13 = (bf16[4,96,384]{2,1,0:T(8,128)(2,1)S(1)}, bf16[4,96,384]{2,1,0:T(8,128)(2,1)S(1)}, u32[]{:S(2)}, u32[]{:S(2)}) collective-permute-start(bf16[4,96,384]{2,1,0:T(8,128)(2,1)S(1)} %get-tuple-element.34), channel_id=1, source_target_pairs={{0,1},{1,2},{2,3},{3,0},{4,5},{5,6},{6,7},{7,4},{8,9},{9,10},{10,1... | collective-permute-start | bytes 884744 | tf_op jit(solution)/shard_map/ppermute | solution.py:287
  144.4 8.9 %collective-permute-start.7 = (bf16[2,384,128]{2,1,0:T(8,128)(2,1)S(1)}, bf16[2,384,128]{2,1,0:T(8,128)(2,1)S(1)}, u32[]{:S(2)}, u32[]{:S(2)}) collective-permute-start(bf16[2,384,128]{2,1,0:T(8,128)(2,1)S(1)} %get-tuple-element.27), channel_id=1, source_target_pairs={{0,1},{1,2},{2,3},{3,0},{4,5},{5,6},{6,7},{7,4},{8,9},{9,10},{10,1... | collective-permute-start | bytes 589832 | tf_op jit(solution)/shard_map/ppermute | solution.py:287
  149.2 8.3 %collective-permute-start.8 = (bf16[2,384,128]{2,1,0:T(8,128)(2,1)S(1)}, bf16[2,384,128]{2,1,0:T(8,128)(2,1)S(1)}, u32[]{:S(2)}, u32[]{:S(2)}) collective-permute-start(bf16[2,384,128]{2,1,0:T(8,128)(2,1)S(1)} %get-tuple-element.28), channel_id=1, source_target_pairs={{0,2},{1,3},{2,0},{3,1},{4,6},{5,7},{6,4},{7,5},{8,10},{9,11},{10,... | collective-permute-start | bytes 589832 | tf_op jit(solution)/shard_map/ppermute | solution.py:287
  149.2 9.8 %collective-permute-start.9 = (bf16[2,384,128]{2,1,0:T(8,128)(2,1)S(1)}, bf16[2,384,128]{2,1,0:T(8,128)(2,1)S(1)}, u32[]{:S(2)}, u32[]{:S(2)}) collective-permute-start(bf16[2,384,128]{2,1,0:T(8,128)(2,1)S(1)} %get-tuple-element.29), channel_id=1, source_target_pairs={{0,3},{1,0},{2,1},{3,2},{4,7},{5,4},{6,5},{7,6},{8,11},{9,8},{10,9... | collective-permute-start | bytes 589832 | tf_op jit(solution)/shard_map/ppermute | solution.py:287
  149.7 36.1 %collective-permute-start.14 = (bf16[4,96,384]{2,1,0:T(8,128)(2,1)S(1)}, bf16[4,96,384]{2,1,0:T(8,128)(2,1)S(1)}, u32[]{:S(2)}, u32[]{:S(2)}) collective-permute-start(bf16[4,96,384]{2,1,0:T(8,128)(2,1)S(1)} %get-tuple-element.35), channel_id=1, source_target_pairs={{0,2},{1,3},{2,0},{3,1},{4,6},{5,7},{6,4},{7,5},{8,10},{9,11},{10,... | collective-permute-start | bytes 884744 | tf_op jit(solution)/shard_map/ppermute | solution.py:287
  153.3 32.4 %collective-permute-start.15 = (bf16[4,96,384]{2,1,0:T(8,128)(2,1)S(1)}, bf16[4,96,384]{2,1,0:T(8,128)(2,1)S(1)}, u32[]{:S(2)}, u32[]{:S(2)}) collective-permute-start(bf16[4,96,384]{2,1,0:T(8,128)(2,1)S(1)} %get-tuple-element.36), channel_id=1, source_target_pairs={{0,3},{1,0},{2,1},{3,2},{4,7},{5,4},{6,5},{7,6},{8,11},{9,8},{10,9... | collective-permute-start | bytes 884744 | tf_op jit(solution)/shard_map/ppermute | solution.py:287
  183.3 5.0 %collective-permute-start.10 = (bf16[4,96,384]{2,1,0:T(8,128)(2,1)S(1)}, bf16[4,96,384]{2,1,0:T(8,128)(2,1)S(1)}, u32[]{:S(2)}, u32[]{:S(2)}) collective-permute-start(bf16[4,96,384]{2,1,0:T(8,128)(2,1)S(1)} %get-tuple-element.31), channel_id=1, source_target_pairs={{0,1},{1,2},{2,3},{3,0},{4,5},{5,6},{6,7},{7,4},{8,9},{9,10},{10,1... | collective-permute-start | bytes 884744 | tf_op jit(solution)/shard_map/ppermute | solution.py:287
  183.4 14.4 %collective-permute-start.11 = (bf16[4,96,384]{2,1,0:T(8,128)(2,1)S(1)}, bf16[4,96,384]{2,1,0:T(8,128)(2,1)S(1)}, u32[]{:S(2)}, u32[]{:S(2)}) collective-permute-start(bf16[4,96,384]{2,1,0:T(8,128)(2,1)S(1)} %get-tuple-element.32), channel_id=1, source_target_pairs={{0,2},{1,3},{2,0},{3,1},{4,6},{5,7},{6,4},{7,5},{8,10},{9,11},{10,... | collective-permute-start | bytes 884744 | tf_op jit(solution)/shard_map/ppermute | solution.py:287
  185.0 13.5 %collective-permute-start.12 = (bf16[4,96,384]{2,1,0:T(8,128)(2,1)S(1)}, bf16[4,96,384]{2,1,0:T(8,128)(2,1)S(1)}, u32[]{:S(2)}, u32[]{:S(2)}) collective-permute-start(bf16[4,96,384]{2,1,0:T(8,128)(2,1)S(1)} %get-tuple-element.33), channel_id=1, source_target_pairs={{0,3},{1,0},{2,1},{3,2},{4,7},{5,4},{6,5},{7,6},{8,11},{9,8},{10,9... | collective-permute-start | bytes 884744 | tf_op jit(solution)/shard_map/ppermute | solution.py:287

commit v2 on v1

--- a/solution.py
+++ b/solution.py
@@ -225,19 +225,17 @@
     )(index, gates, *spectra)
 
 
-def beam_kernel(index_ref, weights_ref, arrived_ref, *refs, ranges):
-    out_refs = refs[-ranges:]
-    sources, groups, rows, width = arrived_ref.shape
-    share = groups // ranges
+def beam_kernel(weights_ref, arrived_ref, *refs):
+    out_ref = refs[-1]
+    sources, ranges, groups, rows, width = arrived_ref.shape
     dof = weights_ref.shape[2]
     half = rows // 2
-    for shift, out_ref in enumerate(out_refs):
-        lead = lax.rem(index_ref[1] + shift, ranges) * share
+    for block in range(ranges):
         packed = jnp.concatenate(
             [
-                arrived_ref[:, lead + g, s * half : (s + 1) * half].reshape(sources * half, width)
+                arrived_ref[:, block, g, s * half : (s + 1) * half].reshape(sources * half, width)
                 for s in range(2)
-                for g in range(share)
+                for g in range(groups)
             ],
             axis=1,
         )
@@ -247,28 +245,24 @@
             )
             for part in range(2)
         ]
-        middle = share * width
+        middle = groups * width
         real_part = by_real[:, :middle] + by_imag[:, middle:]
         imag_part = by_real[:, middle:] - by_imag[:, :middle]
-        for g in range(share):
+        for g in range(groups):
             span = slice(g * width, (g + 1) * width)
-            out_ref[g, :dof] = real_part[:, span].astype(BF16)
-            out_ref[g, dof:] = imag_part[:, span].astype(BF16)
-
-
-def form_beams(arrived, weights, index, ranges, earlier):
-    _, groups, _, width = arrived.shape
-    shape = (groups // ranges, 2 * weights.shape[2], width)
+            out_ref[block, g, :dof] = real_part[:, span].astype(BF16)
+            out_ref[block, g, dof:] = imag_part[:, span].astype(BF16)
+
+
+def form_beams(arrived, weights, earlier):
+    _, ranges, groups, _, width = arrived.shape
+    shape = (ranges, groups, 2 * weights.shape[2], width)
     return pl.pallas_call(
-        functools.partial(beam_kernel, ranges=ranges),
-        out_shape=[jax.ShapeDtypeStruct(shape, BF16)] * ranges,
-        in_specs=[
-            pl.BlockSpec(memory_space=pltpu.SMEM),
-            pl.BlockSpec(memory_space=pltpu.VMEM),
-            pl.BlockSpec(memory_space=pltpu.VMEM),
-        ]
+        beam_kernel,
+        out_shape=jax.ShapeDtypeStruct(shape, BF16),
+        in_specs=[pl.BlockSpec(memory_space=pltpu.VMEM)] * 2
         + [pl.BlockSpec(memory_space=pl.ANY)] * len(earlier),
-        out_specs=[pl.BlockSpec(memory_space=pltpu.VMEM)] * ranges,
+        out_specs=pl.BlockSpec(memory_space=pltpu.VMEM),
         compiler_params=PARAMS,
         cost_estimate=pl.CostEstimate(
             flops=4 * arrived.size * weights.shape[2],
@@ -276,7 +270,7 @@
             transcendentals=0,
         ),
         name="form_beams",
-    )(index, weights, arrived, *earlier)
+    )(weights, arrived, *earlier)
 
 
 def exchange(arrays, axis):
@@ -341,47 +335,48 @@
     return guess * (2.0 - value * guess)
 
 
+def tree_sum(terms):
+    while len(terms) > 1:
+        terms = [x + y for x, y in zip(terms[::2], terms[1::2])]
+    return terms[0]
+
+
 def eliminate(rows):
     scales = []
-
-    def diagonal_piece(first):
+    for first in range(0, PANEL, 8):
         span = range(first, first + 8)
-        return {(i, j): lane_spread(rows[i][0], j) for i in span for j in span if j >= i}
-
-    small = diagonal_piece(0)
-    for first in range(0, PANEL, 8):
-        stop = first + 8
-        following = diagonal_piece(stop) if stop < PANEL else {}
-        for t in range(first, stop, 2):
+        small = {(i, j): lane_spread(rows[i][0], j) for i in span for j in span if j >= i}
+        for t in range(first, first + 8, 2):
             u = t + 1
             inverse = refined_reciprocal(small[t, t])
             cross = small[t, t] * small[u, u] - small[t, u] * small[t, u]
             second = refined_reciprocal(cross) * small[t, t]
             scales += [lax.rsqrt(small[t, t]), lax.rsqrt(cross * inverse)]
             factor = small[t, u] * inverse
-            for j in range(u + 1, stop):
+            for j in range(u + 1, first + 8):
                 small[u, j] = small[u, j] - factor * small[t, j]
             rows[u] = [x - factor * y for x, y in zip(rows[u], rows[t])]
-            upper = {i: (small[t, i], small[u, i]) for i in range(u + 1, stop)}
-            for i in range(stop, PANEL):
-                upper[i] = (lane_spread(rows[t][0], i), lane_spread(rows[u][0], i))
-            scaled = {i: (x * inverse, y * second) for i, (x, y) in upper.items()}
-            for piece in (small, following):
-                for i, j in piece:
-                    if i > u:
-                        one, two = scaled[i]
-                        x, y = upper[j]
-                        piece[i, j] = piece[i, j] - one * x - two * y
-            for i, (one, two) in scaled.items():
-                rows[i] = [x - one * y - two * z for x, y, z in zip(rows[i], rows[t], rows[u])]
-        small = following
-    return [[x * scale for x in row] for row, scale in zip(rows, scales)]
+            for i in range(u + 1, first + 8):
+                one, two = small[t, i] * inverse, small[u, i] * second
+                for j in range(i, first + 8):
+                    small[i, j] = small[i, j] - one * small[t, j] - two * small[u, j]
+                rows[i] = [
+                    x - one * y - two * z for x, y, z in zip(rows[i], rows[t], rows[u])
+                ]
+        for t in span:
+            rows[t] = [x * scales[t] for x in rows[t]]
+        for i in range(first + 8, PANEL):
+            factors = [lane_spread(rows[t][0], i) for t in span]
+            rows[i] = [
+                x - tree_sum([f * rows[t][w] for f, t in zip(factors, span)])
+                for w, x in enumerate(rows[i])
+            ]
+    return rows
 
 
 def factor_kernel(
-    index_ref, pivots_ref, *refs, first, share_slots, ranges, waits, pack, count_rows
+    index_ref, pivots_ref, beams_ref, *refs, first, share_slots, ranges, pack, count_rows
 ):
-    beams_refs, refs = refs[:ranges], refs[ranges + waits :]
     out_refs = refs[:ranges]
     arriving, leaving, *scratch = refs[ranges:]
     slots = len(scratch) // 3
@@ -398,7 +393,7 @@
         group, part = divmod(slot, pack)
         own_bin = jnp.minimum(bin_lead + slot, pivots_ref.shape[0] - 1)
         work[slot][...] = loaded_covariance(
-            [ref[group] for ref in beams_refs],
+            [beams_ref[r, group] for r in range(ranges)],
             pivots_ref[pl.ds(own_bin, 1), :],
             part,
             pack,
@@ -487,9 +482,8 @@
             out_ref[slot] = jnp.where(upper, piece, 0.0).astype(out_ref.dtype)
 
 
-def factor_slots(beams, pivots, index, first, slots, share_slots, pack, count_rows, earlier):
-    ranges = len(beams)
-    order = beams[0].shape[1]
+def factor_slots(beams, pivots, index, first, slots, share_slots, pack, count_rows):
+    ranges, _, order, _ = beams.shape
     height = -(-slots // 8) * 8
     return pl.pallas_call(
         functools.partial(
@@ -497,14 +491,12 @@
             first=first,
             share_slots=share_slots,
             ranges=ranges,
-            waits=len(earlier),
             pack=pack,
             count_rows=count_rows,
         ),
         out_shape=[jax.ShapeDtypeStruct((slots, order // ranges, order), BF16)] * ranges,
         in_specs=[pl.BlockSpec(memory_space=pltpu.SMEM)]
-        + [pl.BlockSpec(memory_space=pltpu.VMEM)] * (1 + ranges)
-        + [pl.BlockSpec(memory_space=pl.ANY)] * len(earlier),
+        + [pl.BlockSpec(memory_space=pltpu.VMEM)] * 2,
         out_specs=[pl.BlockSpec(memory_space=pltpu.VMEM)] * ranges,
         scratch_shapes=[pltpu.VMEM((order // LANES, PANEL * height, LANES), F32)] * 2
         + [pltpu.VMEM((order, order), F32) for _ in range(slots)]
@@ -513,11 +505,11 @@
         compiler_params=PARAMS,
         cost_estimate=pl.CostEstimate(
             flops=slots * order**3,
-            bytes_accessed=ranges * beams[0].size * 2,
+            bytes_accessed=beams.size * 2,
             transcendentals=0,
         ),
         name="factor_slots",
-    )(index, pivots, *beams, *earlier)
+    )(index, pivots, beams)
 
 
 def place_kernel(index_ref, *refs, first, share_slots, ranges):
@@ -565,9 +557,8 @@
 
 
 def slot_parts(share_slots, pack):
-    halves = 2 if share_slots % (2 * pack) == 0 else 1
-    count = share_slots // halves
-    return [(i * count, count) for i in range(halves)]
+    head = share_slots - pack
+    return [(0, head), (head, pack)] if head > 0 else [(0, share_slots)]
 
 
 def local(raw_echo, replica, beam_weights, pivots, owner_counts, train_gates):
@@ -605,15 +596,21 @@
         select_gates(spectra, index, gates, first, count, share_slots, owners, ranges, pack)
         for first, count in parts
     ]
+    axes = ("dop", "rng")
     sent = [
-        lax.all_to_all(array, "dop", split_axis=0, concat_axis=0, tiled=True) for array in outgoing
+        lax.all_to_all(
+            array.reshape(owners * ranges, -1, *array.shape[2:]),
+            axes,
+            split_axis=0,
+            concat_axis=0,
+            tiled=True,
+        ).reshape(owners, ranges, -1, *array.shape[2:])
+        for array in outgoing
     ]
     result, earlier = [], outgoing[1:]
     for (first, count), arrived in zip(parts, sent):
-        beams = exchange(form_beams(arrived, beam_weights, index, ranges, earlier), "rng")
-        factors = factor_slots(
-            beams, pivots, index, first, count, share_slots, pack, count_rows, []
-        )
+        beams = form_beams(arrived, beam_weights, earlier)
+        factors = factor_slots(beams, pivots, index, first, count, share_slots, pack, count_rows)
         earlier = factors[:1]
         rows = exchange(factors, "rng")
         result = [place_rows(index, rows, first, share_slots, result)]

time: 202 us -> 186 us (0.921)
  starting transfers between devices: 31.9 us -> 22.2 us
  waiting for transfers between devices: 78.9 us -> 70.6 us
  local copies, waits for them, and re-layouts: 4.6 us -> 11.5 us
  Pallas kernels: 84.5 us -> 79 us
    ppermute x12 -> x6, waiting for transfers between devices: 27.4 us -> 1.96 us  [exchange(): moved.append(lax.ppermute(arrays[shift], axis, pairs))]
    all_to_all x2, waiting for transfers between devices: 48.5 us -> 63.1 us  [local(): lax.all_to_all(array.reshape(owners * ranges, -1, *array.shape[2:]), axes...]
    ppermute x12 -> x6, starting transfers between devices: 14.2 us -> 4.94 us  [exchange(): moved.append(lax.ppermute(arrays[shift], axis, pairs))]
    unnamed x24 -> x36, local copies, waits for them, and re-layouts: 4.46 us -> 11.4 us
    pallas_call x2, Pallas kernels: 48.5 us -> 43.3 us  [factor_slots(): pl.pallas_call(functools.partial(factor_kernel, first=first, share_slots=...]
    ppermute x4, waiting for transfers between devices: 2.93 us -> 5.48 us  [shifted(): return lax.ppermute(array, axis, pairs)]
    pallas_call x2, Pallas kernels: 5.11 us -> 7.5 us  [place_rows(): pl.pallas_call(functools.partial(place_kernel, first=first, share_slots=s...]
  transfers between devices with their start and end apart: 18 -> 12, of which waited for: 12 -> 6; matrix products, arithmetic and copies ran while one was open for 1% -> 2% of each run, Pallas kernels for 37% -> 37%
where the time goes in v2:
time: 186 us; the launch traced here: 185 us
  Pallas kernels  79 us (42%)
  waiting for transfers between devices  70.6 us (38%)
  starting transfers between devices  22.2 us (12%)
  local copies, waits for them, and re-layouts  11.5 us (6%)
    all_to_all x2, waiting for transfers between devices, local(): lax.all_to_all(array.reshape(owners * ranges, -1, *array.shape[2:]), axes...  63.1 us
    pallas_call x2, Pallas kernels, factor_slots(): pl.pallas_call(functools.partial(factor_kernel, first=first, share_slots=...  43.3 us
    pallas_call x4, Pallas kernels, form_spectrum(): pl.pallas_call(spectrum_kernel, out_shape=jax.ShapeDtypeStruct((bins, hei...  11.8 us
    unnamed x36, local copies, waits for them, and re-layouts  11.4 us
    all_to_all x2, starting transfers between devices, local(): lax.all_to_all(array.reshape(owners * ranges, -1, *array.shape[2:]), axes...  9.4 us
    ppermute x4, starting transfers between devices, shifted(): return lax.ppermute(array, axis, pairs)  7.83 us
    pallas_call x2, Pallas kernels, place_rows(): pl.pallas_call(functools.partial(place_kernel, first=first, share_slots=s...  7.5 us
    pallas_call x4, Pallas kernels, rim_rows(): pl.pallas_call(rim_kernel, out_shape=jax.ShapeDtypeStruct(shape, BF16), g...  6.75 us
  transfers between devices with their start and end apart: 12, of which 6 were waited for; matrix products, arithmetic and copies ran while one was open for 2% of the time, Pallas kernels for 37%

profile of v2, /device:TPU:1, one launch (start us, length us, event | category | flops | bytes accessed | tf_op | source)
XLA Modules:
  0.0 184.6 jit_solution(11124253657188183276)
XLA Ops:
  0.0 2.1 %rim_rows.7 = bf16[2,16,64,128]{3,2,1,0:T(8,128)(2,1)} custom-call(f32[2,64,128,128]{3,2,1,0:T(8,128)} %own_ref.7), custom_call_target="tpu_custom_call" | custom-call | tf_op jit(solution)/shard_map/rim_rows/pallas_call | solution.py:77
  2.1 2.0 %collective-permute-start.3 = (bf16[2,16,64,128]{3,2,1,0:T(8,128)(2,1)}, bf16[2,16,64,128]{3,2,1,0:T(8,128)(2,1)S(1)}, u32[]{:S(2)}, u32[]{:S(2)}) collective-permute-start(bf16[2,16,64,128]{3,2,1,0:T(8,128)(2,1)} %rim_rows.7), channel_id=1, source_target_pairs={{1,0},{2,1},{3,2},{5,4},{6,5},{7,6},{9,8},{10,9},{11,10},{13,12},{... | collective-permute-start | bytes 1572872 | tf_op jit(solution)/shard_map/ppermute | solution.py:22
  4.1 2.1 %rim_rows.4 = bf16[2,16,64,128]{3,2,1,0:T(8,128)(2,1)} custom-call(f32[2,64,128,128]{3,2,1,0:T(8,128)} %own_ref.7), custom_call_target="tpu_custom_call" | custom-call | tf_op jit(solution)/shard_map/rim_rows/pallas_call | solution.py:77
  6.1 1.9 %collective-permute-start = (bf16[2,16,64,128]{3,2,1,0:T(8,128)(2,1)}, bf16[2,16,64,128]{3,2,1,0:T(8,128)(2,1)S(1)}, u32[]{:S(2)}, u32[]{:S(2)}) collective-permute-start(bf16[2,16,64,128]{3,2,1,0:T(8,128)(2,1)} %rim_rows.4), channel_id=1, source_target_pairs={{1,0},{2,1},{3,2},{5,4},{6,5},{7,6},{9,8},{10,9},{11,10},{13,12},{... | collective-permute-start | bytes 1572872 | tf_op jit(solution)/shard_map/ppermute | solution.py:22
  8.0 1.3 rim_rows.5
  9.4 2.1 %collective-permute-start.1 = (bf16[2,16,64,128]{3,2,1,0:T(8,128)(2,1)S(1)}, bf16[2,16,64,128]{3,2,1,0:T(8,128)(2,1)S(1)}, u32[]{:S(2)}, u32[]{:S(2)}) collective-permute-start(bf16[2,16,64,128]{3,2,1,0:T(8,128)(2,1)S(1)} %rim_rows.5), channel_id=1, source_target_pairs={{1,0},{2,1},{3,2},{5,4},{6,5},{7,6},{9,8},{10,9},{11,10},{13,12},{... | collective-permute-start | bytes 1572872 | tf_op jit(solution)/shard_map/ppermute | solution.py:22
  11.4 1.3 rim_rows.6
  12.7 1.9 %collective-permute-start.2 = (bf16[2,16,64,128]{3,2,1,0:T(8,128)(2,1)S(1)}, bf16[2,16,64,128]{3,2,1,0:T(8,128)(2,1)S(1)}, u32[]{:S(2)}, u32[]{:S(2)}) collective-permute-start(bf16[2,16,64,128]{3,2,1,0:T(8,128)(2,1)S(1)} %rim_rows.6), channel_id=1, source_target_pairs={{1,0},{2,1},{3,2},{5,4},{6,5},{7,6},{9,8},{10,9},{11,10},{13,12},{... | collective-permute-start | bytes 1572872 | tf_op jit(solution)/shard_map/ppermute | solution.py:22
  14.7 0.3 fusion.7
  14.9 0.3 negate_convert_fusion
  15.2 0.2 reduce-window.9
  15.6 0.1 copy.26
  15.8 0.1 filter_rows.1.rows_ref
  16.1 2.9 %form_spectrum.7.refs_3_ = bf16[128,32,128]{2,1,0:T(8,128)(2,1)S(1)} custom-call(bf16[256,512]{1,0:T(8,128)(2,1)S(1)} %filter_rows.1.rows_ref, bf16[256,256]{1,0:T(8,128)(2,1)S(1)} %bitcast.24, f32[2,64,128,128]{3,2,1,0:T(8,128)} %own_ref.7, bf16[2,16,64,128]{3,2,1,0:T(8,128)(2,1)S(1)} %collective-permute-done.3.next_ref), custom_call_target="tpu_custom_call" | custom-call | flops 805306368 | bytes 2097152 | tf_op jit(solution)/shard_map/form_spectrum/pallas_call | solution.py:139
  19.0 0.2 collective-permute-done.next_ref
  19.3 3.0 %form_spectrum.4.refs_0_ = bf16[128,32,128]{2,1,0:T(8,128)(2,1)S(1)} custom-call(bf16[256,512]{1,0:T(8,128)(2,1)S(1)} %filter_rows.1.rows_ref, bf16[256,256]{1,0:T(8,128)(2,1)S(1)} %bitcast.25, f32[2,64,128,128]{3,2,1,0:T(8,128)} %own_ref.7, bf16[2,16,64,128]{3,2,1,0:T(8,128)(2,1)S(1)} %collective-permute-done.next_ref), custom_call_target="tpu_custom_call" | custom-call | flops 805306368 | bytes 2097152 | tf_op jit(solution)/shard_map/form_spectrum/pallas_call | solution.py:139
  22.3 2.6 %collective-permute-done.1.next_ref = bf16[2,16,64,128]{3,2,1,0:T(8,128)(2,1)S(1)} collective-permute-done((bf16[2,16,64,128]{3,2,1,0:T(8,128)(2,1)S(1)}, bf16[2,16,64,128]{3,2,1,0:T(8,128)(2,1)S(1)}, u32[]{:S(2)}, u32[]{:S(2)}) %collective-permute-start.1) | collective-permute-done | bytes 524320 | tf_op jit(solution)/shard_map/ppermute | solution.py:22
  24.9 2.9 %form_spectrum.5.refs_1_ = bf16[128,32,128]{2,1,0:T(8,128)(2,1)S(1)} custom-call(bf16[256,512]{1,0:T(8,128)(2,1)S(1)} %filter_rows.1.rows_ref, bf16[256,256]{1,0:T(8,128)(2,1)S(1)} %bitcast.26, f32[2,64,128,128]{3,2,1,0:T(8,128)} %own_ref.7, bf16[2,16,64,128]{3,2,1,0:T(8,128)(2,1)S(1)} %collective-permute-done.1.next_ref), custom_call_target="tpu_custom_call" | custom-call | flops 805306368 | bytes 2097152 | tf_op jit(solution)/shard_map/form_spectrum/pallas_call | solution.py:139
  27.8 2.7 %collective-permute-done.2.next_ref = bf16[2,16,64,128]{3,2,1,0:T(8,128)(2,1)S(1)} collective-permute-done((bf16[2,16,64,128]{3,2,1,0:T(8,128)(2,1)S(1)}, bf16[2,16,64,128]{3,2,1,0:T(8,128)(2,1)S(1)}, u32[]{:S(2)}, u32[]{:S(2)}) %collective-permute-start.2) | collective-permute-done | bytes 524320 | tf_op jit(solution)/shard_map/ppermute | solution.py:22
  30.5 2.9 %form_spectrum.6.refs_2_ = bf16[128,32,128]{2,1,0:T(8,128)(2,1)S(1)} custom-call(bf16[256,512]{1,0:T(8,128)(2,1)S(1)} %filter_rows.1.rows_ref, bf16[256,256]{1,0:T(8,128)(2,1)S(1)} %bitcast.27, f32[2,64,128,128]{3,2,1,0:T(8,128)} %own_ref.7, bf16[2,16,64,128]{3,2,1,0:T(8,128)(2,1)S(1)} %collective-permute-done.2.next_ref), custom_call_target="tpu_custom_call" | custom-call | flops 805306368 | bytes 2097152 | tf_op jit(solution)/shard_map/form_spectrum/pallas_call | solution.py:139
  33.5 4.1 %select_gates.3 = bf16[8,12,128,128]{3,2,1,0:T(8,128)(2,1)} custom-call(s32[18]{0:T(128)S(1)} %pad_add_fusion.1.index_ref, s32[128,128]{1,0:T(8,128)S(1)} %pad_add_fusion.gates_ref, bf16[128,32,128]{2,1,0:T(8,128)(2,1)S(1)} %form_spectrum.4.refs_0_, bf16[128,32,128]{2,1,0:T(8,128)(2,1)S(1)} %form_spectrum.5.refs_1_, ...), custom_call_target="tpu_custom_call" | custom-call | flops 805306368 | bytes 3145728 | tf_op jit(solution)/shard_map/select_gates/pallas_call | solution.py:204
  37.6 4.8 %all-to-all-start.1 = ((bf16[32,3,128,128]{3,2,1,0:T(8,128)(2,1)}), bf16[32,3,128,128]{3,2,1,0:T(8,128)(2,1)S(1)}, u32[]{:S(2)}, u32[]{:S(2)}) async-start(bf16[32,3,128,128]{3,2,1,0:T(8,128)(2,1)} %bitcast.28), calls=%async_computation.1 | async-start | bytes 6291456 | tf_op jit(solution)/shard_map/all_to_all | solution.py:601
  42.4 1.2 copy-done.3
  43.6 1.2 copy-done.5
  44.9 1.2 copy-done.7
  46.1 1.2 copy-done.9
  47.3 1.8 select_gates.2.refs_0_
  49.1 1.0 copy-done
  50.1 63.1 %all-to-all-done.1 = bf16[32,3,128,128]{3,2,1,0:T(8,128)(2,1)S(1)} async-done(((bf16[32,3,128,128]{3,2,1,0:T(8,128)(2,1)}), bf16[32,3,128,128]{3,2,1,0:T(8,128)(2,1)S(1)}, u32[]{:S(2)}, u32[]{:S(2)}) %all-to-all-start.1) | async-done | bytes 3145760 | tf_op jit(solution)/shard_map/all_to_all | solution.py:601
  113.2 4.6 %all-to-all-start = ((bf16[32,1,128,128]{3,2,1,0:T(8,128)(2,1)}), bf16[32,1,128,128]{3,2,1,0:T(8,128)(2,1)}, u32[]{:S(2)}, u32[]{:S(2)}) async-start(bf16[32,1,128,128]{3,2,1,0:T(8,128)(2,1)} %bitcast.23), calls=%async_computation | async-start | bytes 2097152 | tf_op jit(solution)/shard_map/all_to_all | solution.py:601
  117.9 0.1 copy.31.pivots_ref
  118.0 2.0 %copy.30.weights_ref = bf16[2,512,192]{2,1,0:T(8,128)(2,1)} copy(bf16[2,512,192]{1,2,0:T(8,128)(2,1)} %param.8) | data formatting | bytes 786432 | tf_op args[2]
  120.0 1.2 copy-done.1
  121.2 1.0 copy-done.10
  122.2 1.4 form_beams.2.beams_ref
  123.7 23.5 %factor_slots.2 = (bf16[6,96,384]{2,1,0:T(8,128)(2,1)S(1)}, bf16[6,96,384]{2,1,0:T(8,128)(2,1)S(1)}, bf16[6,96,384]{2,1,0:T(8,128)(2,1)S(1)}, bf16[6,96,384]{2,1,0:T(8,128)(2,1)S(1)}) custom-call(s32[18]{0:T(128)S(1)} %pad_add_fusion.1.index_ref, s32[128,192]{1,0:T(8,128)S(1)} %copy.31.pivots_ref, bf16[4,3,384,128]{3,2,1,0:T(8,128)(2,1)S(1)} %form_beams.2.beams_ref), custom_call_target="tpu_custom_call" | custom-call | flops 339738624 | bytes 1179648 | tf_op jit(solution)/shard_map/factor_slots/pallas_call | solution.py:488
  147.2 1.7 collective-permute-start.7
  148.8 0.2 collective-permute-start.8
  149.0 0.3 collective-permute-start.9
  149.4 1.0 copy-done.11
  150.4 2.1 %form_beams.3.beams_ref = bf16[4,1,384,128]{3,2,1,0:T(8,128)(2,1)S(1)} custom-call(bf16[2,512,192]{2,1,0:T(8,128)(2,1)S(1)} %copy-done.11, bf16[8,4,1,128,128]{4,3,2,1,0:T(8,128)(2,1)} %bitcast.9.arrived_ref, bf16[6,96,384]{2,1,0:T(8,128)(2,1)S(1)} %get-tuple-element.13.refs_0_), custom_call_target="tpu_custom_call" | custom-call | flops 402653184 | bytes 1048576 | tf_op jit(solution)/shard_map/form_beams/pallas_call | solution.py:260
  152.5 19.9 %factor_slots.3 = (bf16[2,96,384]{2,1,0:T(8,128)(2,1)S(1)}, bf16[2,96,384]{2,1,0:T(8,128)(2,1)S(1)}, bf16[2,96,384]{2,1,0:T(8,128)(2,1)S(1)}, bf16[2,96,384]{2,1,0:T(8,128)(2,1)S(1)}) custom-call(s32[18]{0:T(128)S(1)} %pad_add_fusion.1.index_ref, s32[128,192]{1,0:T(8,128)S(1)} %copy.31.pivots_ref, bf16[4,1,384,128]{3,2,1,0:T(8,128)(2,1)S(1)} %form_beams.3.beams_ref), custom_call_target="tpu_custom_call" | custom-call | flops 113246208 | bytes 393216 | tf_op jit(solution)/shard_map/factor_slots/pallas_call | solution.py:488
  172.4 1.5 collective-permute-start.4
  173.8 1.3 collective-permute-start.5
  175.1 5.3 %place_rows.2.refs_4_ = f32[32,96,384]{2,1,0:T(8,128)} custom-call(s32[18]{0:T(128)S(1)} %pad_add_fusion.1.index_ref, bf16[6,96,384]{2,1,0:T(8,128)(2,1)S(1)} %get-tuple-element.13.refs_0_, bf16[6,96,384]{2,1,0:T(8,128)(2,1)S(1)} %collective-permute-done.7.refs_1_, bf16[6,96,384]{2,1,0:T(8,128)(2,1)S(1)} %collective-permute-done.8.refs_2_, ...), custom_call_target="tpu_custom_call" | custom-call | tf_op jit(solution)/shard_map/place_rows/pallas_call | solution.py:543
  180.4 1.3 collective-permute-done.5.refs_2_
  181.8 0.6 collective-permute-done.6.refs_3_
  182.4 2.2 %place_rows.3 = f32[32,96,384]{2,1,0:T(8,128)} custom-call(s32[18]{0:T(128)S(1)} %pad_add_fusion.1.index_ref, bf16[2,96,384]{2,1,0:T(8,128)(2,1)S(1)} %get-tuple-element.14.refs_0_, bf16[2,96,384]{2,1,0:T(8,128)(2,1)S(1)} %collective-permute-done.4.refs_1_, bf16[2,96,384]{2,1,0:T(8,128)(2,1)S(1)} %collective-permute-done.5.refs_2_, ...), custom_call_target="tpu_custom_call", output_to_operand_aliasing={{}: (5, {})} | custom-call | tf_op jit(solution)/shard_map/place_rows/pallas_call | solution.py:543
  (40 shorter events, 0.4 us)
Async XLA Ops:
  2.1 14.0 %collective-permute-start.3 = (bf16[2,16,64,128]{3,2,1,0:T(8,128)(2,1)}, bf16[2,16,64,128]{3,2,1,0:T(8,128)(2,1)S(1)}, u32[]{:S(2)}, u32[]{:S(2)}) collective-permute-start(bf16[2,16,64,128]{3,2,1,0:T(8,128)(2,1)} %rim_rows.7), channel_id=1, source_target_pairs={{1,0},{2,1},{3,2},{5,4},{6,5},{7,6},{9,8},{10,9},{11,10},{13,12},{... | collective-permute-start | bytes 1572872 | tf_op jit(solution)/shard_map/ppermute | solution.py:22
  6.1 13.1 %collective-permute-start = (bf16[2,16,64,128]{3,2,1,0:T(8,128)(2,1)}, bf16[2,16,64,128]{3,2,1,0:T(8,128)(2,1)S(1)}, u32[]{:S(2)}, u32[]{:S(2)}) collective-permute-start(bf16[2,16,64,128]{3,2,1,0:T(8,128)(2,1)} %rim_rows.4), channel_id=1, source_target_pairs={{1,0},{2,1},{3,2},{5,4},{6,5},{7,6},{9,8},{10,9},{11,10},{13,12},{... | collective-permute-start | bytes 1572872 | tf_op jit(solution)/shard_map/ppermute | solution.py:22
  9.3 5.9 %copy-start.15 = (s32[8]{0:T(128)S(1)}, s32[8]{0:T(128)}, u32[]{:S(2)}) copy-start(s32[8]{0:T(128)} %param.10) | copy-start | bytes 100
  9.4 6.2 %copy-start.13 = (s32[128,64]{0,1:T(8,128)S(1)}, s32[128,64]{0,1:T(8,128)}, u32[]{:S(2)}) copy-start(s32[128,64]{0,1:T(8,128)} %param.11) | copy-start | bytes 98308
  9.4 6.4 %copy-start.14 = (f32[2,64]{1,0:T(2,128)S(1)}, f32[2,64]{1,0:T(2,128)}, u32[]{:S(2)}) copy-start(f32[2,64]{1,0:T(2,128)} %param.7) | copy-start | bytes 1540
  9.4 15.5 %collective-permute-start.1 = (bf16[2,16,64,128]{3,2,1,0:T(8,128)(2,1)S(1)}, bf16[2,16,64,128]{3,2,1,0:T(8,128)(2,1)S(1)}, u32[]{:S(2)}, u32[]{:S(2)}) collective-permute-start(bf16[2,16,64,128]{3,2,1,0:T(8,128)(2,1)S(1)} %rim_rows.5), channel_id=1, source_target_pairs={{1,0},{2,1},{3,2},{5,4},{6,5},{7,6},{9,8},{10,9},{11,10},{13,12},{... | collective-permute-start | bytes 1572872 | tf_op jit(solution)/shard_map/ppermute | solution.py:22
  12.7 17.8 %collective-permute-start.2 = (bf16[2,16,64,128]{3,2,1,0:T(8,128)(2,1)S(1)}, bf16[2,16,64,128]{3,2,1,0:T(8,128)(2,1)S(1)}, u32[]{:S(2)}, u32[]{:S(2)}) collective-permute-start(bf16[2,16,64,128]{3,2,1,0:T(8,128)(2,1)S(1)} %rim_rows.6), channel_id=1, source_target_pairs={{1,0},{2,1},{3,2},{5,4},{6,5},{7,6},{9,8},{10,9},{11,10},{13,12},{... | collective-permute-start | bytes 1572872 | tf_op jit(solution)/shard_map/ppermute | solution.py:22
  19.0 14.4 %copy-start.2 = (bf16[128,32,128]{2,1,0:T(8,128)(2,1)}, bf16[128,32,128]{2,1,0:T(8,128)(2,1)S(1)}, u32[]{:S(2)}) copy-start(bf16[128,32,128]{2,1,0:T(8,128)(2,1)S(1)} %form_spectrum.7.refs_3_) | copy-start | bytes 3145732
  22.3 11.1 %copy-start.4 = (bf16[128,32,128]{2,1,0:T(8,128)(2,1)}, bf16[128,32,128]{2,1,0:T(8,128)(2,1)S(1)}, u32[]{:S(2)}) copy-start(bf16[128,32,128]{2,1,0:T(8,128)(2,1)S(1)} %form_spectrum.4.refs_0_) | copy-start | bytes 3145732
  27.8 5.6 %copy-start.6 = (bf16[128,32,128]{2,1,0:T(8,128)(2,1)}, bf16[128,32,128]{2,1,0:T(8,128)(2,1)S(1)}, u32[]{:S(2)}) copy-start(bf16[128,32,128]{2,1,0:T(8,128)(2,1)S(1)} %form_spectrum.5.refs_1_) | copy-start | bytes 3145732
  33.5 4.1 %copy-start.8 = (bf16[128,32,128]{2,1,0:T(8,128)(2,1)}, bf16[128,32,128]{2,1,0:T(8,128)(2,1)S(1)}, u32[]{:S(2)}) copy-start(bf16[128,32,128]{2,1,0:T(8,128)(2,1)S(1)} %form_spectrum.6.refs_2_) | copy-start | bytes 3145732
  37.6 75.6 %all-to-all-start.1 = ((bf16[32,3,128,128]{3,2,1,0:T(8,128)(2,1)}), bf16[32,3,128,128]{3,2,1,0:T(8,128)(2,1)S(1)}, u32[]{:S(2)}, u32[]{:S(2)}) async-start(bf16[32,3,128,128]{3,2,1,0:T(8,128)(2,1)} %bitcast.28), calls=%async_computation.1 | async-start | bytes 6291456 | tf_op jit(solution)/shard_map/all_to_all | solution.py:601
  42.4 1.2 copy-start.3
  43.6 1.2 copy-start.5
  44.8 1.2 copy-start.7
  46.1 1.2 copy-start.9
  47.3 70.6 %copy-start.12 = (s32[128,192]{0,1:T(8,128)S(1)}, s32[128,192]{0,1:T(8,128)}, u32[]{:S(2)}) copy-start(s32[128,192]{0,1:T(8,128)} %param.9) | copy-start | bytes 294916
  49.1 1.0 copy-start
  113.2 36.1 %all-to-all-start = ((bf16[32,1,128,128]{3,2,1,0:T(8,128)(2,1)}), bf16[32,1,128,128]{3,2,1,0:T(8,128)(2,1)}, u32[]{:S(2)}, u32[]{:S(2)}) async-start(bf16[32,1,128,128]{3,2,1,0:T(8,128)(2,1)} %bitcast.23), calls=%async_computation | async-start | bytes 2097152 | tf_op jit(solution)/shard_map/all_to_all | solution.py:601
  120.0 1.2 copy-start.1
  121.2 1.0 copy-start.10
  147.2 28.0 %collective-permute-start.7 = (bf16[6,96,384]{2,1,0:T(8,128)(2,1)S(1)}, bf16[6,96,384]{2,1,0:T(8,128)(2,1)S(1)}, u32[]{:S(2)}, u32[]{:S(2)}) collective-permute-start(bf16[6,96,384]{2,1,0:T(8,128)(2,1)S(1)} %get-tuple-element.18), channel_id=1, source_target_pairs={{0,1},{1,2},{2,3},{3,0},{4,5},{5,6},{6,7},{7,4},{8,9},{9,10},{10,1... | collective-permute-start | bytes 1327112 | tf_op jit(solution)/shard_map/ppermute | solution.py:281
  148.8 26.3 %collective-permute-start.8 = (bf16[6,96,384]{2,1,0:T(8,128)(2,1)S(1)}, bf16[6,96,384]{2,1,0:T(8,128)(2,1)S(1)}, u32[]{:S(2)}, u32[]{:S(2)}) collective-permute-start(bf16[6,96,384]{2,1,0:T(8,128)(2,1)S(1)} %get-tuple-element.19), channel_id=1, source_target_pairs={{0,2},{1,3},{2,0},{3,1},{4,6},{5,7},{6,4},{7,5},{8,10},{9,11},{10,... | collective-permute-start | bytes 1327112 | tf_op jit(solution)/shard_map/ppermute | solution.py:281
  149.0 26.1 %collective-permute-start.9 = (bf16[6,96,384]{2,1,0:T(8,128)(2,1)S(1)}, bf16[6,96,384]{2,1,0:T(8,128)(2,1)S(1)}, u32[]{:S(2)}, u32[]{:S(2)}) collective-permute-start(bf16[6,96,384]{2,1,0:T(8,128)(2,1)S(1)} %get-tuple-element.20), channel_id=1, source_target_pairs={{0,3},{1,0},{2,1},{3,2},{4,7},{5,4},{6,5},{7,6},{8,11},{9,8},{10,9... | collective-permute-start | bytes 1327112 | tf_op jit(solution)/shard_map/ppermute | solution.py:281
  149.4 1.0 copy-start.11
  172.4 8.0 %collective-permute-start.4 = (bf16[2,96,384]{2,1,0:T(8,128)(2,1)S(1)}, bf16[2,96,384]{2,1,0:T(8,128)(2,1)S(1)}, u32[]{:S(2)}, u32[]{:S(2)}) collective-permute-start(bf16[2,96,384]{2,1,0:T(8,128)(2,1)S(1)} %get-tuple-element.15), channel_id=1, source_target_pairs={{0,1},{1,2},{2,3},{3,0},{4,5},{5,6},{6,7},{7,4},{8,9},{9,10},{10,1... | collective-permute-start | bytes 442376 | tf_op jit(solution)/shard_map/ppermute | solution.py:281
  173.8 7.9 %collective-permute-start.5 = (bf16[2,96,384]{2,1,0:T(8,128)(2,1)S(1)}, bf16[2,96,384]{2,1,0:T(8,128)(2,1)S(1)}, u32[]{:S(2)}, u32[]{:S(2)}) collective-permute-start(bf16[2,96,384]{2,1,0:T(8,128)(2,1)S(1)} %get-tuple-element.16), channel_id=1, source_target_pairs={{0,2},{1,3},{2,0},{3,1},{4,6},{5,7},{6,4},{7,5},{8,10},{9,11},{10,... | collective-permute-start | bytes 442376 | tf_op jit(solution)/shard_map/ppermute | solution.py:281
  175.1 7.3 %collective-permute-start.6 = (bf16[2,96,384]{2,1,0:T(8,128)(2,1)S(1)}, bf16[2,96,384]{2,1,0:T(8,128)(2,1)S(1)}, u32[]{:S(2)}, u32[]{:S(2)}) collective-permute-start(bf16[2,96,384]{2,1,0:T(8,128)(2,1)S(1)} %get-tuple-element.17), channel_id=1, source_target_pairs={{0,3},{1,0},{2,1},{3,2},{4,7},{5,4},{6,5},{7,6},{8,11},{9,8},{10,9... | collective-permute-start | bytes 442376 | tf_op jit(solution)/shard_map/ppermute | solution.py:281

commit v3 on v2

--- a/solution.py
+++ b/solution.py
@@ -101,11 +101,16 @@
         if span > gate_rows + rim:
             samples.append(jnp.zeros((span - gate_rows - rim, channels * pulses), BF16))
     samples = jnp.concatenate(samples, axis=0)
-    matched = jnp.dot(rows_ref[...], samples, preferred_element_type=F32).astype(BF16)
-    halves = [matched[:gate_rows], matched[gate_rows:]]
+    matched = jnp.dot(rows_ref[...], samples, preferred_element_type=F32)
+    high, low = split_terms(matched)
+    pieces = [
+        term[part * gate_rows : (part + 1) * gate_rows]
+        for term in (high, low, high)
+        for part in range(2)
+    ]
     stacked = jnp.concatenate(
         [
-            jnp.concatenate([half[:, c * pulses : (c + 1) * pulses] for half in halves], axis=1)
+            jnp.concatenate([piece[:, c * pulses : (c + 1) * pulses] for piece in pieces], axis=1)
             for c in each
         ],
         axis=0,
@@ -166,8 +171,10 @@
     return index_ref[2 + owners + owner]
 
 
-def select_kernel(index_ref, gates_ref, *refs, owners, ranges, first, share_slots, pack):
-    *spectrum_refs, out_ref = refs
+def select_kernel(
+    index_ref, gates_ref, *refs, chunks, owners, ranges, first, share_slots, pack
+):
+    spectrum_refs, out_ref = refs[:chunks], refs[-1]
     bin_count, height, gate_rows = spectrum_refs[0].shape
     some, groups, _, width = out_ref.shape
     half = height // 2
@@ -195,7 +202,9 @@
             out_ref[inner, group] = picked.astype(BF16)
 
 
-def select_gates(spectra, index, gates, first, count, share_slots, owners, ranges, pack):
+def select_gates(
+    spectra, index, gates, first, count, share_slots, owners, ranges, pack, earlier
+):
     rows = sum(spectrum.shape[1] for spectrum in spectra)
     gate_rows = spectra[0].shape[2]
     groups = ranges * count // pack
@@ -204,6 +213,7 @@
     return pl.pallas_call(
         functools.partial(
             select_kernel,
+            chunks=len(spectra),
             owners=owners,
             ranges=ranges,
             first=first,
@@ -213,7 +223,8 @@
         out_shape=jax.ShapeDtypeStruct((owners, groups, rows, width), BF16),
         grid=(owners // some,),
         in_specs=[pl.BlockSpec(memory_space=pltpu.SMEM)]
-        + [pl.BlockSpec(memory_space=pltpu.VMEM)] * (1 + len(spectra)),
+        + [pl.BlockSpec(memory_space=pltpu.VMEM)] * (1 + len(spectra))
+        + [pl.BlockSpec(memory_space=pl.ANY)] * len(earlier),
         out_specs=pl.BlockSpec((some, groups, rows, width), lambda i: (i, 0, 0, 0)),
         compiler_params=PARAMS,
         cost_estimate=pl.CostEstimate(
@@ -222,7 +233,7 @@
             transcendentals=0,
         ),
         name="select_gates",
-    )(index, gates, *spectra)
+    )(index, gates, *spectra, *earlier)
 
 
 def beam_kernel(weights_ref, arrived_ref, *refs):
@@ -350,7 +361,8 @@
             u = t + 1
             inverse = refined_reciprocal(small[t, t])
             cross = small[t, t] * small[u, u] - small[t, u] * small[t, u]
-            second = refined_reciprocal(cross) * small[t, t]
+            guess = pl.reciprocal(cross, approx=True)
+            second = (small[t, t] * guess) * (2.0 - cross * guess)
             scales += [lax.rsqrt(small[t, t]), lax.rsqrt(cross * inverse)]
             factor = small[t, u] * inverse
             for j in range(u + 1, first + 8):
@@ -359,7 +371,8 @@
             for i in range(u + 1, first + 8):
                 one, two = small[t, i] * inverse, small[u, i] * second
                 for j in range(i, first + 8):
-                    small[i, j] = small[i, j] - one * small[t, j] - two * small[u, j]
+                    both = small[u, i] * small[u, j]
+                    small[i, j] = (small[i, j] - one * small[t, j]) - both * second
                 rows[i] = [
                     x - one * y - two * z for x, y, z in zip(rows[i], rows[t], rows[u])
                 ]
@@ -578,7 +591,9 @@
     rim = -(-(tap_count - 1) // 16) * 16
     filters = filter_rows(replica, gate_rows)
     table = doppler_table(pulse_count).transpose(0, 3, 1, 2)
-    table = table.reshape(2 * pulse_count, -1).astype(BF16)
+    table = table.reshape(2 * pulse_count, -1)
+    table_high = lax.reduce_precision(table, exponent_bits=8, mantissa_bits=7)
+    table = jnp.concatenate([table_high, table_high, table - table_high], axis=1).astype(BF16)
     following = [shifted(rim_rows(raw_echo, rim, c, chunks), "rng", -1) for c in range(chunks)]
     spectra = [
         form_spectrum(filters, table, raw_echo, following[c], c, chunks) for c in range(chunks)
@@ -592,10 +607,14 @@
     count_rows = float(train_local * ranges)
 
     parts = slot_parts(share_slots, pack)
-    outgoing = [
-        select_gates(spectra, index, gates, first, count, share_slots, owners, ranges, pack)
-        for first, count in parts
-    ]
+    outgoing = []
+    for first, count in parts:
+        earlier = [beam_weights] if first > 0 else []
+        outgoing.append(
+            select_gates(
+                spectra, index, gates, first, count, share_slots, owners, ranges, pack, earlier
+            )
+        )
     axes = ("dop", "rng")
     sent = [
         lax.all_to_all(

time: 186 us -> 188 us (1.011)
  waiting for transfers between devices: 70.6 us -> 62 us
  other arithmetic: 0.96 us -> 4.81 us
  starting transfers between devices: 22.2 us -> 25.2 us
  local copies, waits for them, and re-layouts: 11.5 us -> 13.6 us
    ppermute x4, waiting for transfers between devices: 5.48 us -> 0.01 us  [shifted(): return lax.ppermute(array, axis, pairs)]
    all_to_all x2, waiting for transfers between devices: 63.1 us -> 60 us  [local(): lax.all_to_all(array.reshape(owners * ranges, -1, *array.shape[2:]), axes...]
    all_to_all x2, starting transfers between devices: 9.4 us -> 12.4 us  [local(): lax.all_to_all(array.reshape(owners * ranges, -1, *array.shape[2:]), axes...]
    pallas_call x4, Pallas kernels: 11.8 us -> 14.4 us  [form_spectrum(): pl.pallas_call(spectrum_kernel, out_shape=jax.ShapeDtypeStruct((bins, hei...]
    unnamed x36 -> x37, local copies, waits for them, and re-layouts: 11.4 us -> 12.5 us
  transfers between devices with their start and end apart: 12 -> 12, of which waited for: 6 -> 3; matrix products, arithmetic and copies ran while one was open for 2% -> 4% of each run, Pallas kernels for 37% -> 37%
where the time goes in v3:
time: 188 us; the launch traced here: 186 us
  Pallas kernels  80.4 us (43%)
  waiting for transfers between devices  62 us (33%)
  starting transfers between devices  25.2 us (13%)
  local copies, waits for them, and re-layouts  13.6 us (7%)
  other arithmetic  4.81 us (3%)
    all_to_all x2, waiting for transfers between devices, local(): lax.all_to_all(array.reshape(owners * ranges, -1, *array.shape[2:]), axes...  60 us
    pallas_call x2, Pallas kernels, factor_slots(): pl.pallas_call(functools.partial(factor_kernel, first=first, share_slots=...  43.7 us
    pallas_call x4, Pallas kernels, form_spectrum(): pl.pallas_call(spectrum_kernel, out_shape=jax.ShapeDtypeStruct((bins, hei...  14.4 us
    unnamed x37, local copies, waits for them, and re-layouts  12.5 us
    all_to_all x2, starting transfers between devices, local(): lax.all_to_all(array.reshape(owners * ranges, -1, *array.shape[2:]), axes...  12.4 us
    ppermute x4, starting transfers between devices, shifted(): return lax.ppermute(array, axis, pairs)  7.86 us
    pallas_call x2, Pallas kernels, place_rows(): pl.pallas_call(functools.partial(place_kernel, first=first, share_slots=s...  7.5 us
    pallas_call x2, Pallas kernels, select_gates(): pl.pallas_call(functools.partial(select_kernel, chunks=len(spectra), owne...  5.94 us
  transfers between devices with their start and end apart: 12, of which 3 were waited for; matrix products, arithmetic and copies ran while one was open for 4% of the time, Pallas kernels for 37%

profile of v3, /device:TPU:1, one launch (start us, length us, event | category | flops | bytes accessed | tf_op | source)
XLA Modules:
  0.0 186.4 jit_solution(16840232586973227357)
XLA Ops:
  0.0 1.3 rim_rows.7
  1.3 2.0 %collective-permute-start.3 = (bf16[2,16,64,128]{3,2,1,0:T(8,128)(2,1)S(1)}, bf16[2,16,64,128]{3,2,1,0:T(8,128)(2,1)}, u32[]{:S(2)}, u32[]{:S(2)}) collective-permute-start(bf16[2,16,64,128]{3,2,1,0:T(8,128)(2,1)S(1)} %rim_rows.7), channel_id=1, source_target_pairs={{1,0},{2,1},{3,2},{5,4},{6,5},{7,6},{9,8},{10,9},{11,10},{13,12},{... | collective-permute-start | bytes 1572872 | tf_op jit(solution)/shard_map/ppermute | solution.py:22
  3.3 1.3 rim_rows.4
  4.5 1.9 %collective-permute-start = (bf16[2,16,64,128]{3,2,1,0:T(8,128)(2,1)S(1)}, bf16[2,16,64,128]{3,2,1,0:T(8,128)(2,1)}, u32[]{:S(2)}, u32[]{:S(2)}) collective-permute-start(bf16[2,16,64,128]{3,2,1,0:T(8,128)(2,1)S(1)} %rim_rows.4), channel_id=1, source_target_pairs={{1,0},{2,1},{3,2},{5,4},{6,5},{7,6},{9,8},{10,9},{11,10},{13,12},{... | collective-permute-start | bytes 1572872 | tf_op jit(solution)/shard_map/ppermute | solution.py:22
  6.5 1.3 rim_rows.5
  7.8 2.1 %collective-permute-start.1 = (bf16[2,16,64,128]{3,2,1,0:T(8,128)(2,1)S(1)}, bf16[2,16,64,128]{3,2,1,0:T(8,128)(2,1)S(1)}, u32[]{:S(2)}, u32[]{:S(2)}) collective-permute-start(bf16[2,16,64,128]{3,2,1,0:T(8,128)(2,1)S(1)} %rim_rows.5), channel_id=1, source_target_pairs={{1,0},{2,1},{3,2},{5,4},{6,5},{7,6},{9,8},{10,9},{11,10},{13,12},{... | collective-permute-start | bytes 1572872 | tf_op jit(solution)/shard_map/ppermute | solution.py:22
  9.9 1.3 rim_rows.6
  11.2 1.9 %collective-permute-start.2 = (bf16[2,16,64,128]{3,2,1,0:T(8,128)(2,1)S(1)}, bf16[2,16,64,128]{3,2,1,0:T(8,128)(2,1)S(1)}, u32[]{:S(2)}, u32[]{:S(2)}) collective-permute-start(bf16[2,16,64,128]{3,2,1,0:T(8,128)(2,1)S(1)} %rim_rows.6), channel_id=1, source_target_pairs={{1,0},{2,1},{3,2},{5,4},{6,5},{7,6},{9,8},{10,9},{11,10},{13,12},{... | collective-permute-start | bytes 1572872 | tf_op jit(solution)/shard_map/ppermute | solution.py:22
  13.1 0.3 fusion.8
  13.4 0.3 sine_multiply_fusion
  13.7 0.7 add_select_fusion.1
  14.5 0.7 maximum_bitcast_fusion
  15.2 1.1 copy.28
  16.3 0.7 reduce-precision_convert_fusion
  17.2 1.0 pad_add_fusion.gates_ref
  18.3 0.9 pad_maximum_fusion.table_ref
  19.3 3.4 %form_spectrum.7.refs_3_ = bf16[128,32,128]{2,1,0:T(8,128)(2,1)S(1)} custom-call(bf16[256,512]{1,0:T(8,128)(2,1)S(1)} %filter_rows.1.rows_ref, bf16[256,768]{1,0:T(8,128)(2,1)S(1)} %pad_maximum_fusion.table_ref, f32[2,64,128,128]{3,2,1,0:T(8,128)} %own_ref.7, bf16[2,16,64,128]{3,2,1,0:T(8,128)(2,1)} %collective-permute-done.3.next_ref), custom_call_target="tpu_custom_call" | custom-call | flops 1342177280 | bytes 2097152 | tf_op jit(solution)/shard_map/form_spectrum/pallas_call | solution.py:144
  22.7 3.7 %form_spectrum.4.refs_0_ = bf16[128,32,128]{2,1,0:T(8,128)(2,1)S(1)} custom-call(bf16[256,512]{1,0:T(8,128)(2,1)S(1)} %filter_rows.1.rows_ref, bf16[256,768]{1,0:T(8,128)(2,1)S(1)} %pad_maximum_fusion.table_ref, f32[2,64,128,128]{3,2,1,0:T(8,128)} %own_ref.7, bf16[2,16,64,128]{3,2,1,0:T(8,128)(2,1)} %collective-permute-done.next_ref), custom_call_target="tpu_custom_call" | custom-call | flops 1342177280 | bytes 2097152 | tf_op jit(solution)/shard_map/form_spectrum/pallas_call | solution.py:144
  26.4 3.7 %form_spectrum.5.refs_1_ = bf16[128,32,128]{2,1,0:T(8,128)(2,1)S(1)} custom-call(bf16[256,512]{1,0:T(8,128)(2,1)S(1)} %filter_rows.1.rows_ref, bf16[256,768]{1,0:T(8,128)(2,1)S(1)} %pad_maximum_fusion.table_ref, f32[2,64,128,128]{3,2,1,0:T(8,128)} %own_ref.7, bf16[2,16,64,128]{3,2,1,0:T(8,128)(2,1)S(1)} %collective-permute-done.1.next_ref), custom_call_target="tpu_custom_call" | custom-call | flops 1342177280 | bytes 2097152 | tf_op jit(solution)/shard_map/form_spectrum/pallas_call | solution.py:144
  30.1 3.7 %form_spectrum.6.refs_2_ = bf16[128,32,128]{2,1,0:T(8,128)(2,1)S(1)} custom-call(bf16[256,512]{1,0:T(8,128)(2,1)S(1)} %filter_rows.1.rows_ref, bf16[256,768]{1,0:T(8,128)(2,1)S(1)} %pad_maximum_fusion.table_ref, f32[2,64,128,128]{3,2,1,0:T(8,128)} %own_ref.7, bf16[2,16,64,128]{3,2,1,0:T(8,128)(2,1)S(1)} %collective-permute-done.2.next_ref), custom_call_target="tpu_custom_call" | custom-call | flops 1342177280 | bytes 2097152 | tf_op jit(solution)/shard_map/form_spectrum/pallas_call | solution.py:144
  33.8 4.1 %select_gates.3 = bf16[8,12,128,128]{3,2,1,0:T(8,128)(2,1)} custom-call(s32[18]{0:T(128)S(1)} %pad_add_fusion.1.index_ref, s32[128,128]{1,0:T(8,128)S(1)} %pad_add_fusion.gates_ref, bf16[128,32,128]{2,1,0:T(8,128)(2,1)S(1)} %form_spectrum.4.refs_0_, bf16[128,32,128]{2,1,0:T(8,128)(2,1)S(1)} %form_spectrum.5.refs_1_, ...), custom_call_target="tpu_custom_call" | custom-call | flops 805306368 | bytes 3145728 | tf_op jit(solution)/shard_map/select_gates/pallas_call | solution.py:213
  38.0 7.8 %all-to-all-start.1 = ((bf16[32,3,128,128]{3,2,1,0:T(8,128)(2,1)}), bf16[32,3,128,128]{3,2,1,0:T(8,128)(2,1)S(1)}, u32[]{:S(2)}, u32[]{:S(2)}) async-start(bf16[32,3,128,128]{3,2,1,0:T(8,128)(2,1)} %bitcast.24), calls=%async_computation.1 | async-start | bytes 6291456 | tf_op jit(solution)/shard_map/all_to_all | solution.py:620
  45.8 2.1 %copy.33.refs_4_.weights_ref = bf16[2,512,192]{2,1,0:T(8,128)(2,1)} copy(bf16[2,512,192]{1,2,0:T(8,128)(2,1)} %param.8) | data formatting | bytes 786432 | tf_op args[2]
  47.9 1.2 copy-done.3
  49.1 1.2 copy-done.5
  50.3 1.2 copy-done.7
  51.5 1.2 copy-done.9
  52.8 1.0 copy-done.10
  53.8 1.8 select_gates.2.refs_0_
  55.6 1.0 copy-done
  56.6 60.0 %all-to-all-done.1 = bf16[32,3,128,128]{3,2,1,0:T(8,128)(2,1)S(1)} async-done(((bf16[32,3,128,128]{3,2,1,0:T(8,128)(2,1)}), bf16[32,3,128,128]{3,2,1,0:T(8,128)(2,1)S(1)}, u32[]{:S(2)}, u32[]{:S(2)}) %all-to-all-start.1) | async-done | bytes 3145760 | tf_op jit(solution)/shard_map/all_to_all | solution.py:620
  116.6 4.6 %all-to-all-start = ((bf16[32,1,128,128]{3,2,1,0:T(8,128)(2,1)}), bf16[32,1,128,128]{3,2,1,0:T(8,128)(2,1)}, u32[]{:S(2)}, u32[]{:S(2)}) async-start(bf16[32,1,128,128]{3,2,1,0:T(8,128)(2,1)} %bitcast.23), calls=%async_computation | async-start | bytes 2097152 | tf_op jit(solution)/shard_map/all_to_all | solution.py:620
  121.4 1.2 copy-done.1
  122.6 1.0 copy-done.11
  123.6 1.4 form_beams.2.beams_ref
  125.1 23.5 %factor_slots.2 = (bf16[6,96,384]{2,1,0:T(8,128)(2,1)S(1)}, bf16[6,96,384]{2,1,0:T(8,128)(2,1)S(1)}, bf16[6,96,384]{2,1,0:T(8,128)(2,1)S(1)}, bf16[6,96,384]{2,1,0:T(8,128)(2,1)S(1)}) custom-call(s32[18]{0:T(128)S(1)} %pad_add_fusion.1.index_ref, s32[128,192]{1,0:T(8,128)S(1)} %copy.34.pivots_ref, bf16[4,3,384,128]{3,2,1,0:T(8,128)(2,1)S(1)} %form_beams.2.beams_ref), custom_call_target="tpu_custom_call" | custom-call | flops 339738624 | bytes 1179648 | tf_op jit(solution)/shard_map/factor_slots/pallas_call | solution.py:501
  148.6 1.7 collective-permute-start.7
  150.3 0.2 collective-permute-start.8
  150.5 0.3 collective-permute-start.9
  150.8 1.0 copy-done.12
  151.9 2.1 %form_beams.3.beams_ref = bf16[4,1,384,128]{3,2,1,0:T(8,128)(2,1)S(1)} custom-call(bf16[2,512,192]{2,1,0:T(8,128)(2,1)S(1)} %copy-done.12, bf16[8,4,1,128,128]{4,3,2,1,0:T(8,128)(2,1)} %bitcast.9.arrived_ref, bf16[6,96,384]{2,1,0:T(8,128)(2,1)S(1)} %get-tuple-element.13.refs_0_), custom_call_target="tpu_custom_call" | custom-call | flops 402653184 | bytes 1048576 | tf_op jit(solution)/shard_map/form_beams/pallas_call | solution.py:271
  154.0 20.2 %factor_slots.3 = (bf16[2,96,384]{2,1,0:T(8,128)(2,1)S(1)}, bf16[2,96,384]{2,1,0:T(8,128)(2,1)S(1)}, bf16[2,96,384]{2,1,0:T(8,128)(2,1)S(1)}, bf16[2,96,384]{2,1,0:T(8,128)(2,1)S(1)}) custom-call(s32[18]{0:T(128)S(1)} %pad_add_fusion.1.index_ref, s32[128,192]{1,0:T(8,128)S(1)} %copy.34.pivots_ref, bf16[4,1,384,128]{3,2,1,0:T(8,128)(2,1)S(1)} %form_beams.3.beams_ref), custom_call_target="tpu_custom_call" | custom-call | flops 113246208 | bytes 393216 | tf_op jit(solution)/shard_map/factor_slots/pallas_call | solution.py:501
  174.2 1.5 collective-permute-start.4
  175.7 1.3 collective-permute-start.5
  176.9 5.3 %place_rows.2.refs_4_ = f32[32,96,384]{2,1,0:T(8,128)} custom-call(s32[18]{0:T(128)S(1)} %pad_add_fusion.1.index_ref, bf16[6,96,384]{2,1,0:T(8,128)(2,1)S(1)} %get-tuple-element.13.refs_0_, bf16[6,96,384]{2,1,0:T(8,128)(2,1)S(1)} %collective-permute-done.7.refs_1_, bf16[6,96,384]{2,1,0:T(8,128)(2,1)S(1)} %collective-permute-done.8.refs_2_, ...), custom_call_target="tpu_custom_call" | custom-call | tf_op jit(solution)/shard_map/place_rows/pallas_call | solution.py:556
  182.2 1.3 collective-permute-done.5.refs_2_
  183.6 0.6 collective-permute-done.6.refs_3_
  184.2 2.2 %place_rows.3 = f32[32,96,384]{2,1,0:T(8,128)} custom-call(s32[18]{0:T(128)S(1)} %pad_add_fusion.1.index_ref, bf16[2,96,384]{2,1,0:T(8,128)(2,1)S(1)} %get-tuple-element.14.refs_0_, bf16[2,96,384]{2,1,0:T(8,128)(2,1)S(1)} %collective-permute-done.4.refs_1_, bf16[2,96,384]{2,1,0:T(8,128)(2,1)S(1)} %collective-permute-done.5.refs_2_, ...), custom_call_target="tpu_custom_call", output_to_operand_aliasing={{}: (5, {})} | custom-call | tf_op jit(solution)/shard_map/place_rows/pallas_call | solution.py:556
  (43 shorter events, 0.7 us)
Async XLA Ops:
  1.3 18.0 %collective-permute-start.3 = (bf16[2,16,64,128]{3,2,1,0:T(8,128)(2,1)S(1)}, bf16[2,16,64,128]{3,2,1,0:T(8,128)(2,1)}, u32[]{:S(2)}, u32[]{:S(2)}) collective-permute-start(bf16[2,16,64,128]{3,2,1,0:T(8,128)(2,1)S(1)} %rim_rows.7), channel_id=1, source_target_pairs={{1,0},{2,1},{3,2},{5,4},{6,5},{7,6},{9,8},{10,9},{11,10},{13,12},{... | collective-permute-start | bytes 1572872 | tf_op jit(solution)/shard_map/ppermute | solution.py:22
  4.5 18.1 %collective-permute-start = (bf16[2,16,64,128]{3,2,1,0:T(8,128)(2,1)S(1)}, bf16[2,16,64,128]{3,2,1,0:T(8,128)(2,1)}, u32[]{:S(2)}, u32[]{:S(2)}) collective-permute-start(bf16[2,16,64,128]{3,2,1,0:T(8,128)(2,1)S(1)} %rim_rows.4), channel_id=1, source_target_pairs={{1,0},{2,1},{3,2},{5,4},{6,5},{7,6},{9,8},{10,9},{11,10},{13,12},{... | collective-permute-start | bytes 1572872 | tf_op jit(solution)/shard_map/ppermute | solution.py:22
  7.8 5.9 %copy-start.14 = (s32[128,64]{0,1:T(8,128)S(1)}, s32[128,64]{0,1:T(8,128)}, u32[]{:S(2)}) copy-start(s32[128,64]{0,1:T(8,128)} %param.11) | copy-start | bytes 98308
  7.8 9.2 %copy-start.16 = (s32[8]{0:T(128)S(1)}, s32[8]{0:T(128)}, u32[]{:S(2)}) copy-start(s32[8]{0:T(128)} %param.10) | copy-start | bytes 100
  7.8 10.4 %copy-start.15 = (f32[2,64]{1,0:T(2,128)S(1)}, f32[2,64]{1,0:T(2,128)}, u32[]{:S(2)}) copy-start(f32[2,64]{1,0:T(2,128)} %param.7) | copy-start | bytes 1540
  7.8 18.6 %collective-permute-start.1 = (bf16[2,16,64,128]{3,2,1,0:T(8,128)(2,1)S(1)}, bf16[2,16,64,128]{3,2,1,0:T(8,128)(2,1)S(1)}, u32[]{:S(2)}, u32[]{:S(2)}) collective-permute-start(bf16[2,16,64,128]{3,2,1,0:T(8,128)(2,1)S(1)} %rim_rows.5), channel_id=1, source_target_pairs={{1,0},{2,1},{3,2},{5,4},{6,5},{7,6},{9,8},{10,9},{11,10},{13,12},{... | collective-permute-start | bytes 1572872 | tf_op jit(solution)/shard_map/ppermute | solution.py:22
  11.2 18.9 %collective-permute-start.2 = (bf16[2,16,64,128]{3,2,1,0:T(8,128)(2,1)S(1)}, bf16[2,16,64,128]{3,2,1,0:T(8,128)(2,1)S(1)}, u32[]{:S(2)}, u32[]{:S(2)}) collective-permute-start(bf16[2,16,64,128]{3,2,1,0:T(8,128)(2,1)S(1)} %rim_rows.6), channel_id=1, source_target_pairs={{1,0},{2,1},{3,2},{5,4},{6,5},{7,6},{9,8},{10,9},{11,10},{13,12},{... | collective-permute-start | bytes 1572872 | tf_op jit(solution)/shard_map/ppermute | solution.py:22
  22.7 11.1 %copy-start.2 = (bf16[128,32,128]{2,1,0:T(8,128)(2,1)}, bf16[128,32,128]{2,1,0:T(8,128)(2,1)S(1)}, u32[]{:S(2)}) copy-start(bf16[128,32,128]{2,1,0:T(8,128)(2,1)S(1)} %form_spectrum.7.refs_3_) | copy-start | bytes 3145732
  26.4 7.4 %copy-start.4 = (bf16[128,32,128]{2,1,0:T(8,128)(2,1)}, bf16[128,32,128]{2,1,0:T(8,128)(2,1)S(1)}, u32[]{:S(2)}) copy-start(bf16[128,32,128]{2,1,0:T(8,128)(2,1)S(1)} %form_spectrum.4.refs_0_) | copy-start | bytes 3145732
  30.1 3.7 %copy-start.6 = (bf16[128,32,128]{2,1,0:T(8,128)(2,1)}, bf16[128,32,128]{2,1,0:T(8,128)(2,1)S(1)}, u32[]{:S(2)}) copy-start(bf16[128,32,128]{2,1,0:T(8,128)(2,1)S(1)} %form_spectrum.5.refs_1_) | copy-start | bytes 3145732
  33.8 4.1 %copy-start.8 = (bf16[128,32,128]{2,1,0:T(8,128)(2,1)}, bf16[128,32,128]{2,1,0:T(8,128)(2,1)S(1)}, u32[]{:S(2)}) copy-start(bf16[128,32,128]{2,1,0:T(8,128)(2,1)S(1)} %form_spectrum.6.refs_2_) | copy-start | bytes 3145732
  38.0 78.7 %all-to-all-start.1 = ((bf16[32,3,128,128]{3,2,1,0:T(8,128)(2,1)}), bf16[32,3,128,128]{3,2,1,0:T(8,128)(2,1)S(1)}, u32[]{:S(2)}, u32[]{:S(2)}) async-start(bf16[32,3,128,128]{3,2,1,0:T(8,128)(2,1)} %bitcast.24), calls=%async_computation.1 | async-start | bytes 6291456 | tf_op jit(solution)/shard_map/all_to_all | solution.py:620
  45.8 75.5 %copy-start.13 = (s32[128,192]{0,1:T(8,128)S(1)}, s32[128,192]{0,1:T(8,128)}, u32[]{:S(2)}) copy-start(s32[128,192]{0,1:T(8,128)} %param.9) | copy-start | bytes 294916
  47.9 1.2 copy-start.3
  49.1 1.2 copy-start.5
  50.3 1.2 copy-start.7
  51.5 1.2 copy-start.9
  52.8 1.0 copy-start.10
  55.6 1.0 copy-start
  116.6 34.2 %all-to-all-start = ((bf16[32,1,128,128]{3,2,1,0:T(8,128)(2,1)}), bf16[32,1,128,128]{3,2,1,0:T(8,128)(2,1)}, u32[]{:S(2)}, u32[]{:S(2)}) async-start(bf16[32,1,128,128]{3,2,1,0:T(8,128)(2,1)} %bitcast.23), calls=%async_computation | async-start | bytes 2097152 | tf_op jit(solution)/shard_map/all_to_all | solution.py:620
  121.4 1.2 copy-start.1
  122.6 1.0 copy-start.11
  148.6 28.3 %collective-permute-start.7 = (bf16[6,96,384]{2,1,0:T(8,128)(2,1)S(1)}, bf16[6,96,384]{2,1,0:T(8,128)(2,1)S(1)}, u32[]{:S(2)}, u32[]{:S(2)}) collective-permute-start(bf16[6,96,384]{2,1,0:T(8,128)(2,1)S(1)} %get-tuple-element.18), channel_id=1, source_target_pairs={{0,1},{1,2},{2,3},{3,0},{4,5},{5,6},{6,7},{7,4},{8,9},{9,10},{10,1... | collective-permute-start | bytes 1327112 | tf_op jit(solution)/shard_map/ppermute | solution.py:292
  150.3 26.6 %collective-permute-start.8 = (bf16[6,96,384]{2,1,0:T(8,128)(2,1)S(1)}, bf16[6,96,384]{2,1,0:T(8,128)(2,1)S(1)}, u32[]{:S(2)}, u32[]{:S(2)}) collective-permute-start(bf16[6,96,384]{2,1,0:T(8,128)(2,1)S(1)} %get-tuple-element.19), channel_id=1, source_target_pairs={{0,2},{1,3},{2,0},{3,1},{4,6},{5,7},{6,4},{7,5},{8,10},{9,11},{10,... | collective-permute-start | bytes 1327112 | tf_op jit(solution)/shard_map/ppermute | solution.py:292
  150.5 26.4 %collective-permute-start.9 = (bf16[6,96,384]{2,1,0:T(8,128)(2,1)S(1)}, bf16[6,96,384]{2,1,0:T(8,128)(2,1)S(1)}, u32[]{:S(2)}, u32[]{:S(2)}) collective-permute-start(bf16[6,96,384]{2,1,0:T(8,128)(2,1)S(1)} %get-tuple-element.20), channel_id=1, source_target_pairs={{0,3},{1,0},{2,1},{3,2},{4,7},{5,4},{6,5},{7,6},{8,11},{9,8},{10,9... | collective-permute-start | bytes 1327112 | tf_op jit(solution)/shard_map/ppermute | solution.py:292
  150.8 1.0 copy-start.12
  174.2 8.0 %collective-permute-start.4 = (bf16[2,96,384]{2,1,0:T(8,128)(2,1)S(1)}, bf16[2,96,384]{2,1,0:T(8,128)(2,1)S(1)}, u32[]{:S(2)}, u32[]{:S(2)}) collective-permute-start(bf16[2,96,384]{2,1,0:T(8,128)(2,1)S(1)} %get-tuple-element.15), channel_id=1, source_target_pairs={{0,1},{1,2},{2,3},{3,0},{4,5},{5,6},{6,7},{7,4},{8,9},{9,10},{10,1... | collective-permute-start | bytes 442376 | tf_op jit(solution)/shard_map/ppermute | solution.py:292
  175.7 7.9 %collective-permute-start.5 = (bf16[2,96,384]{2,1,0:T(8,128)(2,1)S(1)}, bf16[2,96,384]{2,1,0:T(8,128)(2,1)S(1)}, u32[]{:S(2)}, u32[]{:S(2)}) collective-permute-start(bf16[2,96,384]{2,1,0:T(8,128)(2,1)S(1)} %get-tuple-element.16), channel_id=1, source_target_pairs={{0,2},{1,3},{2,0},{3,1},{4,6},{5,7},{6,4},{7,5},{8,10},{9,11},{10,... | collective-permute-start | bytes 442376 | tf_op jit(solution)/shard_map/ppermute | solution.py:292
  176.9 7.3 %collective-permute-start.6 = (bf16[2,96,384]{2,1,0:T(8,128)(2,1)S(1)}, bf16[2,96,384]{2,1,0:T(8,128)(2,1)S(1)}, u32[]{:S(2)}, u32[]{:S(2)}) collective-permute-start(bf16[2,96,384]{2,1,0:T(8,128)(2,1)S(1)} %get-tuple-element.17), channel_id=1, source_target_pairs={{0,3},{1,0},{2,1},{3,2},{4,7},{5,4},{6,5},{7,6},{8,11},{9,8},{10,9... | collective-permute-start | bytes 442376 | tf_op jit(solution)/shard_map/ppermute | solution.py:292

commit v4 on v3

--- a/solution.py
+++ b/solution.py
@@ -3,6 +3,7 @@
 
 import jax
 import jax.numpy as jnp
+import numpy as np
 from jax import lax
 from jax.experimental import pallas as pl
 from jax.experimental.pallas import tpu as pltpu
@@ -22,18 +23,16 @@
     return lax.ppermute(array, axis, pairs)
 
 
-def complex_block(real_part, imag_part):
-    upper_row = jnp.stack([real_part, imag_part])
-    lower_row = jnp.stack([-imag_part, real_part])
-    return jnp.stack([upper_row, lower_row])
-
-
 def doppler_table(pulse_count):
-    pulse_index = jnp.arange(pulse_count, dtype=jnp.int32)
+    pulse_index = np.arange(pulse_count)
     phase_index = pulse_index[:, None] * pulse_index[None, :] % pulse_count
-    angle_table = phase_index.astype(jnp.float32) * (2.0 * math.pi / pulse_count)
-    norm_scale = 1.0 / math.sqrt(pulse_count)
-    return complex_block(jnp.cos(angle_table) * norm_scale, jnp.sin(angle_table) * norm_scale)
+    angle_table = phase_index.astype(np.float32) * np.float32(2.0 * math.pi / pulse_count)
+    norm_scale = np.float32(1.0 / math.sqrt(pulse_count))
+    real_part, imag_part = np.cos(angle_table) * norm_scale, np.sin(angle_table) * norm_scale
+    table = np.block([[real_part.T, imag_part.T], [-imag_part.T, real_part.T]])
+    high = table.astype(BF16)
+    low = (table - high.astype(np.float32)).astype(BF16)
+    return jnp.asarray(np.concatenate([high, high, low], axis=1))
 
 
 def filter_kernel(replica_ref, out_ref):
@@ -238,42 +237,45 @@
 
 def beam_kernel(weights_ref, arrived_ref, *refs):
     out_ref = refs[-1]
-    sources, ranges, groups, rows, width = arrived_ref.shape
+    sources, _, groups, rows, width = arrived_ref.shape
     dof = weights_ref.shape[2]
     half = rows // 2
-    for block in range(ranges):
-        packed = jnp.concatenate(
-            [
-                arrived_ref[:, block, g, s * half : (s + 1) * half].reshape(sources * half, width)
-                for s in range(2)
-                for g in range(groups)
-            ],
-            axis=1,
+    packed = jnp.concatenate(
+        [
+            arrived_ref[:, 0, g, s * half : (s + 1) * half].reshape(sources * half, width)
+            for s in range(2)
+            for g in range(groups)
+        ],
+        axis=1,
+    )
+    by_real, by_imag = [
+        lax.dot_general(
+            weights_ref[part], packed, (((0,), (0,)), ((), ())), preferred_element_type=F32
         )
-        by_real, by_imag = [
-            lax.dot_general(
-                weights_ref[part], packed, (((0,), (0,)), ((), ())), preferred_element_type=F32
-            )
-            for part in range(2)
-        ]
-        middle = groups * width
-        real_part = by_real[:, :middle] + by_imag[:, middle:]
-        imag_part = by_real[:, middle:] - by_imag[:, :middle]
-        for g in range(groups):
-            span = slice(g * width, (g + 1) * width)
-            out_ref[block, g, :dof] = real_part[:, span].astype(BF16)
-            out_ref[block, g, dof:] = imag_part[:, span].astype(BF16)
+        for part in range(2)
+    ]
+    middle = groups * width
+    real_part = by_real[:, :middle] + by_imag[:, middle:]
+    imag_part = by_real[:, middle:] - by_imag[:, :middle]
+    for g in range(groups):
+        span = slice(g * width, (g + 1) * width)
+        out_ref[0, g, :dof] = real_part[:, span].astype(BF16)
+        out_ref[0, g, dof:] = imag_part[:, span].astype(BF16)
 
 
 def form_beams(arrived, weights, earlier):
-    _, ranges, groups, _, width = arrived.shape
+    sources, ranges, groups, rows, width = arrived.shape
     shape = (ranges, groups, 2 * weights.shape[2], width)
     return pl.pallas_call(
         beam_kernel,
         out_shape=jax.ShapeDtypeStruct(shape, BF16),
-        in_specs=[pl.BlockSpec(memory_space=pltpu.VMEM)] * 2
+        grid=(ranges,),
+        in_specs=[
+            pl.BlockSpec(weights.shape, lambda i: (0, 0, 0)),
+            pl.BlockSpec((sources, 1, groups, rows, width), lambda i: (0, i, 0, 0, 0)),
+        ]
         + [pl.BlockSpec(memory_space=pl.ANY)] * len(earlier),
-        out_specs=pl.BlockSpec(memory_space=pltpu.VMEM),
+        out_specs=pl.BlockSpec((1,) + shape[1:], lambda i: (i, 0, 0, 0)),
         compiler_params=PARAMS,
         cost_estimate=pl.CostEstimate(
             flops=4 * arrived.size * weights.shape[2],
@@ -338,7 +340,8 @@
 
 
 def lane_spread(piece, lane):
-    return jnp.broadcast_to(piece[:, lane : lane + 1], piece.shape)
+    lanes = jnp.full(piece.shape, lane, jnp.int32)
+    return jnp.take_along_axis(piece, lanes, axis=1, mode="promise_in_bounds")
 
 
 def refined_reciprocal(value):
@@ -590,10 +593,7 @@
     chunk_rows = ch_local // chunks
     rim = -(-(tap_count - 1) // 16) * 16
     filters = filter_rows(replica, gate_rows)
-    table = doppler_table(pulse_count).transpose(0, 3, 1, 2)
-    table = table.reshape(2 * pulse_count, -1)
-    table_high = lax.reduce_precision(table, exponent_bits=8, mantissa_bits=7)
-    table = jnp.concatenate([table_high, table_high, table - table_high], axis=1).astype(BF16)
+    table = doppler_table(pulse_count)
     following = [shifted(rim_rows(raw_echo, rim, c, chunks), "rng", -1) for c in range(chunks)]
     spectra = [
         form_spectrum(filters, table, raw_echo, following[c], c, chunks) for c in range(chunks)

time: 188 us -> 185 us (0.984)
  waiting for transfers between devices: 62 us -> 67.7 us
  other arithmetic: 4.81 us -> 0.38 us
  starting transfers between devices: 25.2 us -> 22.2 us
    ppermute x4, waiting for transfers between devices: 0.01 us -> 5.66 us  [shifted(): return lax.ppermute(array, axis, pairs)]
    all_to_all x2, starting transfers between devices: 12.4 us -> 9.4 us  [local(): lax.all_to_all(array.reshape(owners * ranges, -1, *array.shape[2:]), axes...]
    unnamed x37 -> x39, local copies, waits for them, and re-layouts: 12.5 us -> 12.5 us
  transfers between devices with their start and end apart: 12 -> 12, of which waited for: 3 -> 6; matrix products, arithmetic and copies ran while one was open for 4% -> 1% of each run, Pallas kernels for 37% -> 38%
where the time goes in v4:
time: 185 us; the launch traced here: 184 us
  Pallas kernels  81.1 us (44%)
  waiting for transfers between devices  67.7 us (37%)
  starting transfers between devices  22.2 us (12%)
  local copies, waits for them, and re-layouts  12.5 us (7%)
    all_to_all x2, waiting for transfers between devices, local(): lax.all_to_all(array.reshape(owners * ranges, -1, *array.shape[2:]), axes...  60 us
    pallas_call x2, Pallas kernels, factor_slots(): pl.pallas_call(functools.partial(factor_kernel, first=first, share_slots=...  43.8 us
    pallas_call x4, Pallas kernels, form_spectrum(): pl.pallas_call(spectrum_kernel, out_shape=jax.ShapeDtypeStruct((bins, hei...  13.3 us
    unnamed x39, local copies, waits for them, and re-layouts  12.5 us
    all_to_all x2, starting transfers between devices, local(): lax.all_to_all(array.reshape(owners * ranges, -1, *array.shape[2:]), axes...  9.4 us
    ppermute x4, starting transfers between devices, shifted(): return lax.ppermute(array, axis, pairs)  7.86 us
    pallas_call x2, Pallas kernels, place_rows(): pl.pallas_call(functools.partial(place_kernel, first=first, share_slots=s...  7.5 us
    pallas_call x2, Pallas kernels, select_gates(): pl.pallas_call(functools.partial(select_kernel, chunks=len(spectra), owne...  5.95 us
  transfers between devices with their start and end apart: 12, of which 6 were waited for; matrix products, arithmetic and copies ran while one was open for 1% of the time, Pallas kernels for 38%

profile of v4, /device:TPU:1, one launch (start us, length us, event | category | flops | bytes accessed | tf_op | source)
XLA Modules:
  0.0 184.2 jit_solution(16079672471778748890)
XLA Ops:
  0.0 1.3 rim_rows.7
  1.3 2.0 %collective-permute-start.3 = (bf16[2,16,64,128]{3,2,1,0:T(8,128)(2,1)S(1)}, bf16[2,16,64,128]{3,2,1,0:T(8,128)(2,1)}, u32[]{:S(2)}, u32[]{:S(2)}) collective-permute-start(bf16[2,16,64,128]{3,2,1,0:T(8,128)(2,1)S(1)} %rim_rows.7), channel_id=1, source_target_pairs={{1,0},{2,1},{3,2},{5,4},{6,5},{7,6},{9,8},{10,9},{11,10},{13,12},{... | collective-permute-start | bytes 1572872 | tf_op jit(solution)/shard_map/ppermute | solution.py:23
  3.3 1.3 rim_rows.4
  4.5 1.9 %collective-permute-start = (bf16[2,16,64,128]{3,2,1,0:T(8,128)(2,1)S(1)}, bf16[2,16,64,128]{3,2,1,0:T(8,128)(2,1)}, u32[]{:S(2)}, u32[]{:S(2)}) collective-permute-start(bf16[2,16,64,128]{3,2,1,0:T(8,128)(2,1)S(1)} %rim_rows.4), channel_id=1, source_target_pairs={{1,0},{2,1},{3,2},{5,4},{6,5},{7,6},{9,8},{10,9},{11,10},{13,12},{... | collective-permute-start | bytes 1572872 | tf_op jit(solution)/shard_map/ppermute | solution.py:23
  6.5 1.3 rim_rows.5
  7.8 2.1 %collective-permute-start.1 = (bf16[2,16,64,128]{3,2,1,0:T(8,128)(2,1)S(1)}, bf16[2,16,64,128]{3,2,1,0:T(8,128)(2,1)}, u32[]{:S(2)}, u32[]{:S(2)}) collective-permute-start(bf16[2,16,64,128]{3,2,1,0:T(8,128)(2,1)S(1)} %rim_rows.5), channel_id=1, source_target_pairs={{1,0},{2,1},{3,2},{5,4},{6,5},{7,6},{9,8},{10,9},{11,10},{13,12},{... | collective-permute-start | bytes 1572872 | tf_op jit(solution)/shard_map/ppermute | solution.py:23
  9.9 1.3 rim_rows.6
  11.2 1.9 %collective-permute-start.2 = (bf16[2,16,64,128]{3,2,1,0:T(8,128)(2,1)S(1)}, bf16[2,16,64,128]{3,2,1,0:T(8,128)(2,1)S(1)}, u32[]{:S(2)}, u32[]{:S(2)}) collective-permute-start(bf16[2,16,64,128]{3,2,1,0:T(8,128)(2,1)S(1)} %rim_rows.6), channel_id=1, source_target_pairs={{1,0},{2,1},{3,2},{5,4},{6,5},{7,6},{9,8},{10,9},{11,10},{13,12},{... | collective-permute-start | bytes 1572872 | tf_op jit(solution)/shard_map/ppermute | solution.py:23
  13.1 0.1 copy.17
  13.3 0.2 reduce-window.9
  13.5 0.1 filter_rows.1.rows_ref
  13.7 0.1 pad_add_fusion.gates_ref
  13.8 3.4 %form_spectrum.7.refs_3_ = bf16[128,32,128]{2,1,0:T(8,128)(2,1)S(1)} custom-call(bf16[256,512]{1,0:T(8,128)(2,1)S(1)} %filter_rows.1.rows_ref, bf16[256,768]{1,0:T(8,128)(2,1)S(1)} %copy-done.13, f32[2,64,128,128]{3,2,1,0:T(8,128)} %own_ref.7, bf16[2,16,64,128]{3,2,1,0:T(8,128)(2,1)} %collective-permute-done.3.next_ref), custom_call_target="tpu_custom_call" | custom-call | flops 1342177280 | bytes 2097152 | tf_op jit(solution)/shard_map/form_spectrum/pallas_call | solution.py:143
  17.1 1.2 collective-permute-done.next_ref
  18.4 3.3 %form_spectrum.4.refs_0_ = bf16[128,32,128]{2,1,0:T(8,128)(2,1)S(1)} custom-call(bf16[256,512]{1,0:T(8,128)(2,1)S(1)} %filter_rows.1.rows_ref, bf16[256,768]{1,0:T(8,128)(2,1)S(1)} %copy-done.13, f32[2,64,128,128]{3,2,1,0:T(8,128)} %own_ref.7, bf16[2,16,64,128]{3,2,1,0:T(8,128)(2,1)} %collective-permute-done.next_ref), custom_call_target="tpu_custom_call" | custom-call | flops 1342177280 | bytes 2097152 | tf_op jit(solution)/shard_map/form_spectrum/pallas_call | solution.py:143
  21.7 2.3 %collective-permute-done.1.next_ref = bf16[2,16,64,128]{3,2,1,0:T(8,128)(2,1)} collective-permute-done((bf16[2,16,64,128]{3,2,1,0:T(8,128)(2,1)S(1)}, bf16[2,16,64,128]{3,2,1,0:T(8,128)(2,1)}, u32[]{:S(2)}, u32[]{:S(2)}) %collective-permute-start.1) | collective-permute-done | bytes 524320 | tf_op jit(solution)/shard_map/ppermute | solution.py:23
  24.0 3.3 %form_spectrum.5.refs_1_ = bf16[128,32,128]{2,1,0:T(8,128)(2,1)S(1)} custom-call(bf16[256,512]{1,0:T(8,128)(2,1)S(1)} %filter_rows.1.rows_ref, bf16[256,768]{1,0:T(8,128)(2,1)S(1)} %copy-done.13, f32[2,64,128,128]{3,2,1,0:T(8,128)} %own_ref.7, bf16[2,16,64,128]{3,2,1,0:T(8,128)(2,1)} %collective-permute-done.1.next_ref), custom_call_target="tpu_custom_call" | custom-call | flops 1342177280 | bytes 2097152 | tf_op jit(solution)/shard_map/form_spectrum/pallas_call | solution.py:143
  27.3 2.2 %collective-permute-done.2.next_ref = bf16[2,16,64,128]{3,2,1,0:T(8,128)(2,1)S(1)} collective-permute-done((bf16[2,16,64,128]{3,2,1,0:T(8,128)(2,1)S(1)}, bf16[2,16,64,128]{3,2,1,0:T(8,128)(2,1)S(1)}, u32[]{:S(2)}, u32[]{:S(2)}) %collective-permute-start.2) | collective-permute-done | bytes 524320 | tf_op jit(solution)/shard_map/ppermute | solution.py:23
  29.5 3.3 %form_spectrum.6.refs_2_ = bf16[128,32,128]{2,1,0:T(8,128)(2,1)S(1)} custom-call(bf16[256,512]{1,0:T(8,128)(2,1)S(1)} %filter_rows.1.rows_ref, bf16[256,768]{1,0:T(8,128)(2,1)S(1)} %copy-done.13, f32[2,64,128,128]{3,2,1,0:T(8,128)} %own_ref.7, bf16[2,16,64,128]{3,2,1,0:T(8,128)(2,1)S(1)} %collective-permute-done.2.next_ref), custom_call_target="tpu_custom_call" | custom-call | flops 1342177280 | bytes 2097152 | tf_op jit(solution)/shard_map/form_spectrum/pallas_call | solution.py:143
  32.8 4.1 %select_gates.3 = bf16[8,12,128,128]{3,2,1,0:T(8,128)(2,1)} custom-call(s32[18]{0:T(128)S(1)} %pad_add_fusion.1.index_ref, s32[128,128]{1,0:T(8,128)S(1)} %pad_add_fusion.gates_ref, bf16[128,32,128]{2,1,0:T(8,128)(2,1)S(1)} %form_spectrum.4.refs_0_, bf16[128,32,128]{2,1,0:T(8,128)(2,1)S(1)} %form_spectrum.5.refs_1_, ...), custom_call_target="tpu_custom_call" | custom-call | flops 805306368 | bytes 3145728 | tf_op jit(solution)/shard_map/select_gates/pallas_call | solution.py:212
  37.0 4.8 %all-to-all-start.1 = ((bf16[32,3,128,128]{3,2,1,0:T(8,128)(2,1)}), bf16[32,3,128,128]{3,2,1,0:T(8,128)(2,1)S(1)}, u32[]{:S(2)}, u32[]{:S(2)}) async-start(bf16[32,3,128,128]{3,2,1,0:T(8,128)(2,1)} %bitcast.13), calls=%async_computation.1 | async-start | bytes 6291456 | tf_op jit(solution)/shard_map/all_to_all | solution.py:620
  41.8 2.0 %copy.24.refs_4_.weights_ref = bf16[2,512,192]{2,1,0:T(8,128)(2,1)} copy(bf16[2,512,192]{1,2,0:T(8,128)(2,1)} %param.9) | data formatting | bytes 786432 | tf_op args[2]
  43.8 1.2 copy-done.3
  45.1 1.2 copy-done.5
  46.3 1.2 copy-done.7
  47.5 1.2 copy-done.9
  48.7 1.0 copy-done.10
  49.8 1.8 select_gates.2.refs_0_
  51.6 1.0 copy-done
  52.6 60.0 %all-to-all-done.1 = bf16[32,3,128,128]{3,2,1,0:T(8,128)(2,1)S(1)} async-done(((bf16[32,3,128,128]{3,2,1,0:T(8,128)(2,1)}), bf16[32,3,128,128]{3,2,1,0:T(8,128)(2,1)S(1)}, u32[]{:S(2)}, u32[]{:S(2)}) %all-to-all-start.1) | async-done | bytes 3145760 | tf_op jit(solution)/shard_map/all_to_all | solution.py:620
  112.6 4.6 %all-to-all-start = ((bf16[32,1,128,128]{3,2,1,0:T(8,128)(2,1)}), bf16[32,1,128,128]{3,2,1,0:T(8,128)(2,1)}, u32[]{:S(2)}, u32[]{:S(2)}) async-start(bf16[32,1,128,128]{3,2,1,0:T(8,128)(2,1)} %bitcast.12), calls=%async_computation | async-start | bytes 2097152 | tf_op jit(solution)/shard_map/all_to_all | solution.py:620
  117.2 0.1 copy.25.pivots_ref
  117.4 1.2 copy-done.1
  118.6 1.0 copy-done.11
  119.6 2.3 %form_beams.2.beams_ref = bf16[4,3,384,128]{3,2,1,0:T(8,128)(2,1)S(1)} custom-call(bf16[2,512,192]{2,1,0:T(8,128)(2,1)S(1)} %copy-done.11, bf16[8,4,3,128,128]{4,3,2,1,0:T(8,128)(2,1)S(1)} %bitcast.11, bf16[8,4,128,128]{3,2,1,0:T(8,128)(2,1)S(1)} %copy-done.1), custom_call_target="tpu_custom_call" | custom-call | flops 1207959552 | bytes 3145728 | tf_op jit(solution)/shard_map/form_beams/pallas_call | solution.py:269
  121.9 23.5 %factor_slots.2 = (bf16[6,96,384]{2,1,0:T(8,128)(2,1)S(1)}, bf16[6,96,384]{2,1,0:T(8,128)(2,1)S(1)}, bf16[6,96,384]{2,1,0:T(8,128)(2,1)S(1)}, bf16[6,96,384]{2,1,0:T(8,128)(2,1)S(1)}) custom-call(s32[18]{0:T(128)S(1)} %pad_add_fusion.1.index_ref, s32[128,192]{1,0:T(8,128)S(1)} %copy.25.pivots_ref, bf16[4,3,384,128]{3,2,1,0:T(8,128)(2,1)S(1)} %form_beams.2.beams_ref), custom_call_target="tpu_custom_call" | custom-call | flops 339738624 | bytes 1179648 | tf_op jit(solution)/shard_map/factor_slots/pallas_call | solution.py:504
  145.5 1.7 collective-permute-start.7
  147.1 0.2 collective-permute-start.8
  147.4 0.3 collective-permute-start.9
  147.7 1.0 copy-done.12
  148.7 3.0 %form_beams.3.beams_ref = bf16[4,1,384,128]{3,2,1,0:T(8,128)(2,1)S(1)} custom-call(bf16[2,512,192]{2,1,0:T(8,128)(2,1)S(1)} %copy-done.12, bf16[8,4,1,128,128]{4,3,2,1,0:T(8,128)(2,1)} %bitcast.6.arrived_ref, bf16[6,96,384]{2,1,0:T(8,128)(2,1)S(1)} %get-tuple-element.13.refs_0_), custom_call_target="tpu_custom_call" | custom-call | flops 402653184 | bytes 1048576 | tf_op jit(solution)/shard_map/form_beams/pallas_call | solution.py:269
  151.7 20.2 %factor_slots.3 = (bf16[2,96,384]{2,1,0:T(8,128)(2,1)S(1)}, bf16[2,96,384]{2,1,0:T(8,128)(2,1)S(1)}, bf16[2,96,384]{2,1,0:T(8,128)(2,1)S(1)}, bf16[2,96,384]{2,1,0:T(8,128)(2,1)S(1)}) custom-call(s32[18]{0:T(128)S(1)} %pad_add_fusion.1.index_ref, s32[128,192]{1,0:T(8,128)S(1)} %copy.25.pivots_ref, bf16[4,1,384,128]{3,2,1,0:T(8,128)(2,1)S(1)} %form_beams.3.beams_ref), custom_call_target="tpu_custom_call" | custom-call | flops 113246208 | bytes 393216 | tf_op jit(solution)/shard_map/factor_slots/pallas_call | solution.py:504
  172.0 1.5 collective-permute-start.4
  173.5 1.2 collective-permute-start.5
  174.7 5.3 %place_rows.2.refs_4_ = f32[32,96,384]{2,1,0:T(8,128)} custom-call(s32[18]{0:T(128)S(1)} %pad_add_fusion.1.index_ref, bf16[6,96,384]{2,1,0:T(8,128)(2,1)S(1)} %get-tuple-element.13.refs_0_, bf16[6,96,384]{2,1,0:T(8,128)(2,1)S(1)} %collective-permute-done.7.refs_1_, bf16[6,96,384]{2,1,0:T(8,128)(2,1)S(1)} %collective-permute-done.8.refs_2_, ...), custom_call_target="tpu_custom_call" | custom-call | tf_op jit(solution)/shard_map/place_rows/pallas_call | solution.py:559
  180.0 1.3 collective-permute-done.5.refs_2_
  181.3 0.6 collective-permute-done.6.refs_3_
  181.9 2.2 %place_rows.3 = f32[32,96,384]{2,1,0:T(8,128)} custom-call(s32[18]{0:T(128)S(1)} %pad_add_fusion.1.index_ref, bf16[2,96,384]{2,1,0:T(8,128)(2,1)S(1)} %get-tuple-element.14.refs_0_, bf16[2,96,384]{2,1,0:T(8,128)(2,1)S(1)} %collective-permute-done.4.refs_1_, bf16[2,96,384]{2,1,0:T(8,128)(2,1)S(1)} %collective-permute-done.5.refs_2_, ...), custom_call_target="tpu_custom_call", output_to_operand_aliasing={{}: (5, {})} | custom-call | tf_op jit(solution)/shard_map/place_rows/pallas_call | solution.py:559
  (38 shorter events, 0.2 us)
Async XLA Ops:
  1.3 12.5 %collective-permute-start.3 = (bf16[2,16,64,128]{3,2,1,0:T(8,128)(2,1)S(1)}, bf16[2,16,64,128]{3,2,1,0:T(8,128)(2,1)}, u32[]{:S(2)}, u32[]{:S(2)}) collective-permute-start(bf16[2,16,64,128]{3,2,1,0:T(8,128)(2,1)S(1)} %rim_rows.7), channel_id=1, source_target_pairs={{1,0},{2,1},{3,2},{5,4},{6,5},{7,6},{9,8},{10,9},{11,10},{13,12},{... | collective-permute-start | bytes 1572872 | tf_op jit(solution)/shard_map/ppermute | solution.py:23
  4.5 13.8 %collective-permute-start = (bf16[2,16,64,128]{3,2,1,0:T(8,128)(2,1)S(1)}, bf16[2,16,64,128]{3,2,1,0:T(8,128)(2,1)}, u32[]{:S(2)}, u32[]{:S(2)}) collective-permute-start(bf16[2,16,64,128]{3,2,1,0:T(8,128)(2,1)S(1)} %rim_rows.4), channel_id=1, source_target_pairs={{1,0},{2,1},{3,2},{5,4},{6,5},{7,6},{9,8},{10,9},{11,10},{13,12},{... | collective-permute-start | bytes 1572872 | tf_op jit(solution)/shard_map/ppermute | solution.py:23
  7.8 5.3 %copy-start.15 = (s32[128,64]{0,1:T(8,128)S(1)}, s32[128,64]{0,1:T(8,128)}, u32[]{:S(2)}) copy-start(s32[128,64]{0,1:T(8,128)} %param.12) | copy-start | bytes 98308
  7.8 5.5 %copy-start.17 = (s32[8]{0:T(128)S(1)}, s32[8]{0:T(128)}, u32[]{:S(2)}) copy-start(s32[8]{0:T(128)} %param.11) | copy-start | bytes 100
  7.8 5.7 %copy-start.16 = (f32[2,64]{1,0:T(2,128)S(1)}, f32[2,64]{1,0:T(2,128)}, u32[]{:S(2)}) copy-start(f32[2,64]{1,0:T(2,128)} %param.8) | copy-start | bytes 1540
  7.8 6.0 %copy-start.13 = (bf16[256,768]{1,0:T(8,128)(2,1)S(1)}, bf16[256,768]{1,0:T(8,128)(2,1)}, u32[]{:S(2)}) copy-start(bf16[256,768]{1,0:T(8,128)(2,1)} %constant.33.clone.table_ref) | copy-start | bytes 1179652
  7.8 16.2 %collective-permute-start.1 = (bf16[2,16,64,128]{3,2,1,0:T(8,128)(2,1)S(1)}, bf16[2,16,64,128]{3,2,1,0:T(8,128)(2,1)}, u32[]{:S(2)}, u32[]{:S(2)}) collective-permute-start(bf16[2,16,64,128]{3,2,1,0:T(8,128)(2,1)S(1)} %rim_rows.5), channel_id=1, source_target_pairs={{1,0},{2,1},{3,2},{5,4},{6,5},{7,6},{9,8},{10,9},{11,10},{13,12},{... | collective-permute-start | bytes 1572872 | tf_op jit(solution)/shard_map/ppermute | solution.py:23
  11.2 18.3 %collective-permute-start.2 = (bf16[2,16,64,128]{3,2,1,0:T(8,128)(2,1)S(1)}, bf16[2,16,64,128]{3,2,1,0:T(8,128)(2,1)S(1)}, u32[]{:S(2)}, u32[]{:S(2)}) collective-permute-start(bf16[2,16,64,128]{3,2,1,0:T(8,128)(2,1)S(1)} %rim_rows.6), channel_id=1, source_target_pairs={{1,0},{2,1},{3,2},{5,4},{6,5},{7,6},{9,8},{10,9},{11,10},{13,12},{... | collective-permute-start | bytes 1572872 | tf_op jit(solution)/shard_map/ppermute | solution.py:23
  17.1 15.7 %copy-start.2 = (bf16[128,32,128]{2,1,0:T(8,128)(2,1)}, bf16[128,32,128]{2,1,0:T(8,128)(2,1)S(1)}, u32[]{:S(2)}) copy-start(bf16[128,32,128]{2,1,0:T(8,128)(2,1)S(1)} %form_spectrum.7.refs_3_) | copy-start | bytes 3145732
  21.7 11.1 %copy-start.4 = (bf16[128,32,128]{2,1,0:T(8,128)(2,1)}, bf16[128,32,128]{2,1,0:T(8,128)(2,1)S(1)}, u32[]{:S(2)}) copy-start(bf16[128,32,128]{2,1,0:T(8,128)(2,1)S(1)} %form_spectrum.4.refs_0_) | copy-start | bytes 3145732
  27.3 5.5 %copy-start.6 = (bf16[128,32,128]{2,1,0:T(8,128)(2,1)}, bf16[128,32,128]{2,1,0:T(8,128)(2,1)S(1)}, u32[]{:S(2)}) copy-start(bf16[128,32,128]{2,1,0:T(8,128)(2,1)S(1)} %form_spectrum.5.refs_1_) | copy-start | bytes 3145732
  32.8 4.1 %copy-start.8 = (bf16[128,32,128]{2,1,0:T(8,128)(2,1)}, bf16[128,32,128]{2,1,0:T(8,128)(2,1)S(1)}, u32[]{:S(2)}) copy-start(bf16[128,32,128]{2,1,0:T(8,128)(2,1)S(1)} %form_spectrum.6.refs_2_) | copy-start | bytes 3145732
  37.0 75.6 %all-to-all-start.1 = ((bf16[32,3,128,128]{3,2,1,0:T(8,128)(2,1)}), bf16[32,3,128,128]{3,2,1,0:T(8,128)(2,1)S(1)}, u32[]{:S(2)}, u32[]{:S(2)}) async-start(bf16[32,3,128,128]{3,2,1,0:T(8,128)(2,1)} %bitcast.13), calls=%async_computation.1 | async-start | bytes 6291456 | tf_op jit(solution)/shard_map/all_to_all | solution.py:620
  41.8 75.5 %copy-start.14 = (s32[128,192]{0,1:T(8,128)S(1)}, s32[128,192]{0,1:T(8,128)}, u32[]{:S(2)}) copy-start(s32[128,192]{0,1:T(8,128)} %param.10) | copy-start | bytes 294916
  43.8 1.2 copy-start.3
  45.1 1.2 copy-start.5
  46.3 1.2 copy-start.7
  47.5 1.2 copy-start.9
  48.7 1.0 copy-start.10
  51.6 1.0 copy-start
  112.6 35.1 %all-to-all-start = ((bf16[32,1,128,128]{3,2,1,0:T(8,128)(2,1)}), bf16[32,1,128,128]{3,2,1,0:T(8,128)(2,1)}, u32[]{:S(2)}, u32[]{:S(2)}) async-start(bf16[32,1,128,128]{3,2,1,0:T(8,128)(2,1)} %bitcast.12), calls=%async_computation | async-start | bytes 2097152 | tf_op jit(solution)/shard_map/all_to_all | solution.py:620
  117.4 1.2 copy-start.1
  118.6 1.0 copy-start.11
  145.5 29.2 %collective-permute-start.7 = (bf16[6,96,384]{2,1,0:T(8,128)(2,1)S(1)}, bf16[6,96,384]{2,1,0:T(8,128)(2,1)S(1)}, u32[]{:S(2)}, u32[]{:S(2)}) collective-permute-start(bf16[6,96,384]{2,1,0:T(8,128)(2,1)S(1)} %get-tuple-element.18), channel_id=1, source_target_pairs={{0,1},{1,2},{2,3},{3,0},{4,5},{5,6},{6,7},{7,4},{8,9},{9,10},{10,1... | collective-permute-start | bytes 1327112 | tf_op jit(solution)/shard_map/ppermute | solution.py:294
  147.1 27.6 %collective-permute-start.8 = (bf16[6,96,384]{2,1,0:T(8,128)(2,1)S(1)}, bf16[6,96,384]{2,1,0:T(8,128)(2,1)S(1)}, u32[]{:S(2)}, u32[]{:S(2)}) collective-permute-start(bf16[6,96,384]{2,1,0:T(8,128)(2,1)S(1)} %get-tuple-element.19), channel_id=1, source_target_pairs={{0,2},{1,3},{2,0},{3,1},{4,6},{5,7},{6,4},{7,5},{8,10},{9,11},{10,... | collective-permute-start | bytes 1327112 | tf_op jit(solution)/shard_map/ppermute | solution.py:294
  147.4 27.3 %collective-permute-start.9 = (bf16[6,96,384]{2,1,0:T(8,128)(2,1)S(1)}, bf16[6,96,384]{2,1,0:T(8,128)(2,1)S(1)}, u32[]{:S(2)}, u32[]{:S(2)}) collective-permute-start(bf16[6,96,384]{2,1,0:T(8,128)(2,1)S(1)} %get-tuple-element.20), channel_id=1, source_target_pairs={{0,3},{1,0},{2,1},{3,2},{4,7},{5,4},{6,5},{7,6},{8,11},{9,8},{10,9... | collective-permute-start | bytes 1327112 | tf_op jit(solution)/shard_map/ppermute | solution.py:294
  147.7 1.0 copy-start.12
  172.0 8.0 %collective-permute-start.4 = (bf16[2,96,384]{2,1,0:T(8,128)(2,1)S(1)}, bf16[2,96,384]{2,1,0:T(8,128)(2,1)S(1)}, u32[]{:S(2)}, u32[]{:S(2)}) collective-permute-start(bf16[2,96,384]{2,1,0:T(8,128)(2,1)S(1)} %get-tuple-element.15), channel_id=1, source_target_pairs={{0,1},{1,2},{2,3},{3,0},{4,5},{5,6},{6,7},{7,4},{8,9},{9,10},{10,1... | collective-permute-start | bytes 442376 | tf_op jit(solution)/shard_map/ppermute | solution.py:294
  173.5 7.9 %collective-permute-start.5 = (bf16[2,96,384]{2,1,0:T(8,128)(2,1)S(1)}, bf16[2,96,384]{2,1,0:T(8,128)(2,1)S(1)}, u32[]{:S(2)}, u32[]{:S(2)}) collective-permute-start(bf16[2,96,384]{2,1,0:T(8,128)(2,1)S(1)} %get-tuple-element.16), channel_id=1, source_target_pairs={{0,2},{1,3},{2,0},{3,1},{4,6},{5,7},{6,4},{7,5},{8,10},{9,11},{10,... | collective-permute-start | bytes 442376 | tf_op jit(solution)/shard_map/ppermute | solution.py:294
  174.7 7.3 %collective-permute-start.6 = (bf16[2,96,384]{2,1,0:T(8,128)(2,1)S(1)}, bf16[2,96,384]{2,1,0:T(8,128)(2,1)S(1)}, u32[]{:S(2)}, u32[]{:S(2)}) collective-permute-start(bf16[2,96,384]{2,1,0:T(8,128)(2,1)S(1)} %get-tuple-element.17), channel_id=1, source_target_pairs={{0,3},{1,0},{2,1},{3,2},{4,7},{5,4},{6,5},{7,6},{8,11},{9,8},{10,9... | collective-permute-start | bytes 442376 | tf_op jit(solution)/shard_map/ppermute | solution.py:294

commit v5 on v3

--- a/solution.py
+++ b/solution.py
@@ -3,6 +3,7 @@
 
 import jax
 import jax.numpy as jnp
+import numpy as np
 from jax import lax
 from jax.experimental import pallas as pl
 from jax.experimental.pallas import tpu as pltpu
@@ -22,18 +23,16 @@
     return lax.ppermute(array, axis, pairs)
 
 
-def complex_block(real_part, imag_part):
-    upper_row = jnp.stack([real_part, imag_part])
-    lower_row = jnp.stack([-imag_part, real_part])
-    return jnp.stack([upper_row, lower_row])
-
-
 def doppler_table(pulse_count):
-    pulse_index = jnp.arange(pulse_count, dtype=jnp.int32)
+    pulse_index = np.arange(pulse_count)
     phase_index = pulse_index[:, None] * pulse_index[None, :] % pulse_count
-    angle_table = phase_index.astype(jnp.float32) * (2.0 * math.pi / pulse_count)
-    norm_scale = 1.0 / math.sqrt(pulse_count)
-    return complex_block(jnp.cos(angle_table) * norm_scale, jnp.sin(angle_table) * norm_scale)
+    angle_table = phase_index.astype(np.float32) * np.float32(2.0 * math.pi / pulse_count)
+    norm_scale = np.float32(1.0 / math.sqrt(pulse_count))
+    real_part, imag_part = np.cos(angle_table) * norm_scale, np.sin(angle_table) * norm_scale
+    table = np.block([[real_part.T, imag_part.T], [-imag_part.T, real_part.T]])
+    high = table.astype(BF16)
+    low = (table - high.astype(np.float32)).astype(BF16)
+    return jnp.asarray(np.concatenate([high, high, low], axis=1))
 
 
 def filter_kernel(replica_ref, out_ref):
@@ -174,7 +173,8 @@
 def select_kernel(
     index_ref, gates_ref, *refs, chunks, owners, ranges, first, share_slots, pack
 ):
-    spectrum_refs, out_ref = refs[:chunks], refs[-1]
+    spectrum_refs, out_ref, token_ref = refs[:chunks], refs[-2], refs[-1]
+    token_ref[...] = jnp.zeros_like(token_ref)
     bin_count, height, gate_rows = spectrum_refs[0].shape
     some, groups, _, width = out_ref.shape
     half = height // 2
@@ -220,12 +220,18 @@
             share_slots=share_slots,
             pack=pack,
         ),
-        out_shape=jax.ShapeDtypeStruct((owners, groups, rows, width), BF16),
+        out_shape=[
+            jax.ShapeDtypeStruct((owners, groups, rows, width), BF16),
+            jax.ShapeDtypeStruct((8, LANES), jnp.int32),
+        ],
         grid=(owners // some,),
         in_specs=[pl.BlockSpec(memory_space=pltpu.SMEM)]
         + [pl.BlockSpec(memory_space=pltpu.VMEM)] * (1 + len(spectra))
         + [pl.BlockSpec(memory_space=pl.ANY)] * len(earlier),
-        out_specs=pl.BlockSpec((some, groups, rows, width), lambda i: (i, 0, 0, 0)),
+        out_specs=[
+            pl.BlockSpec((some, groups, rows, width), lambda i: (i, 0, 0, 0)),
+            pl.BlockSpec((8, LANES), lambda i: (0, 0)),
+        ],
         compiler_params=PARAMS,
         cost_estimate=pl.CostEstimate(
             flops=2 * owners * groups * pack * rows * gate_rows * width,
@@ -357,12 +363,14 @@
     for first in range(0, PANEL, 8):
         span = range(first, first + 8)
         small = {(i, j): lane_spread(rows[i][0], j) for i in span for j in span if j >= i}
+        inverses = []
         for t in range(first, first + 8, 2):
             u = t + 1
             inverse = refined_reciprocal(small[t, t])
             cross = small[t, t] * small[u, u] - small[t, u] * small[t, u]
             guess = pl.reciprocal(cross, approx=True)
             second = (small[t, t] * guess) * (2.0 - cross * guess)
+            inverses += [inverse, second]
             scales += [lax.rsqrt(small[t, t]), lax.rsqrt(cross * inverse)]
             factor = small[t, u] * inverse
             for j in range(u + 1, first + 8):
@@ -376,15 +384,14 @@
                 rows[i] = [
                     x - one * y - two * z for x, y, z in zip(rows[i], rows[t], rows[u])
                 ]
-        for t in span:
-            rows[t] = [x * scales[t] for x in rows[t]]
+        ratios = [rows[t][0] * inverse for t, inverse in zip(span, inverses)]
         for i in range(first + 8, PANEL):
-            factors = [lane_spread(rows[t][0], i) for t in span]
+            factors = [lane_spread(ratio, i) for ratio in ratios]
             rows[i] = [
                 x - tree_sum([f * rows[t][w] for f, t in zip(factors, span)])
                 for w, x in enumerate(rows[i])
             ]
-    return rows
+    return [[x * scale for x in row] for row, scale in zip(rows, scales)]
 
 
 def factor_kernel(
@@ -590,10 +597,7 @@
     chunk_rows = ch_local // chunks
     rim = -(-(tap_count - 1) // 16) * 16
     filters = filter_rows(replica, gate_rows)
-    table = doppler_table(pulse_count).transpose(0, 3, 1, 2)
-    table = table.reshape(2 * pulse_count, -1)
-    table_high = lax.reduce_precision(table, exponent_bits=8, mantissa_bits=7)
-    table = jnp.concatenate([table_high, table_high, table - table_high], axis=1).astype(BF16)
+    table = doppler_table(pulse_count)
     following = [shifted(rim_rows(raw_echo, rim, c, chunks), "rng", -1) for c in range(chunks)]
     spectra = [
         form_spectrum(filters, table, raw_echo, following[c], c, chunks) for c in range(chunks)
@@ -607,14 +611,14 @@
     count_rows = float(train_local * ranges)
 
     parts = slot_parts(share_slots, pack)
-    outgoing = []
+    outgoing, tokens = [], []
     for first, count in parts:
         earlier = [beam_weights] if first > 0 else []
-        outgoing.append(
-            select_gates(
-                spectra, index, gates, first, count, share_slots, owners, ranges, pack, earlier
-            )
+        array, token = select_gates(
+            spectra, index, gates, first, count, share_slots, owners, ranges, pack, earlier
         )
+        outgoing.append(array)
+        tokens.append(token)
     axes = ("dop", "rng")
     sent = [
         lax.all_to_all(
@@ -626,7 +630,7 @@
         ).reshape(owners, ranges, -1, *array.shape[2:])
         for array in outgoing
     ]
-    result, earlier = [], outgoing[1:]
+    result, earlier = [], tokens[1:]
     for (first, count), arrived in zip(parts, sent):
         beams = form_beams(arrived, beam_weights, earlier)
         factors = factor_slots(beams, pivots, index, first, count, share_slots, pack, count_rows)

time: 188 us -> 182 us (0.968)
  waiting for transfers between devices: 62 us -> 67.7 us
  other arithmetic: 4.81 us -> 0.38 us
  starting transfers between devices: 25.2 us -> 22.2 us
  local copies, waits for them, and re-layouts: 13.6 us -> 11.3 us
    ppermute x4, waiting for transfers between devices: 0.01 us -> 5.66 us  [shifted(): return lax.ppermute(array, axis, pairs)]
    all_to_all x2, starting transfers between devices: 12.4 us -> 9.4 us  [local(): lax.all_to_all(array.reshape(owners * ranges, -1, *array.shape[2:]), axes...]
  transfers between devices with their start and end apart: 12 -> 12, of which waited for: 3 -> 6; matrix products, arithmetic and copies ran while one was open for 4% -> 1% of each run, Pallas kernels for 37% -> 38%
where the time goes in v5:
time: 182 us; the launch traced here: 181 us
  Pallas kernels  78.8 us (43%)
  waiting for transfers between devices  67.7 us (37%)
  starting transfers between devices  22.2 us (12%)
  local copies, waits for them, and re-layouts  11.3 us (6%)
    all_to_all x2, waiting for transfers between devices, local(): lax.all_to_all(array.reshape(owners * ranges, -1, *array.shape[2:]), axes...  60.1 us
    pallas_call x2, Pallas kernels, factor_slots(): pl.pallas_call(functools.partial(factor_kernel, first=first, share_slots=...  43.3 us
    pallas_call x4, Pallas kernels, form_spectrum(): pl.pallas_call(spectrum_kernel, out_shape=jax.ShapeDtypeStruct((bins, hei...  13.3 us
    unnamed x37, local copies, waits for them, and re-layouts  11.3 us
    all_to_all x2, starting transfers between devices, local(): lax.all_to_all(array.reshape(owners * ranges, -1, *array.shape[2:]), axes...  9.4 us
    ppermute x4, starting transfers between devices, shifted(): return lax.ppermute(array, axis, pairs)  7.86 us
    pallas_call x2, Pallas kernels, place_rows(): pl.pallas_call(functools.partial(place_kernel, first=first, share_slots=s...  7.5 us
    pallas_call x2, Pallas kernels, select_gates(): pl.pallas_call(functools.partial(select_kernel, chunks=len(spectra), owne...  5.93 us
  transfers between devices with their start and end apart: 12, of which 6 were waited for; matrix products, arithmetic and copies ran while one was open for 1% of the time, Pallas kernels for 38%

profile of v5, /device:TPU:1, one launch (start us, length us, event | category | flops | bytes accessed | tf_op | source)
XLA Modules:
  0.0 180.7 jit_solution(11568430763073990646)
XLA Ops:
  0.0 1.3 rim_rows.7
  1.3 2.0 %collective-permute-start.3 = (bf16[2,16,64,128]{3,2,1,0:T(8,128)(2,1)S(1)}, bf16[2,16,64,128]{3,2,1,0:T(8,128)(2,1)}, u32[]{:S(2)}, u32[]{:S(2)}) collective-permute-start(bf16[2,16,64,128]{3,2,1,0:T(8,128)(2,1)S(1)} %rim_rows.7), channel_id=1, source_target_pairs={{1,0},{2,1},{3,2},{5,4},{6,5},{7,6},{9,8},{10,9},{11,10},{13,12},{... | collective-permute-start | bytes 1572872 | tf_op jit(solution)/shard_map/ppermute | solution.py:23
  3.3 1.3 rim_rows.4
  4.5 1.9 %collective-permute-start = (bf16[2,16,64,128]{3,2,1,0:T(8,128)(2,1)S(1)}, bf16[2,16,64,128]{3,2,1,0:T(8,128)(2,1)}, u32[]{:S(2)}, u32[]{:S(2)}) collective-permute-start(bf16[2,16,64,128]{3,2,1,0:T(8,128)(2,1)S(1)} %rim_rows.4), channel_id=1, source_target_pairs={{1,0},{2,1},{3,2},{5,4},{6,5},{7,6},{9,8},{10,9},{11,10},{13,12},{... | collective-permute-start | bytes 1572872 | tf_op jit(solution)/shard_map/ppermute | solution.py:23
  6.5 1.3 rim_rows.5
  7.8 2.1 %collective-permute-start.1 = (bf16[2,16,64,128]{3,2,1,0:T(8,128)(2,1)S(1)}, bf16[2,16,64,128]{3,2,1,0:T(8,128)(2,1)}, u32[]{:S(2)}, u32[]{:S(2)}) collective-permute-start(bf16[2,16,64,128]{3,2,1,0:T(8,128)(2,1)S(1)} %rim_rows.5), channel_id=1, source_target_pairs={{1,0},{2,1},{3,2},{5,4},{6,5},{7,6},{9,8},{10,9},{11,10},{13,12},{... | collective-permute-start | bytes 1572872 | tf_op jit(solution)/shard_map/ppermute | solution.py:23
  9.9 1.3 rim_rows.6
  11.2 1.9 %collective-permute-start.2 = (bf16[2,16,64,128]{3,2,1,0:T(8,128)(2,1)S(1)}, bf16[2,16,64,128]{3,2,1,0:T(8,128)(2,1)S(1)}, u32[]{:S(2)}, u32[]{:S(2)}) collective-permute-start(bf16[2,16,64,128]{3,2,1,0:T(8,128)(2,1)S(1)} %rim_rows.6), channel_id=1, source_target_pairs={{1,0},{2,1},{3,2},{5,4},{6,5},{7,6},{9,8},{10,9},{11,10},{13,12},{... | collective-permute-start | bytes 1572872 | tf_op jit(solution)/shard_map/ppermute | solution.py:23
  13.1 0.1 copy.17
  13.3 0.2 reduce-window.9
  13.5 0.1 pad_add_fusion.1.index_ref
  13.5 0.1 filter_rows.1.rows_ref
  13.7 0.1 pad_add_fusion.gates_ref
  13.8 3.4 %form_spectrum.7.refs_3_ = bf16[128,32,128]{2,1,0:T(8,128)(2,1)S(1)} custom-call(bf16[256,512]{1,0:T(8,128)(2,1)S(1)} %filter_rows.1.rows_ref, bf16[256,768]{1,0:T(8,128)(2,1)S(1)} %copy-done.11, f32[2,64,128,128]{3,2,1,0:T(8,128)} %own_ref.7, bf16[2,16,64,128]{3,2,1,0:T(8,128)(2,1)} %collective-permute-done.3.next_ref), custom_call_target="tpu_custom_call" | custom-call | flops 1342177280 | bytes 2097152 | tf_op jit(solution)/shard_map/form_spectrum/pallas_call | solution.py:143
  17.1 1.2 collective-permute-done.next_ref
  18.4 3.3 %form_spectrum.4.refs_0_ = bf16[128,32,128]{2,1,0:T(8,128)(2,1)S(1)} custom-call(bf16[256,512]{1,0:T(8,128)(2,1)S(1)} %filter_rows.1.rows_ref, bf16[256,768]{1,0:T(8,128)(2,1)S(1)} %copy-done.11, f32[2,64,128,128]{3,2,1,0:T(8,128)} %own_ref.7, bf16[2,16,64,128]{3,2,1,0:T(8,128)(2,1)} %collective-permute-done.next_ref), custom_call_target="tpu_custom_call" | custom-call | flops 1342177280 | bytes 2097152 | tf_op jit(solution)/shard_map/form_spectrum/pallas_call | solution.py:143
  21.7 2.3 %collective-permute-done.1.next_ref = bf16[2,16,64,128]{3,2,1,0:T(8,128)(2,1)} collective-permute-done((bf16[2,16,64,128]{3,2,1,0:T(8,128)(2,1)S(1)}, bf16[2,16,64,128]{3,2,1,0:T(8,128)(2,1)}, u32[]{:S(2)}, u32[]{:S(2)}) %collective-permute-start.1) | collective-permute-done | bytes 524320 | tf_op jit(solution)/shard_map/ppermute | solution.py:23
  24.0 3.3 %form_spectrum.5.refs_1_ = bf16[128,32,128]{2,1,0:T(8,128)(2,1)S(1)} custom-call(bf16[256,512]{1,0:T(8,128)(2,1)S(1)} %filter_rows.1.rows_ref, bf16[256,768]{1,0:T(8,128)(2,1)S(1)} %copy-done.11, f32[2,64,128,128]{3,2,1,0:T(8,128)} %own_ref.7, bf16[2,16,64,128]{3,2,1,0:T(8,128)(2,1)} %collective-permute-done.1.next_ref), custom_call_target="tpu_custom_call" | custom-call | flops 1342177280 | bytes 2097152 | tf_op jit(solution)/shard_map/form_spectrum/pallas_call | solution.py:143
  27.3 2.2 %collective-permute-done.2.next_ref = bf16[2,16,64,128]{3,2,1,0:T(8,128)(2,1)S(1)} collective-permute-done((bf16[2,16,64,128]{3,2,1,0:T(8,128)(2,1)S(1)}, bf16[2,16,64,128]{3,2,1,0:T(8,128)(2,1)S(1)}, u32[]{:S(2)}, u32[]{:S(2)}) %collective-permute-start.2) | collective-permute-done | bytes 524320 | tf_op jit(solution)/shard_map/ppermute | solution.py:23
  29.5 3.3 %form_spectrum.6.refs_2_ = bf16[128,32,128]{2,1,0:T(8,128)(2,1)S(1)} custom-call(bf16[256,512]{1,0:T(8,128)(2,1)S(1)} %filter_rows.1.rows_ref, bf16[256,768]{1,0:T(8,128)(2,1)S(1)} %copy-done.11, f32[2,64,128,128]{3,2,1,0:T(8,128)} %own_ref.7, bf16[2,16,64,128]{3,2,1,0:T(8,128)(2,1)S(1)} %collective-permute-done.2.next_ref), custom_call_target="tpu_custom_call" | custom-call | flops 1342177280 | bytes 2097152 | tf_op jit(solution)/shard_map/form_spectrum/pallas_call | solution.py:143
  32.8 4.1 %select_gates.3 = (bf16[8,12,128,128]{3,2,1,0:T(8,128)(2,1)}, s32[8,128]{1,0:T(8,128)}) custom-call(s32[18]{0:T(128)S(1)} %pad_add_fusion.1.index_ref, s32[128,128]{1,0:T(8,128)S(1)} %pad_add_fusion.gates_ref, bf16[128,32,128]{2,1,0:T(8,128)(2,1)S(1)} %form_spectrum.4.refs_0_, bf16[128,32,128]{2,1,0:T(8,128)(2,1)S(1)} %form_spectrum.5.refs_1_, ...), custom_call_target="tpu_custom_call" | custom-call | flops 805306368 | bytes 3145728 | tf_op jit(solution)/shard_map/select_gates/pallas_call | solution.py:213
  37.0 4.8 %all-to-all-start.1 = ((bf16[32,3,128,128]{3,2,1,0:T(8,128)(2,1)}), bf16[32,3,128,128]{3,2,1,0:T(8,128)(2,1)S(1)}, u32[]{:S(2)}, u32[]{:S(2)}) async-start(bf16[32,3,128,128]{3,2,1,0:T(8,128)(2,1)} %bitcast.13), calls=%async_computation.1 | async-start | bytes 6291456 | tf_op jit(solution)/shard_map/all_to_all | solution.py:624
  41.8 2.0 %copy.24.refs_4_.weights_ref = bf16[2,512,192]{2,1,0:T(8,128)(2,1)} copy(bf16[2,512,192]{1,2,0:T(8,128)(2,1)} %param.9) | data formatting | bytes 786432 | tf_op args[2]
  43.8 1.2 copy-done.1
  45.1 1.2 copy-done.3
  46.3 1.2 copy-done.5
  47.5 1.2 copy-done.7
  48.7 1.0 copy-done.8
  49.8 1.8 select_gates.2
  51.6 1.0 copy-done.12
  52.6 60.1 %all-to-all-done.1 = bf16[32,3,128,128]{3,2,1,0:T(8,128)(2,1)S(1)} async-done(((bf16[32,3,128,128]{3,2,1,0:T(8,128)(2,1)}), bf16[32,3,128,128]{3,2,1,0:T(8,128)(2,1)S(1)}, u32[]{:S(2)}, u32[]{:S(2)}) %all-to-all-start.1) | async-done | bytes 3145760 | tf_op jit(solution)/shard_map/all_to_all | solution.py:624
  112.6 4.6 %all-to-all-start = ((bf16[32,1,128,128]{3,2,1,0:T(8,128)(2,1)}), bf16[32,1,128,128]{3,2,1,0:T(8,128)(2,1)}, u32[]{:S(2)}, u32[]{:S(2)}) async-start(bf16[32,1,128,128]{3,2,1,0:T(8,128)(2,1)} %bitcast.12), calls=%async_computation | async-start | bytes 2097152 | tf_op jit(solution)/shard_map/all_to_all | solution.py:624
  117.2 0.1 copy.25.pivots_ref
  117.4 1.0 copy-done.9
  118.4 1.4 form_beams.2.beams_ref
  119.8 23.7 %factor_slots.2 = (bf16[6,96,384]{2,1,0:T(8,128)(2,1)S(1)}, bf16[6,96,384]{2,1,0:T(8,128)(2,1)S(1)}, bf16[6,96,384]{2,1,0:T(8,128)(2,1)S(1)}, bf16[6,96,384]{2,1,0:T(8,128)(2,1)S(1)}) custom-call(s32[18]{0:T(128)S(1)} %pad_add_fusion.1.index_ref, s32[128,192]{1,0:T(8,128)S(1)} %copy.25.pivots_ref, bf16[4,3,384,128]{3,2,1,0:T(8,128)(2,1)S(1)} %form_beams.2.beams_ref), custom_call_target="tpu_custom_call" | custom-call | flops 339738624 | bytes 1179648 | tf_op jit(solution)/shard_map/factor_slots/pallas_call | solution.py:508
  143.6 1.7 collective-permute-start.7
  145.2 0.2 collective-permute-start.8
  145.4 0.3 collective-permute-start.9
  145.8 1.0 copy-done.10
  146.8 2.1 %form_beams.3.beams_ref = bf16[4,1,384,128]{3,2,1,0:T(8,128)(2,1)S(1)} custom-call(bf16[2,512,192]{2,1,0:T(8,128)(2,1)S(1)} %copy-done.10, bf16[8,4,1,128,128]{4,3,2,1,0:T(8,128)(2,1)} %bitcast.6.arrived_ref, bf16[6,96,384]{2,1,0:T(8,128)(2,1)S(1)} %get-tuple-element.19.refs_0_), custom_call_target="tpu_custom_call" | custom-call | flops 402653184 | bytes 1048576 | tf_op jit(solution)/shard_map/form_beams/pallas_call | solution.py:277
  148.9 19.6 %factor_slots.3 = (bf16[2,96,384]{2,1,0:T(8,128)(2,1)S(1)}, bf16[2,96,384]{2,1,0:T(8,128)(2,1)S(1)}, bf16[2,96,384]{2,1,0:T(8,128)(2,1)S(1)}, bf16[2,96,384]{2,1,0:T(8,128)(2,1)S(1)}) custom-call(s32[18]{0:T(128)S(1)} %pad_add_fusion.1.index_ref, s32[128,192]{1,0:T(8,128)S(1)} %copy.25.pivots_ref, bf16[4,1,384,128]{3,2,1,0:T(8,128)(2,1)S(1)} %form_beams.3.beams_ref), custom_call_target="tpu_custom_call" | custom-call | flops 113246208 | bytes 393216 | tf_op jit(solution)/shard_map/factor_slots/pallas_call | solution.py:508
  168.5 1.4 collective-permute-start.4
  169.9 1.3 collective-permute-start.5
  171.2 5.3 %place_rows.2.refs_4_ = f32[32,96,384]{2,1,0:T(8,128)} custom-call(s32[18]{0:T(128)S(1)} %pad_add_fusion.1.index_ref, bf16[6,96,384]{2,1,0:T(8,128)(2,1)S(1)} %get-tuple-element.19.refs_0_, bf16[6,96,384]{2,1,0:T(8,128)(2,1)S(1)} %collective-permute-done.7.refs_1_, bf16[6,96,384]{2,1,0:T(8,128)(2,1)S(1)} %collective-permute-done.8.refs_2_, ...), custom_call_target="tpu_custom_call" | custom-call | tf_op jit(solution)/shard_map/place_rows/pallas_call | solution.py:563
  176.5 1.3 collective-permute-done.5.refs_2_
  177.9 0.6 collective-permute-done.6.refs_3_
  178.5 2.2 %place_rows.3 = f32[32,96,384]{2,1,0:T(8,128)} custom-call(s32[18]{0:T(128)S(1)} %pad_add_fusion.1.index_ref, bf16[2,96,384]{2,1,0:T(8,128)(2,1)S(1)} %get-tuple-element.20.refs_0_, bf16[2,96,384]{2,1,0:T(8,128)(2,1)S(1)} %collective-permute-done.4.refs_1_, bf16[2,96,384]{2,1,0:T(8,128)(2,1)S(1)} %collective-permute-done.5.refs_2_, ...), custom_call_target="tpu_custom_call", output_to_operand_aliasing={{}: (5, {})} | custom-call | tf_op jit(solution)/shard_map/place_rows/pallas_call | solution.py:563
  (36 shorter events, 0.1 us)
Async XLA Ops:
  1.3 12.5 %collective-permute-start.3 = (bf16[2,16,64,128]{3,2,1,0:T(8,128)(2,1)S(1)}, bf16[2,16,64,128]{3,2,1,0:T(8,128)(2,1)}, u32[]{:S(2)}, u32[]{:S(2)}) collective-permute-start(bf16[2,16,64,128]{3,2,1,0:T(8,128)(2,1)S(1)} %rim_rows.7), channel_id=1, source_target_pairs={{1,0},{2,1},{3,2},{5,4},{6,5},{7,6},{9,8},{10,9},{11,10},{13,12},{... | collective-permute-start | bytes 1572872 | tf_op jit(solution)/shard_map/ppermute | solution.py:23
  4.5 13.8 %collective-permute-start = (bf16[2,16,64,128]{3,2,1,0:T(8,128)(2,1)S(1)}, bf16[2,16,64,128]{3,2,1,0:T(8,128)(2,1)}, u32[]{:S(2)}, u32[]{:S(2)}) collective-permute-start(bf16[2,16,64,128]{3,2,1,0:T(8,128)(2,1)S(1)} %rim_rows.4), channel_id=1, source_target_pairs={{1,0},{2,1},{3,2},{5,4},{6,5},{7,6},{9,8},{10,9},{11,10},{13,12},{... | collective-permute-start | bytes 1572872 | tf_op jit(solution)/shard_map/ppermute | solution.py:23
  7.8 5.3 %copy-start.14 = (s32[128,64]{0,1:T(8,128)S(1)}, s32[128,64]{0,1:T(8,128)}, u32[]{:S(2)}) copy-start(s32[128,64]{0,1:T(8,128)} %param.12) | copy-start | bytes 98308
  7.8 5.5 %copy-start.16 = (s32[8]{0:T(128)S(1)}, s32[8]{0:T(128)}, u32[]{:S(2)}) copy-start(s32[8]{0:T(128)} %param.11) | copy-start | bytes 100
  7.8 5.7 %copy-start.15 = (f32[2,64]{1,0:T(2,128)S(1)}, f32[2,64]{1,0:T(2,128)}, u32[]{:S(2)}) copy-start(f32[2,64]{1,0:T(2,128)} %param.8) | copy-start | bytes 1540
  7.8 6.0 %copy-start.11 = (bf16[256,768]{1,0:T(8,128)(2,1)S(1)}, bf16[256,768]{1,0:T(8,128)(2,1)}, u32[]{:S(2)}) copy-start(bf16[256,768]{1,0:T(8,128)(2,1)} %constant.33.clone.table_ref) | copy-start | bytes 1179652
  7.8 16.2 %collective-permute-start.1 = (bf16[2,16,64,128]{3,2,1,0:T(8,128)(2,1)S(1)}, bf16[2,16,64,128]{3,2,1,0:T(8,128)(2,1)}, u32[]{:S(2)}, u32[]{:S(2)}) collective-permute-start(bf16[2,16,64,128]{3,2,1,0:T(8,128)(2,1)S(1)} %rim_rows.5), channel_id=1, source_target_pairs={{1,0},{2,1},{3,2},{5,4},{6,5},{7,6},{9,8},{10,9},{11,10},{13,12},{... | collective-permute-start | bytes 1572872 | tf_op jit(solution)/shard_map/ppermute | solution.py:23
  11.2 18.3 %collective-permute-start.2 = (bf16[2,16,64,128]{3,2,1,0:T(8,128)(2,1)S(1)}, bf16[2,16,64,128]{3,2,1,0:T(8,128)(2,1)S(1)}, u32[]{:S(2)}, u32[]{:S(2)}) collective-permute-start(bf16[2,16,64,128]{3,2,1,0:T(8,128)(2,1)S(1)} %rim_rows.6), channel_id=1, source_target_pairs={{1,0},{2,1},{3,2},{5,4},{6,5},{7,6},{9,8},{10,9},{11,10},{13,12},{... | collective-permute-start | bytes 1572872 | tf_op jit(solution)/shard_map/ppermute | solution.py:23
  17.1 15.7 %copy-start = (bf16[128,32,128]{2,1,0:T(8,128)(2,1)}, bf16[128,32,128]{2,1,0:T(8,128)(2,1)S(1)}, u32[]{:S(2)}) copy-start(bf16[128,32,128]{2,1,0:T(8,128)(2,1)S(1)} %form_spectrum.7.refs_3_) | copy-start | bytes 3145732
  21.7 11.1 %copy-start.2 = (bf16[128,32,128]{2,1,0:T(8,128)(2,1)}, bf16[128,32,128]{2,1,0:T(8,128)(2,1)S(1)}, u32[]{:S(2)}) copy-start(bf16[128,32,128]{2,1,0:T(8,128)(2,1)S(1)} %form_spectrum.4.refs_0_) | copy-start | bytes 3145732
  27.3 5.5 %copy-start.4 = (bf16[128,32,128]{2,1,0:T(8,128)(2,1)}, bf16[128,32,128]{2,1,0:T(8,128)(2,1)S(1)}, u32[]{:S(2)}) copy-start(bf16[128,32,128]{2,1,0:T(8,128)(2,1)S(1)} %form_spectrum.5.refs_1_) | copy-start | bytes 3145732
  32.8 4.1 %copy-start.6 = (bf16[128,32,128]{2,1,0:T(8,128)(2,1)}, bf16[128,32,128]{2,1,0:T(8,128)(2,1)S(1)}, u32[]{:S(2)}) copy-start(bf16[128,32,128]{2,1,0:T(8,128)(2,1)S(1)} %form_spectrum.6.refs_2_) | copy-start | bytes 3145732
  37.0 75.6 %all-to-all-start.1 = ((bf16[32,3,128,128]{3,2,1,0:T(8,128)(2,1)}), bf16[32,3,128,128]{3,2,1,0:T(8,128)(2,1)S(1)}, u32[]{:S(2)}, u32[]{:S(2)}) async-start(bf16[32,3,128,128]{3,2,1,0:T(8,128)(2,1)} %bitcast.13), calls=%async_computation.1 | async-start | bytes 6291456 | tf_op jit(solution)/shard_map/all_to_all | solution.py:624
  41.8 75.5 %copy-start.13 = (s32[128,192]{0,1:T(8,128)S(1)}, s32[128,192]{0,1:T(8,128)}, u32[]{:S(2)}) copy-start(s32[128,192]{0,1:T(8,128)} %param.10) | copy-start | bytes 294916
  43.8 1.2 copy-start.1
  45.1 1.2 copy-start.3
  46.3 1.2 copy-start.5
  47.5 1.2 copy-start.7
  48.7 1.0 copy-start.8
  51.6 1.0 copy-start.12
  112.6 33.2 %all-to-all-start = ((bf16[32,1,128,128]{3,2,1,0:T(8,128)(2,1)}), bf16[32,1,128,128]{3,2,1,0:T(8,128)(2,1)}, u32[]{:S(2)}, u32[]{:S(2)}) async-start(bf16[32,1,128,128]{3,2,1,0:T(8,128)(2,1)} %bitcast.12), calls=%async_computation | async-start | bytes 2097152 | tf_op jit(solution)/shard_map/all_to_all | solution.py:624
  117.4 1.0 copy-start.9
  143.6 27.6 %collective-permute-start.7 = (bf16[6,96,384]{2,1,0:T(8,128)(2,1)S(1)}, bf16[6,96,384]{2,1,0:T(8,128)(2,1)S(1)}, u32[]{:S(2)}, u32[]{:S(2)}) collective-permute-start(bf16[6,96,384]{2,1,0:T(8,128)(2,1)S(1)} %get-tuple-element.24), channel_id=1, source_target_pairs={{0,1},{1,2},{2,3},{3,0},{4,5},{5,6},{6,7},{7,4},{8,9},{9,10},{10,1... | collective-permute-start | bytes 1327112 | tf_op jit(solution)/shard_map/ppermute | solution.py:298
  145.2 26.0 %collective-permute-start.8 = (bf16[6,96,384]{2,1,0:T(8,128)(2,1)S(1)}, bf16[6,96,384]{2,1,0:T(8,128)(2,1)S(1)}, u32[]{:S(2)}, u32[]{:S(2)}) collective-permute-start(bf16[6,96,384]{2,1,0:T(8,128)(2,1)S(1)} %get-tuple-element.25), channel_id=1, source_target_pairs={{0,2},{1,3},{2,0},{3,1},{4,6},{5,7},{6,4},{7,5},{8,10},{9,11},{10,... | collective-permute-start | bytes 1327112 | tf_op jit(solution)/shard_map/ppermute | solution.py:298
  145.4 25.8 %collective-permute-start.9 = (bf16[6,96,384]{2,1,0:T(8,128)(2,1)S(1)}, bf16[6,96,384]{2,1,0:T(8,128)(2,1)S(1)}, u32[]{:S(2)}, u32[]{:S(2)}) collective-permute-start(bf16[6,96,384]{2,1,0:T(8,128)(2,1)S(1)} %get-tuple-element.26), channel_id=1, source_target_pairs={{0,3},{1,0},{2,1},{3,2},{4,7},{5,4},{6,5},{7,6},{8,11},{9,8},{10,9... | collective-permute-start | bytes 1327112 | tf_op jit(solution)/shard_map/ppermute | solution.py:298
  145.8 1.0 copy-start.10
  168.5 8.0 %collective-permute-start.4 = (bf16[2,96,384]{2,1,0:T(8,128)(2,1)S(1)}, bf16[2,96,384]{2,1,0:T(8,128)(2,1)S(1)}, u32[]{:S(2)}, u32[]{:S(2)}) collective-permute-start(bf16[2,96,384]{2,1,0:T(8,128)(2,1)S(1)} %get-tuple-element.21), channel_id=1, source_target_pairs={{0,1},{1,2},{2,3},{3,0},{4,5},{5,6},{6,7},{7,4},{8,9},{9,10},{10,1... | collective-permute-start | bytes 442376 | tf_op jit(solution)/shard_map/ppermute | solution.py:298
  169.9 7.9 %collective-permute-start.5 = (bf16[2,96,384]{2,1,0:T(8,128)(2,1)S(1)}, bf16[2,96,384]{2,1,0:T(8,128)(2,1)S(1)}, u32[]{:S(2)}, u32[]{:S(2)}) collective-permute-start(bf16[2,96,384]{2,1,0:T(8,128)(2,1)S(1)} %get-tuple-element.22), channel_id=1, source_target_pairs={{0,2},{1,3},{2,0},{3,1},{4,6},{5,7},{6,4},{7,5},{8,10},{9,11},{10,... | collective-permute-start | bytes 442376 | tf_op jit(solution)/shard_map/ppermute | solution.py:298
  171.2 7.3 %collective-permute-start.6 = (bf16[2,96,384]{2,1,0:T(8,128)(2,1)S(1)}, bf16[2,96,384]{2,1,0:T(8,128)(2,1)S(1)}, u32[]{:S(2)}, u32[]{:S(2)}) collective-permute-start(bf16[2,96,384]{2,1,0:T(8,128)(2,1)S(1)} %get-tuple-element.23), channel_id=1, source_target_pairs={{0,3},{1,0},{2,1},{3,2},{4,7},{5,4},{6,5},{7,6},{8,11},{9,8},{10,9... | collective-permute-start | bytes 442376 | tf_op jit(solution)/shard_map/ppermute | solution.py:298

commit v6 on v5

--- a/solution.py
+++ b/solution.py
@@ -15,6 +15,7 @@
 BF16 = jnp.bfloat16
 F32 = jnp.float32
 PARAMS = pltpu.CompilerParams(vmem_limit_bytes=48 * 1024 * 1024)
+SMALL_PARAMS = pltpu.CompilerParams(vmem_limit_bytes=24 * 1024 * 1024)
 
 
 def shifted(array, axis, by):
@@ -280,7 +281,7 @@
         in_specs=[pl.BlockSpec(memory_space=pltpu.VMEM)] * 2
         + [pl.BlockSpec(memory_space=pl.ANY)] * len(earlier),
         out_specs=pl.BlockSpec(memory_space=pltpu.VMEM),
-        compiler_params=PARAMS,
+        compiler_params=SMALL_PARAMS,
         cost_estimate=pl.CostEstimate(
             flops=4 * arrived.size * weights.shape[2],
             bytes_accessed=arrived.size * 2,
@@ -522,7 +523,7 @@
         + [pltpu.VMEM((order, order), F32) for _ in range(slots)]
         + [pltpu.VMEM((LANES, 3 * PANEL), F32) for _ in range(slots)]
         + [pltpu.VMEM((3 * PANEL, order), BF16) for _ in range(slots)],
-        compiler_params=PARAMS,
+        compiler_params=SMALL_PARAMS,
         cost_estimate=pl.CostEstimate(
             flops=slots * order**3,
             bytes_accessed=beams.size * 2,
@@ -571,7 +572,7 @@
             out_specs=pl.BlockSpec((slots,) + arrays[0].shape[1:], out_index),
         ),
         input_output_aliases={1 + ranges: 0} if earlier else {},
-        compiler_params=PARAMS,
+        compiler_params=SMALL_PARAMS,
         name="place_rows",
     )(index, *arrays, *earlier)
 

time: 182 us -> 182 us (level)
  no operation moved by 1% of the time
where the time goes in v6:
time: 182 us; the launch traced here: 181 us
  Pallas kernels  78.8 us (43%)
  waiting for transfers between devices  67.7 us (37%)
  starting transfers between devices  22.2 us (12%)
  local copies, waits for them, and re-layouts  11.3 us (6%)
    all_to_all x2, waiting for transfers between devices, local(): lax.all_to_all(array.reshape(owners * ranges, -1, *array.shape[2:]), axes...  60.1 us
    pallas_call x2, Pallas kernels, factor_slots(): pl.pallas_call(functools.partial(factor_kernel, first=first, share_slots=...  43.3 us
    pallas_call x4, Pallas kernels, form_spectrum(): pl.pallas_call(spectrum_kernel, out_shape=jax.ShapeDtypeStruct((bins, hei...  13.3 us
    unnamed x37, local copies, waits for them, and re-layouts  11.3 us
    all_to_all x2, starting transfers between devices, local(): lax.all_to_all(array.reshape(owners * ranges, -1, *array.shape[2:]), axes...  9.4 us
    ppermute x4, starting transfers between devices, shifted(): return lax.ppermute(array, axis, pairs)  7.86 us
    pallas_call x2, Pallas kernels, place_rows(): pl.pallas_call(functools.partial(place_kernel, first=first, share_slots=s...  7.5 us
    pallas_call x2, Pallas kernels, select_gates(): pl.pallas_call(functools.partial(select_kernel, chunks=len(spectra), owne...  5.95 us
  transfers between devices with their start and end apart: 12, of which 6 were waited for; matrix products, arithmetic and copies ran while one was open for 1% of the time, Pallas kernels for 38%

profile of v6, /device:TPU:1, one launch (start us, length us, event | category | flops | bytes accessed | tf_op | source)
XLA Modules:
  0.0 180.7 jit_solution(12622648388445742875)
XLA Ops:
  0.0 1.3 rim_rows.7
  1.3 2.0 %collective-permute-start.3 = (bf16[2,16,64,128]{3,2,1,0:T(8,128)(2,1)S(1)}, bf16[2,16,64,128]{3,2,1,0:T(8,128)(2,1)}, u32[]{:S(2)}, u32[]{:S(2)}) collective-permute-start(bf16[2,16,64,128]{3,2,1,0:T(8,128)(2,1)S(1)} %rim_rows.7), channel_id=1, source_target_pairs={{1,0},{2,1},{3,2},{5,4},{6,5},{7,6},{9,8},{10,9},{11,10},{13,12},{... | collective-permute-start | bytes 1572872 | tf_op jit(solution)/shard_map/ppermute | solution.py:24
  3.3 1.3 rim_rows.4
  4.5 1.9 %collective-permute-start = (bf16[2,16,64,128]{3,2,1,0:T(8,128)(2,1)S(1)}, bf16[2,16,64,128]{3,2,1,0:T(8,128)(2,1)}, u32[]{:S(2)}, u32[]{:S(2)}) collective-permute-start(bf16[2,16,64,128]{3,2,1,0:T(8,128)(2,1)S(1)} %rim_rows.4), channel_id=1, source_target_pairs={{1,0},{2,1},{3,2},{5,4},{6,5},{7,6},{9,8},{10,9},{11,10},{13,12},{... | collective-permute-start | bytes 1572872 | tf_op jit(solution)/shard_map/ppermute | solution.py:24
  6.5 1.3 rim_rows.5
  7.8 2.1 %collective-permute-start.1 = (bf16[2,16,64,128]{3,2,1,0:T(8,128)(2,1)S(1)}, bf16[2,16,64,128]{3,2,1,0:T(8,128)(2,1)}, u32[]{:S(2)}, u32[]{:S(2)}) collective-permute-start(bf16[2,16,64,128]{3,2,1,0:T(8,128)(2,1)S(1)} %rim_rows.5), channel_id=1, source_target_pairs={{1,0},{2,1},{3,2},{5,4},{6,5},{7,6},{9,8},{10,9},{11,10},{13,12},{... | collective-permute-start | bytes 1572872 | tf_op jit(solution)/shard_map/ppermute | solution.py:24
  9.9 1.3 rim_rows.6
  11.2 1.9 %collective-permute-start.2 = (bf16[2,16,64,128]{3,2,1,0:T(8,128)(2,1)S(1)}, bf16[2,16,64,128]{3,2,1,0:T(8,128)(2,1)S(1)}, u32[]{:S(2)}, u32[]{:S(2)}) collective-permute-start(bf16[2,16,64,128]{3,2,1,0:T(8,128)(2,1)S(1)} %rim_rows.6), channel_id=1, source_target_pairs={{1,0},{2,1},{3,2},{5,4},{6,5},{7,6},{9,8},{10,9},{11,10},{13,12},{... | collective-permute-start | bytes 1572872 | tf_op jit(solution)/shard_map/ppermute | solution.py:24
  13.1 0.1 copy.17
  13.3 0.2 reduce-window.9
  13.5 0.1 pad_add_fusion.1.index_ref
  13.5 0.1 filter_rows.1.rows_ref
  13.7 0.1 pad_add_fusion.gates_ref
  13.8 3.4 %form_spectrum.7.refs_3_ = bf16[128,32,128]{2,1,0:T(8,128)(2,1)S(1)} custom-call(bf16[256,512]{1,0:T(8,128)(2,1)S(1)} %filter_rows.1.rows_ref, bf16[256,768]{1,0:T(8,128)(2,1)S(1)} %copy-done.11, f32[2,64,128,128]{3,2,1,0:T(8,128)} %own_ref.7, bf16[2,16,64,128]{3,2,1,0:T(8,128)(2,1)} %collective-permute-done.3.next_ref), custom_call_target="tpu_custom_call" | custom-call | flops 1342177280 | bytes 2097152 | tf_op jit(solution)/shard_map/form_spectrum/pallas_call | solution.py:144
  17.1 1.2 collective-permute-done.next_ref
  18.4 3.3 %form_spectrum.4.refs_0_ = bf16[128,32,128]{2,1,0:T(8,128)(2,1)S(1)} custom-call(bf16[256,512]{1,0:T(8,128)(2,1)S(1)} %filter_rows.1.rows_ref, bf16[256,768]{1,0:T(8,128)(2,1)S(1)} %copy-done.11, f32[2,64,128,128]{3,2,1,0:T(8,128)} %own_ref.7, bf16[2,16,64,128]{3,2,1,0:T(8,128)(2,1)} %collective-permute-done.next_ref), custom_call_target="tpu_custom_call" | custom-call | flops 1342177280 | bytes 2097152 | tf_op jit(solution)/shard_map/form_spectrum/pallas_call | solution.py:144
  21.7 2.3 %collective-permute-done.1.next_ref = bf16[2,16,64,128]{3,2,1,0:T(8,128)(2,1)} collective-permute-done((bf16[2,16,64,128]{3,2,1,0:T(8,128)(2,1)S(1)}, bf16[2,16,64,128]{3,2,1,0:T(8,128)(2,1)}, u32[]{:S(2)}, u32[]{:S(2)}) %collective-permute-start.1) | collective-permute-done | bytes 524320 | tf_op jit(solution)/shard_map/ppermute | solution.py:24
  24.0 3.3 %form_spectrum.5.refs_1_ = bf16[128,32,128]{2,1,0:T(8,128)(2,1)S(1)} custom-call(bf16[256,512]{1,0:T(8,128)(2,1)S(1)} %filter_rows.1.rows_ref, bf16[256,768]{1,0:T(8,128)(2,1)S(1)} %copy-done.11, f32[2,64,128,128]{3,2,1,0:T(8,128)} %own_ref.7, bf16[2,16,64,128]{3,2,1,0:T(8,128)(2,1)} %collective-permute-done.1.next_ref), custom_call_target="tpu_custom_call" | custom-call | flops 1342177280 | bytes 2097152 | tf_op jit(solution)/shard_map/form_spectrum/pallas_call | solution.py:144
  27.3 2.2 %collective-permute-done.2.next_ref = bf16[2,16,64,128]{3,2,1,0:T(8,128)(2,1)S(1)} collective-permute-done((bf16[2,16,64,128]{3,2,1,0:T(8,128)(2,1)S(1)}, bf16[2,16,64,128]{3,2,1,0:T(8,128)(2,1)S(1)}, u32[]{:S(2)}, u32[]{:S(2)}) %collective-permute-start.2) | collective-permute-done | bytes 524320 | tf_op jit(solution)/shard_map/ppermute | solution.py:24
  29.5 3.3 %form_spectrum.6.refs_2_ = bf16[128,32,128]{2,1,0:T(8,128)(2,1)S(1)} custom-call(bf16[256,512]{1,0:T(8,128)(2,1)S(1)} %filter_rows.1.rows_ref, bf16[256,768]{1,0:T(8,128)(2,1)S(1)} %copy-done.11, f32[2,64,128,128]{3,2,1,0:T(8,128)} %own_ref.7, bf16[2,16,64,128]{3,2,1,0:T(8,128)(2,1)S(1)} %collective-permute-done.2.next_ref), custom_call_target="tpu_custom_call" | custom-call | flops 1342177280 | bytes 2097152 | tf_op jit(solution)/shard_map/form_spectrum/pallas_call | solution.py:144
  32.8 4.1 %select_gates.3 = (bf16[8,12,128,128]{3,2,1,0:T(8,128)(2,1)}, s32[8,128]{1,0:T(8,128)}) custom-call(s32[18]{0:T(128)S(1)} %pad_add_fusion.1.index_ref, s32[128,128]{1,0:T(8,128)S(1)} %pad_add_fusion.gates_ref, bf16[128,32,128]{2,1,0:T(8,128)(2,1)S(1)} %form_spectrum.4.refs_0_, bf16[128,32,128]{2,1,0:T(8,128)(2,1)S(1)} %form_spectrum.5.refs_1_, ...), custom_call_target="tpu_custom_call" | custom-call | flops 805306368 | bytes 3145728 | tf_op jit(solution)/shard_map/select_gates/pallas_call | solution.py:214
  37.0 4.8 %all-to-all-start.1 = ((bf16[32,3,128,128]{3,2,1,0:T(8,128)(2,1)}), bf16[32,3,128,128]{3,2,1,0:T(8,128)(2,1)S(1)}, u32[]{:S(2)}, u32[]{:S(2)}) async-start(bf16[32,3,128,128]{3,2,1,0:T(8,128)(2,1)} %bitcast.13), calls=%async_computation.1 | async-start | bytes 6291456 | tf_op jit(solution)/shard_map/all_to_all | solution.py:625
  41.8 2.0 %copy.24.refs_4_.weights_ref = bf16[2,512,192]{2,1,0:T(8,128)(2,1)} copy(bf16[2,512,192]{1,2,0:T(8,128)(2,1)} %param.9) | data formatting | bytes 786432 | tf_op args[2]
  43.8 1.2 copy-done.1
  45.1 1.2 copy-done.3
  46.3 1.2 copy-done.5
  47.5 1.2 copy-done.7
  48.7 1.0 copy-done.8
  49.8 1.8 %select_gates.2 = (bf16[8,4,128,128]{3,2,1,0:T(8,128)(2,1)S(1)}, s32[8,128]{1,0:T(8,128)S(1)}) custom-call(s32[18]{0:T(128)S(1)} %pad_add_fusion.1.index_ref, s32[128,128]{1,0:T(8,128)S(1)} %pad_add_fusion.gates_ref, bf16[128,32,128]{2,1,0:T(8,128)(2,1)S(1)} %copy-done.3, bf16[128,32,128]{2,1,0:T(8,128)(2,1)S(1)} %copy-done.5, ...), custom_call_target="tpu_custom_call" | custom-call | flops 268435456 | bytes 1048576 | tf_op jit(solution)/shard_map/select_gates/pallas_call | solution.py:214
  51.6 1.0 copy-done.12
  52.6 60.0 %all-to-all-done.1 = bf16[32,3,128,128]{3,2,1,0:T(8,128)(2,1)S(1)} async-done(((bf16[32,3,128,128]{3,2,1,0:T(8,128)(2,1)}), bf16[32,3,128,128]{3,2,1,0:T(8,128)(2,1)S(1)}, u32[]{:S(2)}, u32[]{:S(2)}) %all-to-all-start.1) | async-done | bytes 3145760 | tf_op jit(solution)/shard_map/all_to_all | solution.py:625
  112.6 4.6 %all-to-all-start = ((bf16[32,1,128,128]{3,2,1,0:T(8,128)(2,1)}), bf16[32,1,128,128]{3,2,1,0:T(8,128)(2,1)}, u32[]{:S(2)}, u32[]{:S(2)}) async-start(bf16[32,1,128,128]{3,2,1,0:T(8,128)(2,1)} %bitcast.12), calls=%async_computation | async-start | bytes 2097152 | tf_op jit(solution)/shard_map/all_to_all | solution.py:625
  117.2 0.1 copy.25.pivots_ref
  117.4 1.0 copy-done.9
  118.4 1.4 form_beams.2.beams_ref
  119.8 23.7 %factor_slots.2 = (bf16[6,96,384]{2,1,0:T(8,128)(2,1)S(1)}, bf16[6,96,384]{2,1,0:T(8,128)(2,1)S(1)}, bf16[6,96,384]{2,1,0:T(8,128)(2,1)S(1)}, bf16[6,96,384]{2,1,0:T(8,128)(2,1)S(1)}) custom-call(s32[18]{0:T(128)S(1)} %pad_add_fusion.1.index_ref, s32[128,192]{1,0:T(8,128)S(1)} %copy.25.pivots_ref, bf16[4,3,384,128]{3,2,1,0:T(8,128)(2,1)S(1)} %form_beams.2.beams_ref), custom_call_target="tpu_custom_call" | custom-call | flops 339738624 | bytes 1179648 | tf_op jit(solution)/shard_map/factor_slots/pallas_call | solution.py:509
  143.6 1.7 collective-permute-start.7
  145.2 0.2 collective-permute-start.8
  145.4 0.3 collective-permute-start.9
  145.8 1.0 copy-done.10
  146.8 2.1 %form_beams.3.beams_ref = bf16[4,1,384,128]{3,2,1,0:T(8,128)(2,1)S(1)} custom-call(bf16[2,512,192]{2,1,0:T(8,128)(2,1)S(1)} %copy-done.10, bf16[8,4,1,128,128]{4,3,2,1,0:T(8,128)(2,1)} %bitcast.6.arrived_ref, bf16[6,96,384]{2,1,0:T(8,128)(2,1)S(1)} %get-tuple-element.19.refs_0_), custom_call_target="tpu_custom_call" | custom-call | flops 402653184 | bytes 1048576 | tf_op jit(solution)/shard_map/form_beams/pallas_call | solution.py:278
  148.9 19.6 %factor_slots.3 = (bf16[2,96,384]{2,1,0:T(8,128)(2,1)S(1)}, bf16[2,96,384]{2,1,0:T(8,128)(2,1)S(1)}, bf16[2,96,384]{2,1,0:T(8,128)(2,1)S(1)}, bf16[2,96,384]{2,1,0:T(8,128)(2,1)S(1)}) custom-call(s32[18]{0:T(128)S(1)} %pad_add_fusion.1.index_ref, s32[128,192]{1,0:T(8,128)S(1)} %copy.25.pivots_ref, bf16[4,1,384,128]{3,2,1,0:T(8,128)(2,1)S(1)} %form_beams.3.beams_ref), custom_call_target="tpu_custom_call" | custom-call | flops 113246208 | bytes 393216 | tf_op jit(solution)/shard_map/factor_slots/pallas_call | solution.py:509
  168.5 1.4 collective-permute-start.4
  169.9 1.3 collective-permute-start.5
  171.2 5.3 %place_rows.2.refs_4_ = f32[32,96,384]{2,1,0:T(8,128)} custom-call(s32[18]{0:T(128)S(1)} %pad_add_fusion.1.index_ref, bf16[6,96,384]{2,1,0:T(8,128)(2,1)S(1)} %get-tuple-element.19.refs_0_, bf16[6,96,384]{2,1,0:T(8,128)(2,1)S(1)} %collective-permute-done.7.refs_1_, bf16[6,96,384]{2,1,0:T(8,128)(2,1)S(1)} %collective-permute-done.8.refs_2_, ...), custom_call_target="tpu_custom_call" | custom-call | tf_op jit(solution)/shard_map/place_rows/pallas_call | solution.py:564
  176.5 1.3 collective-permute-done.5.refs_2_
  177.9 0.6 collective-permute-done.6.refs_3_
  178.5 2.2 %place_rows.3 = f32[32,96,384]{2,1,0:T(8,128)} custom-call(s32[18]{0:T(128)S(1)} %pad_add_fusion.1.index_ref, bf16[2,96,384]{2,1,0:T(8,128)(2,1)S(1)} %get-tuple-element.20.refs_0_, bf16[2,96,384]{2,1,0:T(8,128)(2,1)S(1)} %collective-permute-done.4.refs_1_, bf16[2,96,384]{2,1,0:T(8,128)(2,1)S(1)} %collective-permute-done.5.refs_2_, ...), custom_call_target="tpu_custom_call", output_to_operand_aliasing={{}: (5, {})} | custom-call | tf_op jit(solution)/shard_map/place_rows/pallas_call | solution.py:564
  (36 shorter events, 0.1 us)
Async XLA Ops:
  1.3 12.5 %collective-permute-start.3 = (bf16[2,16,64,128]{3,2,1,0:T(8,128)(2,1)S(1)}, bf16[2,16,64,128]{3,2,1,0:T(8,128)(2,1)}, u32[]{:S(2)}, u32[]{:S(2)}) collective-permute-start(bf16[2,16,64,128]{3,2,1,0:T(8,128)(2,1)S(1)} %rim_rows.7), channel_id=1, source_target_pairs={{1,0},{2,1},{3,2},{5,4},{6,5},{7,6},{9,8},{10,9},{11,10},{13,12},{... | collective-permute-start | bytes 1572872 | tf_op jit(solution)/shard_map/ppermute | solution.py:24
  4.5 13.8 %collective-permute-start = (bf16[2,16,64,128]{3,2,1,0:T(8,128)(2,1)S(1)}, bf16[2,16,64,128]{3,2,1,0:T(8,128)(2,1)}, u32[]{:S(2)}, u32[]{:S(2)}) collective-permute-start(bf16[2,16,64,128]{3,2,1,0:T(8,128)(2,1)S(1)} %rim_rows.4), channel_id=1, source_target_pairs={{1,0},{2,1},{3,2},{5,4},{6,5},{7,6},{9,8},{10,9},{11,10},{13,12},{... | collective-permute-start | bytes 1572872 | tf_op jit(solution)/shard_map/ppermute | solution.py:24
  7.8 5.3 %copy-start.14 = (s32[128,64]{0,1:T(8,128)S(1)}, s32[128,64]{0,1:T(8,128)}, u32[]{:S(2)}) copy-start(s32[128,64]{0,1:T(8,128)} %param.12) | copy-start | bytes 98308
  7.8 5.5 %copy-start.16 = (s32[8]{0:T(128)S(1)}, s32[8]{0:T(128)}, u32[]{:S(2)}) copy-start(s32[8]{0:T(128)} %param.11) | copy-start | bytes 100
  7.8 5.7 %copy-start.15 = (f32[2,64]{1,0:T(2,128)S(1)}, f32[2,64]{1,0:T(2,128)}, u32[]{:S(2)}) copy-start(f32[2,64]{1,0:T(2,128)} %param.8) | copy-start | bytes 1540
  7.8 6.0 %copy-start.11 = (bf16[256,768]{1,0:T(8,128)(2,1)S(1)}, bf16[256,768]{1,0:T(8,128)(2,1)}, u32[]{:S(2)}) copy-start(bf16[256,768]{1,0:T(8,128)(2,1)} %constant.33.clone.table_ref) | copy-start | bytes 1179652
  7.8 16.2 %collective-permute-start.1 = (bf16[2,16,64,128]{3,2,1,0:T(8,128)(2,1)S(1)}, bf16[2,16,64,128]{3,2,1,0:T(8,128)(2,1)}, u32[]{:S(2)}, u32[]{:S(2)}) collective-permute-start(bf16[2,16,64,128]{3,2,1,0:T(8,128)(2,1)S(1)} %rim_rows.5), channel_id=1, source_target_pairs={{1,0},{2,1},{3,2},{5,4},{6,5},{7,6},{9,8},{10,9},{11,10},{13,12},{... | collective-permute-start | bytes 1572872 | tf_op jit(solution)/shard_map/ppermute | solution.py:24
  11.2 18.3 %collective-permute-start.2 = (bf16[2,16,64,128]{3,2,1,0:T(8,128)(2,1)S(1)}, bf16[2,16,64,128]{3,2,1,0:T(8,128)(2,1)S(1)}, u32[]{:S(2)}, u32[]{:S(2)}) collective-permute-start(bf16[2,16,64,128]{3,2,1,0:T(8,128)(2,1)S(1)} %rim_rows.6), channel_id=1, source_target_pairs={{1,0},{2,1},{3,2},{5,4},{6,5},{7,6},{9,8},{10,9},{11,10},{13,12},{... | collective-permute-start | bytes 1572872 | tf_op jit(solution)/shard_map/ppermute | solution.py:24
  17.1 15.7 %copy-start = (bf16[128,32,128]{2,1,0:T(8,128)(2,1)}, bf16[128,32,128]{2,1,0:T(8,128)(2,1)S(1)}, u32[]{:S(2)}) copy-start(bf16[128,32,128]{2,1,0:T(8,128)(2,1)S(1)} %form_spectrum.7.refs_3_) | copy-start | bytes 3145732
  21.7 11.1 %copy-start.2 = (bf16[128,32,128]{2,1,0:T(8,128)(2,1)}, bf16[128,32,128]{2,1,0:T(8,128)(2,1)S(1)}, u32[]{:S(2)}) copy-start(bf16[128,32,128]{2,1,0:T(8,128)(2,1)S(1)} %form_spectrum.4.refs_0_) | copy-start | bytes 3145732
  27.3 5.5 %copy-start.4 = (bf16[128,32,128]{2,1,0:T(8,128)(2,1)}, bf16[128,32,128]{2,1,0:T(8,128)(2,1)S(1)}, u32[]{:S(2)}) copy-start(bf16[128,32,128]{2,1,0:T(8,128)(2,1)S(1)} %form_spectrum.5.refs_1_) | copy-start | bytes 3145732
  32.8 4.1 %copy-start.6 = (bf16[128,32,128]{2,1,0:T(8,128)(2,1)}, bf16[128,32,128]{2,1,0:T(8,128)(2,1)S(1)}, u32[]{:S(2)}) copy-start(bf16[128,32,128]{2,1,0:T(8,128)(2,1)S(1)} %form_spectrum.6.refs_2_) | copy-start | bytes 3145732
  37.0 75.6 %all-to-all-start.1 = ((bf16[32,3,128,128]{3,2,1,0:T(8,128)(2,1)}), bf16[32,3,128,128]{3,2,1,0:T(8,128)(2,1)S(1)}, u32[]{:S(2)}, u32[]{:S(2)}) async-start(bf16[32,3,128,128]{3,2,1,0:T(8,128)(2,1)} %bitcast.13), calls=%async_computation.1 | async-start | bytes 6291456 | tf_op jit(solution)/shard_map/all_to_all | solution.py:625
  41.8 75.5 %copy-start.13 = (s32[128,192]{0,1:T(8,128)S(1)}, s32[128,192]{0,1:T(8,128)}, u32[]{:S(2)}) copy-start(s32[128,192]{0,1:T(8,128)} %param.10) | copy-start | bytes 294916
  43.8 1.2 copy-start.1
  45.1 1.2 copy-start.3
  46.3 1.2 copy-start.5
  47.5 1.2 copy-start.7
  48.7 1.0 copy-start.8
  51.6 1.0 copy-start.12
  112.6 33.2 %all-to-all-start = ((bf16[32,1,128,128]{3,2,1,0:T(8,128)(2,1)}), bf16[32,1,128,128]{3,2,1,0:T(8,128)(2,1)}, u32[]{:S(2)}, u32[]{:S(2)}) async-start(bf16[32,1,128,128]{3,2,1,0:T(8,128)(2,1)} %bitcast.12), calls=%async_computation | async-start | bytes 2097152 | tf_op jit(solution)/shard_map/all_to_all | solution.py:625
  117.4 1.0 copy-start.9
  143.6 27.7 %collective-permute-start.7 = (bf16[6,96,384]{2,1,0:T(8,128)(2,1)S(1)}, bf16[6,96,384]{2,1,0:T(8,128)(2,1)S(1)}, u32[]{:S(2)}, u32[]{:S(2)}) collective-permute-start(bf16[6,96,384]{2,1,0:T(8,128)(2,1)S(1)} %get-tuple-element.24), channel_id=1, source_target_pairs={{0,1},{1,2},{2,3},{3,0},{4,5},{5,6},{6,7},{7,4},{8,9},{9,10},{10,1... | collective-permute-start | bytes 1327112 | tf_op jit(solution)/shard_map/ppermute | solution.py:299
  145.2 26.0 %collective-permute-start.8 = (bf16[6,96,384]{2,1,0:T(8,128)(2,1)S(1)}, bf16[6,96,384]{2,1,0:T(8,128)(2,1)S(1)}, u32[]{:S(2)}, u32[]{:S(2)}) collective-permute-start(bf16[6,96,384]{2,1,0:T(8,128)(2,1)S(1)} %get-tuple-element.25), channel_id=1, source_target_pairs={{0,2},{1,3},{2,0},{3,1},{4,6},{5,7},{6,4},{7,5},{8,10},{9,11},{10,... | collective-permute-start | bytes 1327112 | tf_op jit(solution)/shard_map/ppermute | solution.py:299
  145.4 25.8 %collective-permute-start.9 = (bf16[6,96,384]{2,1,0:T(8,128)(2,1)S(1)}, bf16[6,96,384]{2,1,0:T(8,128)(2,1)S(1)}, u32[]{:S(2)}, u32[]{:S(2)}) collective-permute-start(bf16[6,96,384]{2,1,0:T(8,128)(2,1)S(1)} %get-tuple-element.26), channel_id=1, source_target_pairs={{0,3},{1,0},{2,1},{3,2},{4,7},{5,4},{6,5},{7,6},{8,11},{9,8},{10,9... | collective-permute-start | bytes 1327112 | tf_op jit(solution)/shard_map/ppermute | solution.py:299
  145.8 1.0 copy-start.10
  168.5 8.0 %collective-permute-start.4 = (bf16[2,96,384]{2,1,0:T(8,128)(2,1)S(1)}, bf16[2,96,384]{2,1,0:T(8,128)(2,1)S(1)}, u32[]{:S(2)}, u32[]{:S(2)}) collective-permute-start(bf16[2,96,384]{2,1,0:T(8,128)(2,1)S(1)} %get-tuple-element.21), channel_id=1, source_target_pairs={{0,1},{1,2},{2,3},{3,0},{4,5},{5,6},{6,7},{7,4},{8,9},{9,10},{10,1... | collective-permute-start | bytes 442376 | tf_op jit(solution)/shard_map/ppermute | solution.py:299
  169.9 7.9 %collective-permute-start.5 = (bf16[2,96,384]{2,1,0:T(8,128)(2,1)S(1)}, bf16[2,96,384]{2,1,0:T(8,128)(2,1)S(1)}, u32[]{:S(2)}, u32[]{:S(2)}) collective-permute-start(bf16[2,96,384]{2,1,0:T(8,128)(2,1)S(1)} %get-tuple-element.22), channel_id=1, source_target_pairs={{0,2},{1,3},{2,0},{3,1},{4,6},{5,7},{6,4},{7,5},{8,10},{9,11},{10,... | collective-permute-start | bytes 442376 | tf_op jit(solution)/shard_map/ppermute | solution.py:299
  171.2 7.3 %collective-permute-start.6 = (bf16[2,96,384]{2,1,0:T(8,128)(2,1)S(1)}, bf16[2,96,384]{2,1,0:T(8,128)(2,1)S(1)}, u32[]{:S(2)}, u32[]{:S(2)}) collective-permute-start(bf16[2,96,384]{2,1,0:T(8,128)(2,1)S(1)} %get-tuple-element.23), channel_id=1, source_target_pairs={{0,3},{1,0},{2,1},{3,2},{4,7},{5,4},{6,5},{7,6},{8,11},{9,8},{10,9... | collective-permute-start | bytes 442376 | tf_op jit(solution)/shard_map/ppermute | solution.py:299

commit v7 on v6

--- a/solution.py
+++ b/solution.py
@@ -210,7 +210,7 @@
     gate_rows = spectra[0].shape[2]
     groups = ranges * count // pack
     width = gates.shape[1]
-    some = math.gcd(owners, 2)
+    some = math.gcd(owners, 4)
     return pl.pallas_call(
         functools.partial(
             select_kernel,

time: 182 us -> 181 us (level)
  transfers between devices with their start and end apart: 12 -> 12, of which waited for: 6 -> 6; matrix products, arithmetic and copies ran while one was open for 1% -> 1% of each run, Pallas kernels for 38% -> 37%
where the time goes in v7:
time: 181 us; the launch traced here: 180 us
  Pallas kernels  78.1 us (43%)
  waiting for transfers between devices  68 us (38%)
  starting transfers between devices  22.2 us (12%)
  local copies, waits for them, and re-layouts  11.3 us (6%)
    all_to_all x2, waiting for transfers between devices, local(): lax.all_to_all(array.reshape(owners * ranges, -1, *array.shape[2:]), axes...  60.4 us
    pallas_call x2, Pallas kernels, factor_slots(): pl.pallas_call(functools.partial(factor_kernel, first=first, share_slots=...  43.3 us
    pallas_call x4, Pallas kernels, form_spectrum(): pl.pallas_call(spectrum_kernel, out_shape=jax.ShapeDtypeStruct((bins, hei...  13.3 us
    unnamed x37, local copies, waits for them, and re-layouts  11.3 us
    all_to_all x2, starting transfers between devices, local(): lax.all_to_all(array.reshape(owners * ranges, -1, *array.shape[2:]), axes...  9.4 us
    ppermute x4, starting transfers between devices, shifted(): return lax.ppermute(array, axis, pairs)  7.86 us
    pallas_call x2, Pallas kernels, place_rows(): pl.pallas_call(functools.partial(place_kernel, first=first, share_slots=s...  7.5 us
    ppermute x4, waiting for transfers between devices, shifted(): return lax.ppermute(array, axis, pairs)  5.66 us
  transfers between devices with their start and end apart: 12, of which 6 were waited for; matrix products, arithmetic and copies ran while one was open for 1% of the time, Pallas kernels for 37%

profile of v7, /device:TPU:1, one launch (start us, length us, event | category | flops | bytes accessed | tf_op | source)
XLA Modules:
  0.0 180.3 jit_solution(12488440697392112720)
XLA Ops:
  0.0 1.3 rim_rows.7
  1.3 2.0 %collective-permute-start.3 = (bf16[2,16,64,128]{3,2,1,0:T(8,128)(2,1)S(1)}, bf16[2,16,64,128]{3,2,1,0:T(8,128)(2,1)}, u32[]{:S(2)}, u32[]{:S(2)}) collective-permute-start(bf16[2,16,64,128]{3,2,1,0:T(8,128)(2,1)S(1)} %rim_rows.7), channel_id=1, source_target_pairs={{1,0},{2,1},{3,2},{5,4},{6,5},{7,6},{9,8},{10,9},{11,10},{13,12},{... | collective-permute-start | bytes 1572872 | tf_op jit(solution)/shard_map/ppermute | solution.py:24
  3.3 1.3 rim_rows.4
  4.5 1.9 %collective-permute-start = (bf16[2,16,64,128]{3,2,1,0:T(8,128)(2,1)S(1)}, bf16[2,16,64,128]{3,2,1,0:T(8,128)(2,1)}, u32[]{:S(2)}, u32[]{:S(2)}) collective-permute-start(bf16[2,16,64,128]{3,2,1,0:T(8,128)(2,1)S(1)} %rim_rows.4), channel_id=1, source_target_pairs={{1,0},{2,1},{3,2},{5,4},{6,5},{7,6},{9,8},{10,9},{11,10},{13,12},{... | collective-permute-start | bytes 1572872 | tf_op jit(solution)/shard_map/ppermute | solution.py:24
  6.5 1.3 rim_rows.5
  7.8 2.1 %collective-permute-start.1 = (bf16[2,16,64,128]{3,2,1,0:T(8,128)(2,1)S(1)}, bf16[2,16,64,128]{3,2,1,0:T(8,128)(2,1)}, u32[]{:S(2)}, u32[]{:S(2)}) collective-permute-start(bf16[2,16,64,128]{3,2,1,0:T(8,128)(2,1)S(1)} %rim_rows.5), channel_id=1, source_target_pairs={{1,0},{2,1},{3,2},{5,4},{6,5},{7,6},{9,8},{10,9},{11,10},{13,12},{... | collective-permute-start | bytes 1572872 | tf_op jit(solution)/shard_map/ppermute | solution.py:24
  9.9 1.3 rim_rows.6
  11.2 1.9 %collective-permute-start.2 = (bf16[2,16,64,128]{3,2,1,0:T(8,128)(2,1)S(1)}, bf16[2,16,64,128]{3,2,1,0:T(8,128)(2,1)S(1)}, u32[]{:S(2)}, u32[]{:S(2)}) collective-permute-start(bf16[2,16,64,128]{3,2,1,0:T(8,128)(2,1)S(1)} %rim_rows.6), channel_id=1, source_target_pairs={{1,0},{2,1},{3,2},{5,4},{6,5},{7,6},{9,8},{10,9},{11,10},{13,12},{... | collective-permute-start | bytes 1572872 | tf_op jit(solution)/shard_map/ppermute | solution.py:24
  13.1 0.1 copy.17
  13.3 0.2 reduce-window.9
  13.5 0.1 pad_add_fusion.1.index_ref
  13.5 0.1 filter_rows.1.rows_ref
  13.7 0.1 pad_add_fusion.gates_ref
  13.8 3.4 %form_spectrum.7.refs_3_ = bf16[128,32,128]{2,1,0:T(8,128)(2,1)S(1)} custom-call(bf16[256,512]{1,0:T(8,128)(2,1)S(1)} %filter_rows.1.rows_ref, bf16[256,768]{1,0:T(8,128)(2,1)S(1)} %copy-done.11, f32[2,64,128,128]{3,2,1,0:T(8,128)} %own_ref.7, bf16[2,16,64,128]{3,2,1,0:T(8,128)(2,1)} %collective-permute-done.3.next_ref), custom_call_target="tpu_custom_call" | custom-call | flops 1342177280 | bytes 2097152 | tf_op jit(solution)/shard_map/form_spectrum/pallas_call | solution.py:144
  17.1 1.2 collective-permute-done.next_ref
  18.4 3.3 %form_spectrum.4.refs_0_ = bf16[128,32,128]{2,1,0:T(8,128)(2,1)S(1)} custom-call(bf16[256,512]{1,0:T(8,128)(2,1)S(1)} %filter_rows.1.rows_ref, bf16[256,768]{1,0:T(8,128)(2,1)S(1)} %copy-done.11, f32[2,64,128,128]{3,2,1,0:T(8,128)} %own_ref.7, bf16[2,16,64,128]{3,2,1,0:T(8,128)(2,1)} %collective-permute-done.next_ref), custom_call_target="tpu_custom_call" | custom-call | flops 1342177280 | bytes 2097152 | tf_op jit(solution)/shard_map/form_spectrum/pallas_call | solution.py:144
  21.7 2.3 %collective-permute-done.1.next_ref = bf16[2,16,64,128]{3,2,1,0:T(8,128)(2,1)} collective-permute-done((bf16[2,16,64,128]{3,2,1,0:T(8,128)(2,1)S(1)}, bf16[2,16,64,128]{3,2,1,0:T(8,128)(2,1)}, u32[]{:S(2)}, u32[]{:S(2)}) %collective-permute-start.1) | collective-permute-done | bytes 524320 | tf_op jit(solution)/shard_map/ppermute | solution.py:24
  24.0 3.3 %form_spectrum.5.refs_1_ = bf16[128,32,128]{2,1,0:T(8,128)(2,1)S(1)} custom-call(bf16[256,512]{1,0:T(8,128)(2,1)S(1)} %filter_rows.1.rows_ref, bf16[256,768]{1,0:T(8,128)(2,1)S(1)} %copy-done.11, f32[2,64,128,128]{3,2,1,0:T(8,128)} %own_ref.7, bf16[2,16,64,128]{3,2,1,0:T(8,128)(2,1)} %collective-permute-done.1.next_ref), custom_call_target="tpu_custom_call" | custom-call | flops 1342177280 | bytes 2097152 | tf_op jit(solution)/shard_map/form_spectrum/pallas_call | solution.py:144
  27.3 2.2 %collective-permute-done.2.next_ref = bf16[2,16,64,128]{3,2,1,0:T(8,128)(2,1)S(1)} collective-permute-done((bf16[2,16,64,128]{3,2,1,0:T(8,128)(2,1)S(1)}, bf16[2,16,64,128]{3,2,1,0:T(8,128)(2,1)S(1)}, u32[]{:S(2)}, u32[]{:S(2)}) %collective-permute-start.2) | collective-permute-done | bytes 524320 | tf_op jit(solution)/shard_map/ppermute | solution.py:24
  29.5 3.3 %form_spectrum.6.refs_2_ = bf16[128,32,128]{2,1,0:T(8,128)(2,1)S(1)} custom-call(bf16[256,512]{1,0:T(8,128)(2,1)S(1)} %filter_rows.1.rows_ref, bf16[256,768]{1,0:T(8,128)(2,1)S(1)} %copy-done.11, f32[2,64,128,128]{3,2,1,0:T(8,128)} %own_ref.7, bf16[2,16,64,128]{3,2,1,0:T(8,128)(2,1)S(1)} %collective-permute-done.2.next_ref), custom_call_target="tpu_custom_call" | custom-call | flops 1342177280 | bytes 2097152 | tf_op jit(solution)/shard_map/form_spectrum/pallas_call | solution.py:144
  32.8 3.7 %select_gates.3 = (bf16[8,12,128,128]{3,2,1,0:T(8,128)(2,1)}, s32[8,128]{1,0:T(8,128)}) custom-call(s32[18]{0:T(128)S(1)} %pad_add_fusion.1.index_ref, s32[128,128]{1,0:T(8,128)S(1)} %pad_add_fusion.gates_ref, bf16[128,32,128]{2,1,0:T(8,128)(2,1)S(1)} %form_spectrum.4.refs_0_, bf16[128,32,128]{2,1,0:T(8,128)(2,1)S(1)} %form_spectrum.5.refs_1_, ...), custom_call_target="tpu_custom_call" | custom-call | flops 805306368 | bytes 3145728 | tf_op jit(solution)/shard_map/select_gates/pallas_call | solution.py:214
  36.6 4.8 %all-to-all-start.1 = ((bf16[32,3,128,128]{3,2,1,0:T(8,128)(2,1)}), bf16[32,3,128,128]{3,2,1,0:T(8,128)(2,1)S(1)}, u32[]{:S(2)}, u32[]{:S(2)}) async-start(bf16[32,3,128,128]{3,2,1,0:T(8,128)(2,1)} %bitcast.13), calls=%async_computation.1 | async-start | bytes 6291456 | tf_op jit(solution)/shard_map/all_to_all | solution.py:625
  41.4 2.0 %copy.24.refs_4_.weights_ref = bf16[2,512,192]{2,1,0:T(8,128)(2,1)} copy(bf16[2,512,192]{1,2,0:T(8,128)(2,1)} %param.9) | data formatting | bytes 786432 | tf_op args[2]
  43.5 1.2 copy-done.1
  44.7 1.2 copy-done.3
  45.9 1.2 copy-done.5
  47.1 1.2 copy-done.7
  48.4 1.0 copy-done.8
  49.4 1.4 select_gates.2
  50.9 1.0 copy-done.12
  51.8 60.4 %all-to-all-done.1 = bf16[32,3,128,128]{3,2,1,0:T(8,128)(2,1)S(1)} async-done(((bf16[32,3,128,128]{3,2,1,0:T(8,128)(2,1)}), bf16[32,3,128,128]{3,2,1,0:T(8,128)(2,1)S(1)}, u32[]{:S(2)}, u32[]{:S(2)}) %all-to-all-start.1) | async-done | bytes 3145760 | tf_op jit(solution)/shard_map/all_to_all | solution.py:625
  112.2 4.6 %all-to-all-start = ((bf16[32,1,128,128]{3,2,1,0:T(8,128)(2,1)}), bf16[32,1,128,128]{3,2,1,0:T(8,128)(2,1)}, u32[]{:S(2)}, u32[]{:S(2)}) async-start(bf16[32,1,128,128]{3,2,1,0:T(8,128)(2,1)} %bitcast.12), calls=%async_computation | async-start | bytes 2097152 | tf_op jit(solution)/shard_map/all_to_all | solution.py:625
  116.9 0.1 copy.25.pivots_ref
  117.0 1.0 copy-done.9
  118.0 1.4 form_beams.2.beams_ref
  119.5 23.7 %factor_slots.2 = (bf16[6,96,384]{2,1,0:T(8,128)(2,1)S(1)}, bf16[6,96,384]{2,1,0:T(8,128)(2,1)S(1)}, bf16[6,96,384]{2,1,0:T(8,128)(2,1)S(1)}, bf16[6,96,384]{2,1,0:T(8,128)(2,1)S(1)}) custom-call(s32[18]{0:T(128)S(1)} %pad_add_fusion.1.index_ref, s32[128,192]{1,0:T(8,128)S(1)} %copy.25.pivots_ref, bf16[4,3,384,128]{3,2,1,0:T(8,128)(2,1)S(1)} %form_beams.2.beams_ref), custom_call_target="tpu_custom_call" | custom-call | flops 339738624 | bytes 1179648 | tf_op jit(solution)/shard_map/factor_slots/pallas_call | solution.py:509
  143.2 1.7 collective-permute-start.7
  144.8 0.2 collective-permute-start.8
  145.1 0.3 collective-permute-start.9
  145.4 1.0 copy-done.10
  146.5 2.1 %form_beams.3.beams_ref = bf16[4,1,384,128]{3,2,1,0:T(8,128)(2,1)S(1)} custom-call(bf16[2,512,192]{2,1,0:T(8,128)(2,1)S(1)} %copy-done.10, bf16[8,4,1,128,128]{4,3,2,1,0:T(8,128)(2,1)} %bitcast.6.arrived_ref, bf16[6,96,384]{2,1,0:T(8,128)(2,1)S(1)} %get-tuple-element.19.refs_0_), custom_call_target="tpu_custom_call" | custom-call | flops 402653184 | bytes 1048576 | tf_op jit(solution)/shard_map/form_beams/pallas_call | solution.py:278
  148.5 19.6 %factor_slots.3 = (bf16[2,96,384]{2,1,0:T(8,128)(2,1)S(1)}, bf16[2,96,384]{2,1,0:T(8,128)(2,1)S(1)}, bf16[2,96,384]{2,1,0:T(8,128)(2,1)S(1)}, bf16[2,96,384]{2,1,0:T(8,128)(2,1)S(1)}) custom-call(s32[18]{0:T(128)S(1)} %pad_add_fusion.1.index_ref, s32[128,192]{1,0:T(8,128)S(1)} %copy.25.pivots_ref, bf16[4,1,384,128]{3,2,1,0:T(8,128)(2,1)S(1)} %form_beams.3.beams_ref), custom_call_target="tpu_custom_call" | custom-call | flops 113246208 | bytes 393216 | tf_op jit(solution)/shard_map/factor_slots/pallas_call | solution.py:509
  168.1 1.4 collective-permute-start.4
  169.6 1.3 collective-permute-start.5
  170.9 5.3 %place_rows.2.refs_4_ = f32[32,96,384]{2,1,0:T(8,128)} custom-call(s32[18]{0:T(128)S(1)} %pad_add_fusion.1.index_ref, bf16[6,96,384]{2,1,0:T(8,128)(2,1)S(1)} %get-tuple-element.19.refs_0_, bf16[6,96,384]{2,1,0:T(8,128)(2,1)S(1)} %collective-permute-done.7.refs_1_, bf16[6,96,384]{2,1,0:T(8,128)(2,1)S(1)} %collective-permute-done.8.refs_2_, ...), custom_call_target="tpu_custom_call" | custom-call | tf_op jit(solution)/shard_map/place_rows/pallas_call | solution.py:564
  176.1 1.3 collective-permute-done.5.refs_2_
  177.5 0.6 collective-permute-done.6.refs_3_
  178.1 2.2 %place_rows.3 = f32[32,96,384]{2,1,0:T(8,128)} custom-call(s32[18]{0:T(128)S(1)} %pad_add_fusion.1.index_ref, bf16[2,96,384]{2,1,0:T(8,128)(2,1)S(1)} %get-tuple-element.20.refs_0_, bf16[2,96,384]{2,1,0:T(8,128)(2,1)S(1)} %collective-permute-done.4.refs_1_, bf16[2,96,384]{2,1,0:T(8,128)(2,1)S(1)} %collective-permute-done.5.refs_2_, ...), custom_call_target="tpu_custom_call", output_to_operand_aliasing={{}: (5, {})} | custom-call | tf_op jit(solution)/shard_map/place_rows/pallas_call | solution.py:564
  (36 shorter events, 0.1 us)
Async XLA Ops:
  1.3 12.5 %collective-permute-start.3 = (bf16[2,16,64,128]{3,2,1,0:T(8,128)(2,1)S(1)}, bf16[2,16,64,128]{3,2,1,0:T(8,128)(2,1)}, u32[]{:S(2)}, u32[]{:S(2)}) collective-permute-start(bf16[2,16,64,128]{3,2,1,0:T(8,128)(2,1)S(1)} %rim_rows.7), channel_id=1, source_target_pairs={{1,0},{2,1},{3,2},{5,4},{6,5},{7,6},{9,8},{10,9},{11,10},{13,12},{... | collective-permute-start | bytes 1572872 | tf_op jit(solution)/shard_map/ppermute | solution.py:24
  4.5 13.8 %collective-permute-start = (bf16[2,16,64,128]{3,2,1,0:T(8,128)(2,1)S(1)}, bf16[2,16,64,128]{3,2,1,0:T(8,128)(2,1)}, u32[]{:S(2)}, u32[]{:S(2)}) collective-permute-start(bf16[2,16,64,128]{3,2,1,0:T(8,128)(2,1)S(1)} %rim_rows.4), channel_id=1, source_target_pairs={{1,0},{2,1},{3,2},{5,4},{6,5},{7,6},{9,8},{10,9},{11,10},{13,12},{... | collective-permute-start | bytes 1572872 | tf_op jit(solution)/shard_map/ppermute | solution.py:24
  7.8 5.3 %copy-start.14 = (s32[128,64]{0,1:T(8,128)S(1)}, s32[128,64]{0,1:T(8,128)}, u32[]{:S(2)}) copy-start(s32[128,64]{0,1:T(8,128)} %param.12) | copy-start | bytes 98308
  7.8 5.5 %copy-start.16 = (s32[8]{0:T(128)S(1)}, s32[8]{0:T(128)}, u32[]{:S(2)}) copy-start(s32[8]{0:T(128)} %param.11) | copy-start | bytes 100
  7.8 5.7 %copy-start.15 = (f32[2,64]{1,0:T(2,128)S(1)}, f32[2,64]{1,0:T(2,128)}, u32[]{:S(2)}) copy-start(f32[2,64]{1,0:T(2,128)} %param.8) | copy-start | bytes 1540
  7.8 6.0 %copy-start.11 = (bf16[256,768]{1,0:T(8,128)(2,1)S(1)}, bf16[256,768]{1,0:T(8,128)(2,1)}, u32[]{:S(2)}) copy-start(bf16[256,768]{1,0:T(8,128)(2,1)} %constant.33.clone.table_ref) | copy-start | bytes 1179652
  7.8 16.2 %collective-permute-start.1 = (bf16[2,16,64,128]{3,2,1,0:T(8,128)(2,1)S(1)}, bf16[2,16,64,128]{3,2,1,0:T(8,128)(2,1)}, u32[]{:S(2)}, u32[]{:S(2)}) collective-permute-start(bf16[2,16,64,128]{3,2,1,0:T(8,128)(2,1)S(1)} %rim_rows.5), channel_id=1, source_target_pairs={{1,0},{2,1},{3,2},{5,4},{6,5},{7,6},{9,8},{10,9},{11,10},{13,12},{... | collective-permute-start | bytes 1572872 | tf_op jit(solution)/shard_map/ppermute | solution.py:24
  11.2 18.3 %collective-permute-start.2 = (bf16[2,16,64,128]{3,2,1,0:T(8,128)(2,1)S(1)}, bf16[2,16,64,128]{3,2,1,0:T(8,128)(2,1)S(1)}, u32[]{:S(2)}, u32[]{:S(2)}) collective-permute-start(bf16[2,16,64,128]{3,2,1,0:T(8,128)(2,1)S(1)} %rim_rows.6), channel_id=1, source_target_pairs={{1,0},{2,1},{3,2},{5,4},{6,5},{7,6},{9,8},{10,9},{11,10},{13,12},{... | collective-permute-start | bytes 1572872 | tf_op jit(solution)/shard_map/ppermute | solution.py:24
  17.1 15.7 %copy-start = (bf16[128,32,128]{2,1,0:T(8,128)(2,1)}, bf16[128,32,128]{2,1,0:T(8,128)(2,1)S(1)}, u32[]{:S(2)}) copy-start(bf16[128,32,128]{2,1,0:T(8,128)(2,1)S(1)} %form_spectrum.7.refs_3_) | copy-start | bytes 3145732
  21.7 11.1 %copy-start.2 = (bf16[128,32,128]{2,1,0:T(8,128)(2,1)}, bf16[128,32,128]{2,1,0:T(8,128)(2,1)S(1)}, u32[]{:S(2)}) copy-start(bf16[128,32,128]{2,1,0:T(8,128)(2,1)S(1)} %form_spectrum.4.refs_0_) | copy-start | bytes 3145732
  27.3 5.5 %copy-start.4 = (bf16[128,32,128]{2,1,0:T(8,128)(2,1)}, bf16[128,32,128]{2,1,0:T(8,128)(2,1)S(1)}, u32[]{:S(2)}) copy-start(bf16[128,32,128]{2,1,0:T(8,128)(2,1)S(1)} %form_spectrum.5.refs_1_) | copy-start | bytes 3145732
  32.8 3.8 %copy-start.6 = (bf16[128,32,128]{2,1,0:T(8,128)(2,1)}, bf16[128,32,128]{2,1,0:T(8,128)(2,1)S(1)}, u32[]{:S(2)}) copy-start(bf16[128,32,128]{2,1,0:T(8,128)(2,1)S(1)} %form_spectrum.6.refs_2_) | copy-start | bytes 3145732
  36.6 75.6 %all-to-all-start.1 = ((bf16[32,3,128,128]{3,2,1,0:T(8,128)(2,1)}), bf16[32,3,128,128]{3,2,1,0:T(8,128)(2,1)S(1)}, u32[]{:S(2)}, u32[]{:S(2)}) async-start(bf16[32,3,128,128]{3,2,1,0:T(8,128)(2,1)} %bitcast.13), calls=%async_computation.1 | async-start | bytes 6291456 | tf_op jit(solution)/shard_map/all_to_all | solution.py:625
  41.4 75.5 %copy-start.13 = (s32[128,192]{0,1:T(8,128)S(1)}, s32[128,192]{0,1:T(8,128)}, u32[]{:S(2)}) copy-start(s32[128,192]{0,1:T(8,128)} %param.10) | copy-start | bytes 294916
  43.4 1.2 copy-start.1
  44.7 1.2 copy-start.3
  45.9 1.2 copy-start.5
  47.1 1.2 copy-start.7
  48.4 1.0 copy-start.8
  50.8 1.0 copy-start.12
  112.2 33.2 %all-to-all-start = ((bf16[32,1,128,128]{3,2,1,0:T(8,128)(2,1)}), bf16[32,1,128,128]{3,2,1,0:T(8,128)(2,1)}, u32[]{:S(2)}, u32[]{:S(2)}) async-start(bf16[32,1,128,128]{3,2,1,0:T(8,128)(2,1)} %bitcast.12), calls=%async_computation | async-start | bytes 2097152 | tf_op jit(solution)/shard_map/all_to_all | solution.py:625
  117.0 1.0 copy-start.9
  143.2 27.7 %collective-permute-start.7 = (bf16[6,96,384]{2,1,0:T(8,128)(2,1)S(1)}, bf16[6,96,384]{2,1,0:T(8,128)(2,1)S(1)}, u32[]{:S(2)}, u32[]{:S(2)}) collective-permute-start(bf16[6,96,384]{2,1,0:T(8,128)(2,1)S(1)} %get-tuple-element.24), channel_id=1, source_target_pairs={{0,1},{1,2},{2,3},{3,0},{4,5},{5,6},{6,7},{7,4},{8,9},{9,10},{10,1... | collective-permute-start | bytes 1327112 | tf_op jit(solution)/shard_map/ppermute | solution.py:299
  144.8 26.0 %collective-permute-start.8 = (bf16[6,96,384]{2,1,0:T(8,128)(2,1)S(1)}, bf16[6,96,384]{2,1,0:T(8,128)(2,1)S(1)}, u32[]{:S(2)}, u32[]{:S(2)}) collective-permute-start(bf16[6,96,384]{2,1,0:T(8,128)(2,1)S(1)} %get-tuple-element.25), channel_id=1, source_target_pairs={{0,2},{1,3},{2,0},{3,1},{4,6},{5,7},{6,4},{7,5},{8,10},{9,11},{10,... | collective-permute-start | bytes 1327112 | tf_op jit(solution)/shard_map/ppermute | solution.py:299
  145.1 25.8 %collective-permute-start.9 = (bf16[6,96,384]{2,1,0:T(8,128)(2,1)S(1)}, bf16[6,96,384]{2,1,0:T(8,128)(2,1)S(1)}, u32[]{:S(2)}, u32[]{:S(2)}) collective-permute-start(bf16[6,96,384]{2,1,0:T(8,128)(2,1)S(1)} %get-tuple-element.26), channel_id=1, source_target_pairs={{0,3},{1,0},{2,1},{3,2},{4,7},{5,4},{6,5},{7,6},{8,11},{9,8},{10,9... | collective-permute-start | bytes 1327112 | tf_op jit(solution)/shard_map/ppermute | solution.py:299
  145.4 1.0 copy-start.10
  168.1 8.0 %collective-permute-start.4 = (bf16[2,96,384]{2,1,0:T(8,128)(2,1)S(1)}, bf16[2,96,384]{2,1,0:T(8,128)(2,1)S(1)}, u32[]{:S(2)}, u32[]{:S(2)}) collective-permute-start(bf16[2,96,384]{2,1,0:T(8,128)(2,1)S(1)} %get-tuple-element.21), channel_id=1, source_target_pairs={{0,1},{1,2},{2,3},{3,0},{4,5},{5,6},{6,7},{7,4},{8,9},{9,10},{10,1... | collective-permute-start | bytes 442376 | tf_op jit(solution)/shard_map/ppermute | solution.py:299
  169.6 7.9 %collective-permute-start.5 = (bf16[2,96,384]{2,1,0:T(8,128)(2,1)S(1)}, bf16[2,96,384]{2,1,0:T(8,128)(2,1)S(1)}, u32[]{:S(2)}, u32[]{:S(2)}) collective-permute-start(bf16[2,96,384]{2,1,0:T(8,128)(2,1)S(1)} %get-tuple-element.22), channel_id=1, source_target_pairs={{0,2},{1,3},{2,0},{3,1},{4,6},{5,7},{6,4},{7,5},{8,10},{9,11},{10,... | collective-permute-start | bytes 442376 | tf_op jit(solution)/shard_map/ppermute | solution.py:299
  170.8 7.3 %collective-permute-start.6 = (bf16[2,96,384]{2,1,0:T(8,128)(2,1)S(1)}, bf16[2,96,384]{2,1,0:T(8,128)(2,1)S(1)}, u32[]{:S(2)}, u32[]{:S(2)}) collective-permute-start(bf16[2,96,384]{2,1,0:T(8,128)(2,1)S(1)} %get-tuple-element.23), channel_id=1, source_target_pairs={{0,3},{1,0},{2,1},{3,2},{4,7},{5,4},{6,5},{7,6},{8,11},{9,8},{10,9... | collective-permute-start | bytes 442376 | tf_op jit(solution)/shard_map/ppermute | solution.py:299

commit v8 on v7

--- a/solution.py
+++ b/solution.py
@@ -11,7 +11,7 @@
 
 LOADING = 0.25
 LANES = 128
-PANEL = 32
+PANEL = 16
 BF16 = jnp.bfloat16
 F32 = jnp.float32
 PARAMS = pltpu.CompilerParams(vmem_limit_bytes=48 * 1024 * 1024)

time: 181 us -> 184 us (1.017)
  Pallas kernels: 78.1 us -> 80.7 us
    pallas_call x2, Pallas kernels: 43.3 us -> 45.9 us  [factor_slots(): pl.pallas_call(functools.partial(factor_kernel, first=first, share_slots=...]
  transfers between devices with their start and end apart: 12 -> 12, of which waited for: 6 -> 6; matrix products, arithmetic and copies ran while one was open for 1% -> 1% of each run, Pallas kernels for 37% -> 38%
where the time goes in v8:
time: 184 us; the launch traced here: 183 us
  Pallas kernels  80.7 us (44%)
  waiting for transfers between devices  68 us (37%)
  starting transfers between devices  22.2 us (12%)
  local copies, waits for them, and re-layouts  11.3 us (6%)
    all_to_all x2, waiting for transfers between devices, local(): lax.all_to_all(array.reshape(owners * ranges, -1, *array.shape[2:]), axes...  60.4 us
    pallas_call x2, Pallas kernels, factor_slots(): pl.pallas_call(functools.partial(factor_kernel, first=first, share_slots=...  45.9 us
    pallas_call x4, Pallas kernels, form_spectrum(): pl.pallas_call(spectrum_kernel, out_shape=jax.ShapeDtypeStruct((bins, hei...  13.3 us
    unnamed x37, local copies, waits for them, and re-layouts  11.3 us
    all_to_all x2, starting transfers between devices, local(): lax.all_to_all(array.reshape(owners * ranges, -1, *array.shape[2:]), axes...  9.4 us
    ppermute x4, starting transfers between devices, shifted(): return lax.ppermute(array, axis, pairs)  7.86 us
    pallas_call x2, Pallas kernels, place_rows(): pl.pallas_call(functools.partial(place_kernel, first=first, share_slots=s...  7.5 us
    ppermute x4, waiting for transfers between devices, shifted(): return lax.ppermute(array, axis, pairs)  5.66 us
  transfers between devices with their start and end apart: 12, of which 6 were waited for; matrix products, arithmetic and copies ran while one was open for 1% of the time, Pallas kernels for 38%

profile of v8, /device:TPU:1, one launch (start us, length us, event | category | flops | bytes accessed | tf_op | source)
XLA Modules:
  0.0 183.0 jit_solution(1930712225567284568)
XLA Ops:
  0.0 1.3 rim_rows.7
  1.3 2.0 %collective-permute-start.3 = (bf16[2,16,64,128]{3,2,1,0:T(8,128)(2,1)S(1)}, bf16[2,16,64,128]{3,2,1,0:T(8,128)(2,1)}, u32[]{:S(2)}, u32[]{:S(2)}) collective-permute-start(bf16[2,16,64,128]{3,2,1,0:T(8,128)(2,1)S(1)} %rim_rows.7), channel_id=1, source_target_pairs={{1,0},{2,1},{3,2},{5,4},{6,5},{7,6},{9,8},{10,9},{11,10},{13,12},{... | collective-permute-start | bytes 1572872 | tf_op jit(solution)/shard_map/ppermute | solution.py:24
  3.3 1.3 rim_rows.4
  4.5 1.9 %collective-permute-start = (bf16[2,16,64,128]{3,2,1,0:T(8,128)(2,1)S(1)}, bf16[2,16,64,128]{3,2,1,0:T(8,128)(2,1)}, u32[]{:S(2)}, u32[]{:S(2)}) collective-permute-start(bf16[2,16,64,128]{3,2,1,0:T(8,128)(2,1)S(1)} %rim_rows.4), channel_id=1, source_target_pairs={{1,0},{2,1},{3,2},{5,4},{6,5},{7,6},{9,8},{10,9},{11,10},{13,12},{... | collective-permute-start | bytes 1572872 | tf_op jit(solution)/shard_map/ppermute | solution.py:24
  6.5 1.3 rim_rows.5
  7.8 2.1 %collective-permute-start.1 = (bf16[2,16,64,128]{3,2,1,0:T(8,128)(2,1)S(1)}, bf16[2,16,64,128]{3,2,1,0:T(8,128)(2,1)}, u32[]{:S(2)}, u32[]{:S(2)}) collective-permute-start(bf16[2,16,64,128]{3,2,1,0:T(8,128)(2,1)S(1)} %rim_rows.5), channel_id=1, source_target_pairs={{1,0},{2,1},{3,2},{5,4},{6,5},{7,6},{9,8},{10,9},{11,10},{13,12},{... | collective-permute-start | bytes 1572872 | tf_op jit(solution)/shard_map/ppermute | solution.py:24
  9.9 1.3 rim_rows.6
  11.2 1.9 %collective-permute-start.2 = (bf16[2,16,64,128]{3,2,1,0:T(8,128)(2,1)S(1)}, bf16[2,16,64,128]{3,2,1,0:T(8,128)(2,1)S(1)}, u32[]{:S(2)}, u32[]{:S(2)}) collective-permute-start(bf16[2,16,64,128]{3,2,1,0:T(8,128)(2,1)S(1)} %rim_rows.6), channel_id=1, source_target_pairs={{1,0},{2,1},{3,2},{5,4},{6,5},{7,6},{9,8},{10,9},{11,10},{13,12},{... | collective-permute-start | bytes 1572872 | tf_op jit(solution)/shard_map/ppermute | solution.py:24
  13.1 0.1 copy.17
  13.3 0.2 reduce-window.9
  13.5 0.1 pad_add_fusion.1.index_ref
  13.5 0.1 filter_rows.1.rows_ref
  13.7 0.1 pad_add_fusion.gates_ref
  13.8 3.4 %form_spectrum.7.refs_3_ = bf16[128,32,128]{2,1,0:T(8,128)(2,1)S(1)} custom-call(bf16[256,512]{1,0:T(8,128)(2,1)S(1)} %filter_rows.1.rows_ref, bf16[256,768]{1,0:T(8,128)(2,1)S(1)} %copy-done.11, f32[2,64,128,128]{3,2,1,0:T(8,128)} %own_ref.7, bf16[2,16,64,128]{3,2,1,0:T(8,128)(2,1)} %collective-permute-done.3.next_ref), custom_call_target="tpu_custom_call" | custom-call | flops 1342177280 | bytes 2097152 | tf_op jit(solution)/shard_map/form_spectrum/pallas_call | solution.py:144
  17.1 1.2 collective-permute-done.next_ref
  18.4 3.3 %form_spectrum.4.refs_0_ = bf16[128,32,128]{2,1,0:T(8,128)(2,1)S(1)} custom-call(bf16[256,512]{1,0:T(8,128)(2,1)S(1)} %filter_rows.1.rows_ref, bf16[256,768]{1,0:T(8,128)(2,1)S(1)} %copy-done.11, f32[2,64,128,128]{3,2,1,0:T(8,128)} %own_ref.7, bf16[2,16,64,128]{3,2,1,0:T(8,128)(2,1)} %collective-permute-done.next_ref), custom_call_target="tpu_custom_call" | custom-call | flops 1342177280 | bytes 2097152 | tf_op jit(solution)/shard_map/form_spectrum/pallas_call | solution.py:144
  21.7 2.3 %collective-permute-done.1.next_ref = bf16[2,16,64,128]{3,2,1,0:T(8,128)(2,1)} collective-permute-done((bf16[2,16,64,128]{3,2,1,0:T(8,128)(2,1)S(1)}, bf16[2,16,64,128]{3,2,1,0:T(8,128)(2,1)}, u32[]{:S(2)}, u32[]{:S(2)}) %collective-permute-start.1) | collective-permute-done | bytes 524320 | tf_op jit(solution)/shard_map/ppermute | solution.py:24
  24.0 3.3 %form_spectrum.5.refs_1_ = bf16[128,32,128]{2,1,0:T(8,128)(2,1)S(1)} custom-call(bf16[256,512]{1,0:T(8,128)(2,1)S(1)} %filter_rows.1.rows_ref, bf16[256,768]{1,0:T(8,128)(2,1)S(1)} %copy-done.11, f32[2,64,128,128]{3,2,1,0:T(8,128)} %own_ref.7, bf16[2,16,64,128]{3,2,1,0:T(8,128)(2,1)} %collective-permute-done.1.next_ref), custom_call_target="tpu_custom_call" | custom-call | flops 1342177280 | bytes 2097152 | tf_op jit(solution)/shard_map/form_spectrum/pallas_call | solution.py:144
  27.3 2.2 %collective-permute-done.2.next_ref = bf16[2,16,64,128]{3,2,1,0:T(8,128)(2,1)S(1)} collective-permute-done((bf16[2,16,64,128]{3,2,1,0:T(8,128)(2,1)S(1)}, bf16[2,16,64,128]{3,2,1,0:T(8,128)(2,1)S(1)}, u32[]{:S(2)}, u32[]{:S(2)}) %collective-permute-start.2) | collective-permute-done | bytes 524320 | tf_op jit(solution)/shard_map/ppermute | solution.py:24
  29.5 3.3 %form_spectrum.6.refs_2_ = bf16[128,32,128]{2,1,0:T(8,128)(2,1)S(1)} custom-call(bf16[256,512]{1,0:T(8,128)(2,1)S(1)} %filter_rows.1.rows_ref, bf16[256,768]{1,0:T(8,128)(2,1)S(1)} %copy-done.11, f32[2,64,128,128]{3,2,1,0:T(8,128)} %own_ref.7, bf16[2,16,64,128]{3,2,1,0:T(8,128)(2,1)S(1)} %collective-permute-done.2.next_ref), custom_call_target="tpu_custom_call" | custom-call | flops 1342177280 | bytes 2097152 | tf_op jit(solution)/shard_map/form_spectrum/pallas_call | solution.py:144
  32.8 3.7 %select_gates.3 = (bf16[8,12,128,128]{3,2,1,0:T(8,128)(2,1)}, s32[8,128]{1,0:T(8,128)}) custom-call(s32[18]{0:T(128)S(1)} %pad_add_fusion.1.index_ref, s32[128,128]{1,0:T(8,128)S(1)} %pad_add_fusion.gates_ref, bf16[128,32,128]{2,1,0:T(8,128)(2,1)S(1)} %form_spectrum.4.refs_0_, bf16[128,32,128]{2,1,0:T(8,128)(2,1)S(1)} %form_spectrum.5.refs_1_, ...), custom_call_target="tpu_custom_call" | custom-call | flops 805306368 | bytes 3145728 | tf_op jit(solution)/shard_map/select_gates/pallas_call | solution.py:214
  36.6 4.8 %all-to-all-start.1 = ((bf16[32,3,128,128]{3,2,1,0:T(8,128)(2,1)}), bf16[32,3,128,128]{3,2,1,0:T(8,128)(2,1)S(1)}, u32[]{:S(2)}, u32[]{:S(2)}) async-start(bf16[32,3,128,128]{3,2,1,0:T(8,128)(2,1)} %bitcast.13), calls=%async_computation.1 | async-start | bytes 6291456 | tf_op jit(solution)/shard_map/all_to_all | solution.py:625
  41.4 2.0 %copy.24.refs_4_.weights_ref = bf16[2,512,192]{2,1,0:T(8,128)(2,1)} copy(bf16[2,512,192]{1,2,0:T(8,128)(2,1)} %param.9) | data formatting | bytes 786432 | tf_op args[2]
  43.5 1.2 copy-done.1
  44.7 1.2 copy-done.3
  45.9 1.2 copy-done.5
  47.1 1.2 copy-done.7
  48.4 1.0 copy-done.8
  49.4 1.4 select_gates.2
  50.9 1.0 copy-done.12
  51.8 60.4 %all-to-all-done.1 = bf16[32,3,128,128]{3,2,1,0:T(8,128)(2,1)S(1)} async-done(((bf16[32,3,128,128]{3,2,1,0:T(8,128)(2,1)}), bf16[32,3,128,128]{3,2,1,0:T(8,128)(2,1)S(1)}, u32[]{:S(2)}, u32[]{:S(2)}) %all-to-all-start.1) | async-done | bytes 3145760 | tf_op jit(solution)/shard_map/all_to_all | solution.py:625
  112.2 4.6 %all-to-all-start = ((bf16[32,1,128,128]{3,2,1,0:T(8,128)(2,1)}), bf16[32,1,128,128]{3,2,1,0:T(8,128)(2,1)}, u32[]{:S(2)}, u32[]{:S(2)}) async-start(bf16[32,1,128,128]{3,2,1,0:T(8,128)(2,1)} %bitcast.12), calls=%async_computation | async-start | bytes 2097152 | tf_op jit(solution)/shard_map/all_to_all | solution.py:625
  116.9 0.1 copy.25.pivots_ref
  117.0 1.0 copy-done.9
  118.0 1.4 form_beams.2.beams_ref
  119.5 25.1 %factor_slots.2 = (bf16[6,96,384]{2,1,0:T(8,128)(2,1)S(1)}, bf16[6,96,384]{2,1,0:T(8,128)(2,1)S(1)}, bf16[6,96,384]{2,1,0:T(8,128)(2,1)S(1)}, bf16[6,96,384]{2,1,0:T(8,128)(2,1)S(1)}) custom-call(s32[18]{0:T(128)S(1)} %pad_add_fusion.1.index_ref, s32[128,192]{1,0:T(8,128)S(1)} %copy.25.pivots_ref, bf16[4,3,384,128]{3,2,1,0:T(8,128)(2,1)S(1)} %form_beams.2.beams_ref), custom_call_target="tpu_custom_call" | custom-call | flops 339738624 | bytes 1179648 | tf_op jit(solution)/shard_map/factor_slots/pallas_call | solution.py:509
  144.6 1.7 collective-permute-start.7
  146.3 0.2 collective-permute-start.8
  146.5 0.3 collective-permute-start.9
  146.8 1.0 copy-done.10
  147.9 2.1 %form_beams.3.beams_ref = bf16[4,1,384,128]{3,2,1,0:T(8,128)(2,1)S(1)} custom-call(bf16[2,512,192]{2,1,0:T(8,128)(2,1)S(1)} %copy-done.10, bf16[8,4,1,128,128]{4,3,2,1,0:T(8,128)(2,1)} %bitcast.6.arrived_ref, bf16[6,96,384]{2,1,0:T(8,128)(2,1)S(1)} %get-tuple-element.19.refs_0_), custom_call_target="tpu_custom_call" | custom-call | flops 402653184 | bytes 1048576 | tf_op jit(solution)/shard_map/form_beams/pallas_call | solution.py:278
  149.9 20.8 %factor_slots.3 = (bf16[2,96,384]{2,1,0:T(8,128)(2,1)S(1)}, bf16[2,96,384]{2,1,0:T(8,128)(2,1)S(1)}, bf16[2,96,384]{2,1,0:T(8,128)(2,1)S(1)}, bf16[2,96,384]{2,1,0:T(8,128)(2,1)S(1)}) custom-call(s32[18]{0:T(128)S(1)} %pad_add_fusion.1.index_ref, s32[128,192]{1,0:T(8,128)S(1)} %copy.25.pivots_ref, bf16[4,1,384,128]{3,2,1,0:T(8,128)(2,1)S(1)} %form_beams.3.beams_ref), custom_call_target="tpu_custom_call" | custom-call | flops 113246208 | bytes 393216 | tf_op jit(solution)/shard_map/factor_slots/pallas_call | solution.py:509
  170.8 1.5 collective-permute-start.4
  172.2 1.3 collective-permute-start.5
  173.5 5.3 %place_rows.2.refs_4_ = f32[32,96,384]{2,1,0:T(8,128)} custom-call(s32[18]{0:T(128)S(1)} %pad_add_fusion.1.index_ref, bf16[6,96,384]{2,1,0:T(8,128)(2,1)S(1)} %get-tuple-element.19.refs_0_, bf16[6,96,384]{2,1,0:T(8,128)(2,1)S(1)} %collective-permute-done.7.refs_1_, bf16[6,96,384]{2,1,0:T(8,128)(2,1)S(1)} %collective-permute-done.8.refs_2_, ...), custom_call_target="tpu_custom_call" | custom-call | tf_op jit(solution)/shard_map/place_rows/pallas_call | solution.py:564
  178.8 1.3 collective-permute-done.5.refs_2_
  180.1 0.6 collective-permute-done.6.refs_3_
  180.7 2.2 %place_rows.3 = f32[32,96,384]{2,1,0:T(8,128)} custom-call(s32[18]{0:T(128)S(1)} %pad_add_fusion.1.index_ref, bf16[2,96,384]{2,1,0:T(8,128)(2,1)S(1)} %get-tuple-element.20.refs_0_, bf16[2,96,384]{2,1,0:T(8,128)(2,1)S(1)} %collective-permute-done.4.refs_1_, bf16[2,96,384]{2,1,0:T(8,128)(2,1)S(1)} %collective-permute-done.5.refs_2_, ...), custom_call_target="tpu_custom_call", output_to_operand_aliasing={{}: (5, {})} | custom-call | tf_op jit(solution)/shard_map/place_rows/pallas_call | solution.py:564
  (36 shorter events, 0.1 us)
Async XLA Ops:
  1.3 12.5 %collective-permute-start.3 = (bf16[2,16,64,128]{3,2,1,0:T(8,128)(2,1)S(1)}, bf16[2,16,64,128]{3,2,1,0:T(8,128)(2,1)}, u32[]{:S(2)}, u32[]{:S(2)}) collective-permute-start(bf16[2,16,64,128]{3,2,1,0:T(8,128)(2,1)S(1)} %rim_rows.7), channel_id=1, source_target_pairs={{1,0},{2,1},{3,2},{5,4},{6,5},{7,6},{9,8},{10,9},{11,10},{13,12},{... | collective-permute-start | bytes 1572872 | tf_op jit(solution)/shard_map/ppermute | solution.py:24
  4.5 13.8 %collective-permute-start = (bf16[2,16,64,128]{3,2,1,0:T(8,128)(2,1)S(1)}, bf16[2,16,64,128]{3,2,1,0:T(8,128)(2,1)}, u32[]{:S(2)}, u32[]{:S(2)}) collective-permute-start(bf16[2,16,64,128]{3,2,1,0:T(8,128)(2,1)S(1)} %rim_rows.4), channel_id=1, source_target_pairs={{1,0},{2,1},{3,2},{5,4},{6,5},{7,6},{9,8},{10,9},{11,10},{13,12},{... | collective-permute-start | bytes 1572872 | tf_op jit(solution)/shard_map/ppermute | solution.py:24
  7.8 5.3 %copy-start.14 = (s32[128,64]{0,1:T(8,128)S(1)}, s32[128,64]{0,1:T(8,128)}, u32[]{:S(2)}) copy-start(s32[128,64]{0,1:T(8,128)} %param.12) | copy-start | bytes 98308
  7.8 5.5 %copy-start.16 = (s32[8]{0:T(128)S(1)}, s32[8]{0:T(128)}, u32[]{:S(2)}) copy-start(s32[8]{0:T(128)} %param.11) | copy-start | bytes 100
  7.8 5.7 %copy-start.15 = (f32[2,64]{1,0:T(2,128)S(1)}, f32[2,64]{1,0:T(2,128)}, u32[]{:S(2)}) copy-start(f32[2,64]{1,0:T(2,128)} %param.8) | copy-start | bytes 1540
  7.8 6.0 %copy-start.11 = (bf16[256,768]{1,0:T(8,128)(2,1)S(1)}, bf16[256,768]{1,0:T(8,128)(2,1)}, u32[]{:S(2)}) copy-start(bf16[256,768]{1,0:T(8,128)(2,1)} %constant.33.clone.table_ref) | copy-start | bytes 1179652
  7.8 16.2 %collective-permute-start.1 = (bf16[2,16,64,128]{3,2,1,0:T(8,128)(2,1)S(1)}, bf16[2,16,64,128]{3,2,1,0:T(8,128)(2,1)}, u32[]{:S(2)}, u32[]{:S(2)}) collective-permute-start(bf16[2,16,64,128]{3,2,1,0:T(8,128)(2,1)S(1)} %rim_rows.5), channel_id=1, source_target_pairs={{1,0},{2,1},{3,2},{5,4},{6,5},{7,6},{9,8},{10,9},{11,10},{13,12},{... | collective-permute-start | bytes 1572872 | tf_op jit(solution)/shard_map/ppermute | solution.py:24
  11.2 18.3 %collective-permute-start.2 = (bf16[2,16,64,128]{3,2,1,0:T(8,128)(2,1)S(1)}, bf16[2,16,64,128]{3,2,1,0:T(8,128)(2,1)S(1)}, u32[]{:S(2)}, u32[]{:S(2)}) collective-permute-start(bf16[2,16,64,128]{3,2,1,0:T(8,128)(2,1)S(1)} %rim_rows.6), channel_id=1, source_target_pairs={{1,0},{2,1},{3,2},{5,4},{6,5},{7,6},{9,8},{10,9},{11,10},{13,12},{... | collective-permute-start | bytes 1572872 | tf_op jit(solution)/shard_map/ppermute | solution.py:24
  17.1 15.7 %copy-start = (bf16[128,32,128]{2,1,0:T(8,128)(2,1)}, bf16[128,32,128]{2,1,0:T(8,128)(2,1)S(1)}, u32[]{:S(2)}) copy-start(bf16[128,32,128]{2,1,0:T(8,128)(2,1)S(1)} %form_spectrum.7.refs_3_) | copy-start | bytes 3145732
  21.7 11.1 %copy-start.2 = (bf16[128,32,128]{2,1,0:T(8,128)(2,1)}, bf16[128,32,128]{2,1,0:T(8,128)(2,1)S(1)}, u32[]{:S(2)}) copy-start(bf16[128,32,128]{2,1,0:T(8,128)(2,1)S(1)} %form_spectrum.4.refs_0_) | copy-start | bytes 3145732
  27.3 5.5 %copy-start.4 = (bf16[128,32,128]{2,1,0:T(8,128)(2,1)}, bf16[128,32,128]{2,1,0:T(8,128)(2,1)S(1)}, u32[]{:S(2)}) copy-start(bf16[128,32,128]{2,1,0:T(8,128)(2,1)S(1)} %form_spectrum.5.refs_1_) | copy-start | bytes 3145732
  32.8 3.8 %copy-start.6 = (bf16[128,32,128]{2,1,0:T(8,128)(2,1)}, bf16[128,32,128]{2,1,0:T(8,128)(2,1)S(1)}, u32[]{:S(2)}) copy-start(bf16[128,32,128]{2,1,0:T(8,128)(2,1)S(1)} %form_spectrum.6.refs_2_) | copy-start | bytes 3145732
  36.6 75.6 %all-to-all-start.1 = ((bf16[32,3,128,128]{3,2,1,0:T(8,128)(2,1)}), bf16[32,3,128,128]{3,2,1,0:T(8,128)(2,1)S(1)}, u32[]{:S(2)}, u32[]{:S(2)}) async-start(bf16[32,3,128,128]{3,2,1,0:T(8,128)(2,1)} %bitcast.13), calls=%async_computation.1 | async-start | bytes 6291456 | tf_op jit(solution)/shard_map/all_to_all | solution.py:625
  41.4 75.5 %copy-start.13 = (s32[128,192]{0,1:T(8,128)S(1)}, s32[128,192]{0,1:T(8,128)}, u32[]{:S(2)}) copy-start(s32[128,192]{0,1:T(8,128)} %param.10) | copy-start | bytes 294916
  43.4 1.2 copy-start.1
  44.7 1.2 copy-start.3
  45.9 1.2 copy-start.5
  47.1 1.2 copy-start.7
  48.4 1.0 copy-start.8
  50.8 1.0 copy-start.12
  112.2 34.6 %all-to-all-start = ((bf16[32,1,128,128]{3,2,1,0:T(8,128)(2,1)}), bf16[32,1,128,128]{3,2,1,0:T(8,128)(2,1)}, u32[]{:S(2)}, u32[]{:S(2)}) async-start(bf16[32,1,128,128]{3,2,1,0:T(8,128)(2,1)} %bitcast.12), calls=%async_computation | async-start | bytes 2097152 | tf_op jit(solution)/shard_map/all_to_all | solution.py:625
  117.0 1.0 copy-start.9
  144.6 28.9 %collective-permute-start.7 = (bf16[6,96,384]{2,1,0:T(8,128)(2,1)S(1)}, bf16[6,96,384]{2,1,0:T(8,128)(2,1)S(1)}, u32[]{:S(2)}, u32[]{:S(2)}) collective-permute-start(bf16[6,96,384]{2,1,0:T(8,128)(2,1)S(1)} %get-tuple-element.24), channel_id=1, source_target_pairs={{0,1},{1,2},{2,3},{3,0},{4,5},{5,6},{6,7},{7,4},{8,9},{9,10},{10,1... | collective-permute-start | bytes 1327112 | tf_op jit(solution)/shard_map/ppermute | solution.py:299
  146.3 27.2 %collective-permute-start.8 = (bf16[6,96,384]{2,1,0:T(8,128)(2,1)S(1)}, bf16[6,96,384]{2,1,0:T(8,128)(2,1)S(1)}, u32[]{:S(2)}, u32[]{:S(2)}) collective-permute-start(bf16[6,96,384]{2,1,0:T(8,128)(2,1)S(1)} %get-tuple-element.25), channel_id=1, source_target_pairs={{0,2},{1,3},{2,0},{3,1},{4,6},{5,7},{6,4},{7,5},{8,10},{9,11},{10,... | collective-permute-start | bytes 1327112 | tf_op jit(solution)/shard_map/ppermute | solution.py:299
  146.5 27.0 %collective-permute-start.9 = (bf16[6,96,384]{2,1,0:T(8,128)(2,1)S(1)}, bf16[6,96,384]{2,1,0:T(8,128)(2,1)S(1)}, u32[]{:S(2)}, u32[]{:S(2)}) collective-permute-start(bf16[6,96,384]{2,1,0:T(8,128)(2,1)S(1)} %get-tuple-element.26), channel_id=1, source_target_pairs={{0,3},{1,0},{2,1},{3,2},{4,7},{5,4},{6,5},{7,6},{8,11},{9,8},{10,9... | collective-permute-start | bytes 1327112 | tf_op jit(solution)/shard_map/ppermute | solution.py:299
  146.8 1.0 copy-start.10
  170.8 8.0 %collective-permute-start.4 = (bf16[2,96,384]{2,1,0:T(8,128)(2,1)S(1)}, bf16[2,96,384]{2,1,0:T(8,128)(2,1)S(1)}, u32[]{:S(2)}, u32[]{:S(2)}) collective-permute-start(bf16[2,96,384]{2,1,0:T(8,128)(2,1)S(1)} %get-tuple-element.21), channel_id=1, source_target_pairs={{0,1},{1,2},{2,3},{3,0},{4,5},{5,6},{6,7},{7,4},{8,9},{9,10},{10,1... | collective-permute-start | bytes 442376 | tf_op jit(solution)/shard_map/ppermute | solution.py:299
  172.2 7.9 %collective-permute-start.5 = (bf16[2,96,384]{2,1,0:T(8,128)(2,1)S(1)}, bf16[2,96,384]{2,1,0:T(8,128)(2,1)S(1)}, u32[]{:S(2)}, u32[]{:S(2)}) collective-permute-start(bf16[2,96,384]{2,1,0:T(8,128)(2,1)S(1)} %get-tuple-element.22), channel_id=1, source_target_pairs={{0,2},{1,3},{2,0},{3,1},{4,6},{5,7},{6,4},{7,5},{8,10},{9,11},{10,... | collective-permute-start | bytes 442376 | tf_op jit(solution)/shard_map/ppermute | solution.py:299
  173.5 7.3 %collective-permute-start.6 = (bf16[2,96,384]{2,1,0:T(8,128)(2,1)S(1)}, bf16[2,96,384]{2,1,0:T(8,128)(2,1)S(1)}, u32[]{:S(2)}, u32[]{:S(2)}) collective-permute-start(bf16[2,96,384]{2,1,0:T(8,128)(2,1)S(1)} %get-tuple-element.23), channel_id=1, source_target_pairs={{0,3},{1,0},{2,1},{3,2},{4,7},{5,4},{6,5},{7,6},{8,11},{9,8},{10,9... | collective-permute-start | bytes 442376 | tf_op jit(solution)/shard_map/ppermute | solution.py:299

commit v9 on v7

--- a/solution.py
+++ b/solution.py
@@ -137,7 +137,7 @@
 def form_spectrum(rows, table, raw_echo, next_rows, chunk, chunks):
     _, ch_local, gate_rows, pulses = raw_echo.shape
     channels = ch_local // chunks
-    step = math.gcd(channels, 8)
+    step = math.gcd(channels, 16)
     steps = channels // step
     height = 2 * channels
     bins = table.shape[0] // 2

time: 181 us -> 181 us (level)
  transfers between devices with their start and end apart: 12 -> 12, of which waited for: 6 -> 6; matrix products, arithmetic and copies ran while one was open for 1% -> 1% of each run, Pallas kernels for 37% -> 38%
where the time goes in v9:
time: 181 us; the launch traced here: 180 us
  Pallas kernels  78.2 us (43%)
  waiting for transfers between devices  67.9 us (38%)
  starting transfers between devices  22.2 us (12%)
  local copies, waits for them, and re-layouts  11.3 us (6%)
    all_to_all x2, waiting for transfers between devices, local(): lax.all_to_all(array.reshape(owners * ranges, -1, *array.shape[2:]), axes...  60.4 us
    pallas_call x2, Pallas kernels, factor_slots(): pl.pallas_call(functools.partial(factor_kernel, first=first, share_slots=...  43.3 us
    pallas_call x4, Pallas kernels, form_spectrum(): pl.pallas_call(spectrum_kernel, out_shape=jax.ShapeDtypeStruct((bins, hei...  13.4 us
    unnamed x37, local copies, waits for them, and re-layouts  11.3 us
    all_to_all x2, starting transfers between devices, local(): lax.all_to_all(array.reshape(owners * ranges, -1, *array.shape[2:]), axes...  9.39 us
    ppermute x4, starting transfers between devices, shifted(): return lax.ppermute(array, axis, pairs)  7.86 us
    pallas_call x2, Pallas kernels, place_rows(): pl.pallas_call(functools.partial(place_kernel, first=first, share_slots=s...  7.5 us
    ppermute x4, waiting for transfers between devices, shifted(): return lax.ppermute(array, axis, pairs)  5.56 us
  transfers between devices with their start and end apart: 12, of which 6 were waited for; matrix products, arithmetic and copies ran while one was open for 1% of the time, Pallas kernels for 38%

profile of v9, /device:TPU:1, one launch (start us, length us, event | category | flops | bytes accessed | tf_op | source)
XLA Modules:
  0.0 180.3 jit_solution(1840001792821602482)
XLA Ops:
  0.0 1.3 rim_rows.7
  1.3 2.0 %collective-permute-start.3 = (bf16[2,16,64,128]{3,2,1,0:T(8,128)(2,1)S(1)}, bf16[2,16,64,128]{3,2,1,0:T(8,128)(2,1)}, u32[]{:S(2)}, u32[]{:S(2)}) collective-permute-start(bf16[2,16,64,128]{3,2,1,0:T(8,128)(2,1)S(1)} %rim_rows.7), channel_id=1, source_target_pairs={{1,0},{2,1},{3,2},{5,4},{6,5},{7,6},{9,8},{10,9},{11,10},{13,12},{... | collective-permute-start | bytes 1572872 | tf_op jit(solution)/shard_map/ppermute | solution.py:24
  3.3 1.3 rim_rows.4
  4.5 1.9 %collective-permute-start = (bf16[2,16,64,128]{3,2,1,0:T(8,128)(2,1)S(1)}, bf16[2,16,64,128]{3,2,1,0:T(8,128)(2,1)}, u32[]{:S(2)}, u32[]{:S(2)}) collective-permute-start(bf16[2,16,64,128]{3,2,1,0:T(8,128)(2,1)S(1)} %rim_rows.4), channel_id=1, source_target_pairs={{1,0},{2,1},{3,2},{5,4},{6,5},{7,6},{9,8},{10,9},{11,10},{13,12},{... | collective-permute-start | bytes 1572872 | tf_op jit(solution)/shard_map/ppermute | solution.py:24
  6.5 1.3 rim_rows.5
  7.8 2.1 %collective-permute-start.1 = (bf16[2,16,64,128]{3,2,1,0:T(8,128)(2,1)S(1)}, bf16[2,16,64,128]{3,2,1,0:T(8,128)(2,1)}, u32[]{:S(2)}, u32[]{:S(2)}) collective-permute-start(bf16[2,16,64,128]{3,2,1,0:T(8,128)(2,1)S(1)} %rim_rows.5), channel_id=1, source_target_pairs={{1,0},{2,1},{3,2},{5,4},{6,5},{7,6},{9,8},{10,9},{11,10},{13,12},{... | collective-permute-start | bytes 1572872 | tf_op jit(solution)/shard_map/ppermute | solution.py:24
  9.9 1.3 rim_rows.6
  11.2 1.9 %collective-permute-start.2 = (bf16[2,16,64,128]{3,2,1,0:T(8,128)(2,1)S(1)}, bf16[2,16,64,128]{3,2,1,0:T(8,128)(2,1)S(1)}, u32[]{:S(2)}, u32[]{:S(2)}) collective-permute-start(bf16[2,16,64,128]{3,2,1,0:T(8,128)(2,1)S(1)} %rim_rows.6), channel_id=1, source_target_pairs={{1,0},{2,1},{3,2},{5,4},{6,5},{7,6},{9,8},{10,9},{11,10},{13,12},{... | collective-permute-start | bytes 1572872 | tf_op jit(solution)/shard_map/ppermute | solution.py:24
  13.1 0.1 copy.17
  13.3 0.2 reduce-window.9
  13.5 0.1 pad_add_fusion.1.index_ref
  13.5 0.1 filter_rows.1.rows_ref
  13.7 0.1 pad_add_fusion.gates_ref
  13.8 3.4 %form_spectrum.7.refs_3_ = bf16[128,32,128]{2,1,0:T(8,128)(2,1)S(1)} custom-call(bf16[256,512]{1,0:T(8,128)(2,1)S(1)} %filter_rows.1.rows_ref, bf16[256,768]{1,0:T(8,128)(2,1)S(1)} %copy-done.11, f32[2,64,128,128]{3,2,1,0:T(8,128)} %own_ref.7, bf16[2,16,64,128]{3,2,1,0:T(8,128)(2,1)} %collective-permute-done.3.next_ref), custom_call_target="tpu_custom_call" | custom-call | flops 1342177280 | bytes 2097152 | tf_op jit(solution)/shard_map/form_spectrum/pallas_call | solution.py:144
  17.2 1.2 collective-permute-done.next_ref
  18.4 3.4 %form_spectrum.4.refs_0_ = bf16[128,32,128]{2,1,0:T(8,128)(2,1)S(1)} custom-call(bf16[256,512]{1,0:T(8,128)(2,1)S(1)} %filter_rows.1.rows_ref, bf16[256,768]{1,0:T(8,128)(2,1)S(1)} %copy-done.11, f32[2,64,128,128]{3,2,1,0:T(8,128)} %own_ref.7, bf16[2,16,64,128]{3,2,1,0:T(8,128)(2,1)} %collective-permute-done.next_ref), custom_call_target="tpu_custom_call" | custom-call | flops 1342177280 | bytes 2097152 | tf_op jit(solution)/shard_map/form_spectrum/pallas_call | solution.py:144
  21.8 2.2 %collective-permute-done.1.next_ref = bf16[2,16,64,128]{3,2,1,0:T(8,128)(2,1)} collective-permute-done((bf16[2,16,64,128]{3,2,1,0:T(8,128)(2,1)S(1)}, bf16[2,16,64,128]{3,2,1,0:T(8,128)(2,1)}, u32[]{:S(2)}, u32[]{:S(2)}) %collective-permute-start.1) | collective-permute-done | bytes 524320 | tf_op jit(solution)/shard_map/ppermute | solution.py:24
  24.0 3.4 %form_spectrum.5.refs_1_ = bf16[128,32,128]{2,1,0:T(8,128)(2,1)S(1)} custom-call(bf16[256,512]{1,0:T(8,128)(2,1)S(1)} %filter_rows.1.rows_ref, bf16[256,768]{1,0:T(8,128)(2,1)S(1)} %copy-done.11, f32[2,64,128,128]{3,2,1,0:T(8,128)} %own_ref.7, bf16[2,16,64,128]{3,2,1,0:T(8,128)(2,1)} %collective-permute-done.1.next_ref), custom_call_target="tpu_custom_call" | custom-call | flops 1342177280 | bytes 2097152 | tf_op jit(solution)/shard_map/form_spectrum/pallas_call | solution.py:144
  27.4 2.1 %collective-permute-done.2.next_ref = bf16[2,16,64,128]{3,2,1,0:T(8,128)(2,1)S(1)} collective-permute-done((bf16[2,16,64,128]{3,2,1,0:T(8,128)(2,1)S(1)}, bf16[2,16,64,128]{3,2,1,0:T(8,128)(2,1)S(1)}, u32[]{:S(2)}, u32[]{:S(2)}) %collective-permute-start.2) | collective-permute-done | bytes 524320 | tf_op jit(solution)/shard_map/ppermute | solution.py:24
  29.5 3.3 %form_spectrum.6.refs_2_ = bf16[128,32,128]{2,1,0:T(8,128)(2,1)S(1)} custom-call(bf16[256,512]{1,0:T(8,128)(2,1)S(1)} %filter_rows.1.rows_ref, bf16[256,768]{1,0:T(8,128)(2,1)S(1)} %copy-done.11, f32[2,64,128,128]{3,2,1,0:T(8,128)} %own_ref.7, bf16[2,16,64,128]{3,2,1,0:T(8,128)(2,1)S(1)} %collective-permute-done.2.next_ref), custom_call_target="tpu_custom_call" | custom-call | flops 1342177280 | bytes 2097152 | tf_op jit(solution)/shard_map/form_spectrum/pallas_call | solution.py:144
  32.8 3.8 %select_gates.3 = (bf16[8,12,128,128]{3,2,1,0:T(8,128)(2,1)}, s32[8,128]{1,0:T(8,128)}) custom-call(s32[18]{0:T(128)S(1)} %pad_add_fusion.1.index_ref, s32[128,128]{1,0:T(8,128)S(1)} %pad_add_fusion.gates_ref, bf16[128,32,128]{2,1,0:T(8,128)(2,1)S(1)} %form_spectrum.4.refs_0_, bf16[128,32,128]{2,1,0:T(8,128)(2,1)S(1)} %form_spectrum.5.refs_1_, ...), custom_call_target="tpu_custom_call" | custom-call | flops 805306368 | bytes 3145728 | tf_op jit(solution)/shard_map/select_gates/pallas_call | solution.py:214
  36.6 4.8 %all-to-all-start.1 = ((bf16[32,3,128,128]{3,2,1,0:T(8,128)(2,1)}), bf16[32,3,128,128]{3,2,1,0:T(8,128)(2,1)S(1)}, u32[]{:S(2)}, u32[]{:S(2)}) async-start(bf16[32,3,128,128]{3,2,1,0:T(8,128)(2,1)} %bitcast.13), calls=%async_computation.1 | async-start | bytes 6291456 | tf_op jit(solution)/shard_map/all_to_all | solution.py:625
  41.4 2.0 %copy.24.refs_4_.weights_ref = bf16[2,512,192]{2,1,0:T(8,128)(2,1)} copy(bf16[2,512,192]{1,2,0:T(8,128)(2,1)} %param.9) | data formatting | bytes 786432 | tf_op args[2]
  43.4 1.2 copy-done.1
  44.7 1.2 copy-done.3
  45.9 1.2 copy-done.5
  47.1 1.2 copy-done.7
  48.3 1.0 copy-done.8
  49.4 1.4 select_gates.2
  50.9 1.0 copy-done.12
  51.8 60.4 %all-to-all-done.1 = bf16[32,3,128,128]{3,2,1,0:T(8,128)(2,1)S(1)} async-done(((bf16[32,3,128,128]{3,2,1,0:T(8,128)(2,1)}), bf16[32,3,128,128]{3,2,1,0:T(8,128)(2,1)S(1)}, u32[]{:S(2)}, u32[]{:S(2)}) %all-to-all-start.1) | async-done | bytes 3145760 | tf_op jit(solution)/shard_map/all_to_all | solution.py:625
  112.2 4.6 %all-to-all-start = ((bf16[32,1,128,128]{3,2,1,0:T(8,128)(2,1)}), bf16[32,1,128,128]{3,2,1,0:T(8,128)(2,1)}, u32[]{:S(2)}, u32[]{:S(2)}) async-start(bf16[32,1,128,128]{3,2,1,0:T(8,128)(2,1)} %bitcast.12), calls=%async_computation | async-start | bytes 2097152 | tf_op jit(solution)/shard_map/all_to_all | solution.py:625
  116.9 0.1 copy.25.pivots_ref
  117.0 1.0 copy-done.9
  118.0 1.4 form_beams.2.beams_ref
  119.4 23.7 %factor_slots.2 = (bf16[6,96,384]{2,1,0:T(8,128)(2,1)S(1)}, bf16[6,96,384]{2,1,0:T(8,128)(2,1)S(1)}, bf16[6,96,384]{2,1,0:T(8,128)(2,1)S(1)}, bf16[6,96,384]{2,1,0:T(8,128)(2,1)S(1)}) custom-call(s32[18]{0:T(128)S(1)} %pad_add_fusion.1.index_ref, s32[128,192]{1,0:T(8,128)S(1)} %copy.25.pivots_ref, bf16[4,3,384,128]{3,2,1,0:T(8,128)(2,1)S(1)} %form_beams.2.beams_ref), custom_call_target="tpu_custom_call" | custom-call | flops 339738624 | bytes 1179648 | tf_op jit(solution)/shard_map/factor_slots/pallas_call | solution.py:509
  143.2 1.7 collective-permute-start.7
  144.8 0.2 collective-permute-start.8
  145.1 0.3 collective-permute-start.9
  145.4 1.0 copy-done.10
  146.4 2.1 %form_beams.3.beams_ref = bf16[4,1,384,128]{3,2,1,0:T(8,128)(2,1)S(1)} custom-call(bf16[2,512,192]{2,1,0:T(8,128)(2,1)S(1)} %copy-done.10, bf16[8,4,1,128,128]{4,3,2,1,0:T(8,128)(2,1)} %bitcast.6.arrived_ref, bf16[6,96,384]{2,1,0:T(8,128)(2,1)S(1)} %get-tuple-element.19.refs_0_), custom_call_target="tpu_custom_call" | custom-call | flops 402653184 | bytes 1048576 | tf_op jit(solution)/shard_map/form_beams/pallas_call | solution.py:278
  148.5 19.6 %factor_slots.3 = (bf16[2,96,384]{2,1,0:T(8,128)(2,1)S(1)}, bf16[2,96,384]{2,1,0:T(8,128)(2,1)S(1)}, bf16[2,96,384]{2,1,0:T(8,128)(2,1)S(1)}, bf16[2,96,384]{2,1,0:T(8,128)(2,1)S(1)}) custom-call(s32[18]{0:T(128)S(1)} %pad_add_fusion.1.index_ref, s32[128,192]{1,0:T(8,128)S(1)} %copy.25.pivots_ref, bf16[4,1,384,128]{3,2,1,0:T(8,128)(2,1)S(1)} %form_beams.3.beams_ref), custom_call_target="tpu_custom_call" | custom-call | flops 113246208 | bytes 393216 | tf_op jit(solution)/shard_map/factor_slots/pallas_call | solution.py:509
  168.1 1.5 collective-permute-start.4
  169.6 1.3 collective-permute-start.5
  170.8 5.3 %place_rows.2.refs_4_ = f32[32,96,384]{2,1,0:T(8,128)} custom-call(s32[18]{0:T(128)S(1)} %pad_add_fusion.1.index_ref, bf16[6,96,384]{2,1,0:T(8,128)(2,1)S(1)} %get-tuple-element.19.refs_0_, bf16[6,96,384]{2,1,0:T(8,128)(2,1)S(1)} %collective-permute-done.7.refs_1_, bf16[6,96,384]{2,1,0:T(8,128)(2,1)S(1)} %collective-permute-done.8.refs_2_, ...), custom_call_target="tpu_custom_call" | custom-call | tf_op jit(solution)/shard_map/place_rows/pallas_call | solution.py:564
  176.1 1.3 collective-permute-done.5.refs_2_
  177.5 0.6 collective-permute-done.6.refs_3_
  178.1 2.2 %place_rows.3 = f32[32,96,384]{2,1,0:T(8,128)} custom-call(s32[18]{0:T(128)S(1)} %pad_add_fusion.1.index_ref, bf16[2,96,384]{2,1,0:T(8,128)(2,1)S(1)} %get-tuple-element.20.refs_0_, bf16[2,96,384]{2,1,0:T(8,128)(2,1)S(1)} %collective-permute-done.4.refs_1_, bf16[2,96,384]{2,1,0:T(8,128)(2,1)S(1)} %collective-permute-done.5.refs_2_, ...), custom_call_target="tpu_custom_call", output_to_operand_aliasing={{}: (5, {})} | custom-call | tf_op jit(solution)/shard_map/place_rows/pallas_call | solution.py:564
  (36 shorter events, 0.1 us)
Async XLA Ops:
  1.3 12.5 %collective-permute-start.3 = (bf16[2,16,64,128]{3,2,1,0:T(8,128)(2,1)S(1)}, bf16[2,16,64,128]{3,2,1,0:T(8,128)(2,1)}, u32[]{:S(2)}, u32[]{:S(2)}) collective-permute-start(bf16[2,16,64,128]{3,2,1,0:T(8,128)(2,1)S(1)} %rim_rows.7), channel_id=1, source_target_pairs={{1,0},{2,1},{3,2},{5,4},{6,5},{7,6},{9,8},{10,9},{11,10},{13,12},{... | collective-permute-start | bytes 1572872 | tf_op jit(solution)/shard_map/ppermute | solution.py:24
  4.5 13.8 %collective-permute-start = (bf16[2,16,64,128]{3,2,1,0:T(8,128)(2,1)S(1)}, bf16[2,16,64,128]{3,2,1,0:T(8,128)(2,1)}, u32[]{:S(2)}, u32[]{:S(2)}) collective-permute-start(bf16[2,16,64,128]{3,2,1,0:T(8,128)(2,1)S(1)} %rim_rows.4), channel_id=1, source_target_pairs={{1,0},{2,1},{3,2},{5,4},{6,5},{7,6},{9,8},{10,9},{11,10},{13,12},{... | collective-permute-start | bytes 1572872 | tf_op jit(solution)/shard_map/ppermute | solution.py:24
  7.8 5.3 %copy-start.14 = (s32[128,64]{0,1:T(8,128)S(1)}, s32[128,64]{0,1:T(8,128)}, u32[]{:S(2)}) copy-start(s32[128,64]{0,1:T(8,128)} %param.12) | copy-start | bytes 98308
  7.8 5.5 %copy-start.16 = (s32[8]{0:T(128)S(1)}, s32[8]{0:T(128)}, u32[]{:S(2)}) copy-start(s32[8]{0:T(128)} %param.11) | copy-start | bytes 100
  7.8 5.7 %copy-start.15 = (f32[2,64]{1,0:T(2,128)S(1)}, f32[2,64]{1,0:T(2,128)}, u32[]{:S(2)}) copy-start(f32[2,64]{1,0:T(2,128)} %param.8) | copy-start | bytes 1540
  7.8 6.0 %copy-start.11 = (bf16[256,768]{1,0:T(8,128)(2,1)S(1)}, bf16[256,768]{1,0:T(8,128)(2,1)}, u32[]{:S(2)}) copy-start(bf16[256,768]{1,0:T(8,128)(2,1)} %constant.33.clone.table_ref) | copy-start | bytes 1179652
  7.8 16.2 %collective-permute-start.1 = (bf16[2,16,64,128]{3,2,1,0:T(8,128)(2,1)S(1)}, bf16[2,16,64,128]{3,2,1,0:T(8,128)(2,1)}, u32[]{:S(2)}, u32[]{:S(2)}) collective-permute-start(bf16[2,16,64,128]{3,2,1,0:T(8,128)(2,1)S(1)} %rim_rows.5), channel_id=1, source_target_pairs={{1,0},{2,1},{3,2},{5,4},{6,5},{7,6},{9,8},{10,9},{11,10},{13,12},{... | collective-permute-start | bytes 1572872 | tf_op jit(solution)/shard_map/ppermute | solution.py:24
  11.2 18.3 %collective-permute-start.2 = (bf16[2,16,64,128]{3,2,1,0:T(8,128)(2,1)S(1)}, bf16[2,16,64,128]{3,2,1,0:T(8,128)(2,1)S(1)}, u32[]{:S(2)}, u32[]{:S(2)}) collective-permute-start(bf16[2,16,64,128]{3,2,1,0:T(8,128)(2,1)S(1)} %rim_rows.6), channel_id=1, source_target_pairs={{1,0},{2,1},{3,2},{5,4},{6,5},{7,6},{9,8},{10,9},{11,10},{13,12},{... | collective-permute-start | bytes 1572872 | tf_op jit(solution)/shard_map/ppermute | solution.py:24
  17.2 15.6 %copy-start = (bf16[128,32,128]{2,1,0:T(8,128)(2,1)}, bf16[128,32,128]{2,1,0:T(8,128)(2,1)S(1)}, u32[]{:S(2)}) copy-start(bf16[128,32,128]{2,1,0:T(8,128)(2,1)S(1)} %form_spectrum.7.refs_3_) | copy-start | bytes 3145732
  21.8 11.1 %copy-start.2 = (bf16[128,32,128]{2,1,0:T(8,128)(2,1)}, bf16[128,32,128]{2,1,0:T(8,128)(2,1)S(1)}, u32[]{:S(2)}) copy-start(bf16[128,32,128]{2,1,0:T(8,128)(2,1)S(1)} %form_spectrum.4.refs_0_) | copy-start | bytes 3145732
  27.4 5.5 %copy-start.4 = (bf16[128,32,128]{2,1,0:T(8,128)(2,1)}, bf16[128,32,128]{2,1,0:T(8,128)(2,1)S(1)}, u32[]{:S(2)}) copy-start(bf16[128,32,128]{2,1,0:T(8,128)(2,1)S(1)} %form_spectrum.5.refs_1_) | copy-start | bytes 3145732
  32.8 3.8 %copy-start.6 = (bf16[128,32,128]{2,1,0:T(8,128)(2,1)}, bf16[128,32,128]{2,1,0:T(8,128)(2,1)S(1)}, u32[]{:S(2)}) copy-start(bf16[128,32,128]{2,1,0:T(8,128)(2,1)S(1)} %form_spectrum.6.refs_2_) | copy-start | bytes 3145732
  36.6 75.6 %all-to-all-start.1 = ((bf16[32,3,128,128]{3,2,1,0:T(8,128)(2,1)}), bf16[32,3,128,128]{3,2,1,0:T(8,128)(2,1)S(1)}, u32[]{:S(2)}, u32[]{:S(2)}) async-start(bf16[32,3,128,128]{3,2,1,0:T(8,128)(2,1)} %bitcast.13), calls=%async_computation.1 | async-start | bytes 6291456 | tf_op jit(solution)/shard_map/all_to_all | solution.py:625
  41.4 75.5 %copy-start.13 = (s32[128,192]{0,1:T(8,128)S(1)}, s32[128,192]{0,1:T(8,128)}, u32[]{:S(2)}) copy-start(s32[128,192]{0,1:T(8,128)} %param.10) | copy-start | bytes 294916
  43.4 1.2 copy-start.1
  44.7 1.2 copy-start.3
  45.9 1.2 copy-start.5
  47.1 1.2 copy-start.7
  48.3 1.0 copy-start.8
  50.8 1.0 copy-start.12
  112.2 33.2 %all-to-all-start = ((bf16[32,1,128,128]{3,2,1,0:T(8,128)(2,1)}), bf16[32,1,128,128]{3,2,1,0:T(8,128)(2,1)}, u32[]{:S(2)}, u32[]{:S(2)}) async-start(bf16[32,1,128,128]{3,2,1,0:T(8,128)(2,1)} %bitcast.12), calls=%async_computation | async-start | bytes 2097152 | tf_op jit(solution)/shard_map/all_to_all | solution.py:625
  117.0 1.0 copy-start.9
  143.2 27.7 %collective-permute-start.7 = (bf16[6,96,384]{2,1,0:T(8,128)(2,1)S(1)}, bf16[6,96,384]{2,1,0:T(8,128)(2,1)S(1)}, u32[]{:S(2)}, u32[]{:S(2)}) collective-permute-start(bf16[6,96,384]{2,1,0:T(8,128)(2,1)S(1)} %get-tuple-element.24), channel_id=1, source_target_pairs={{0,1},{1,2},{2,3},{3,0},{4,5},{5,6},{6,7},{7,4},{8,9},{9,10},{10,1... | collective-permute-start | bytes 1327112 | tf_op jit(solution)/shard_map/ppermute | solution.py:299
  144.8 26.0 %collective-permute-start.8 = (bf16[6,96,384]{2,1,0:T(8,128)(2,1)S(1)}, bf16[6,96,384]{2,1,0:T(8,128)(2,1)S(1)}, u32[]{:S(2)}, u32[]{:S(2)}) collective-permute-start(bf16[6,96,384]{2,1,0:T(8,128)(2,1)S(1)} %get-tuple-element.25), channel_id=1, source_target_pairs={{0,2},{1,3},{2,0},{3,1},{4,6},{5,7},{6,4},{7,5},{8,10},{9,11},{10,... | collective-permute-start | bytes 1327112 | tf_op jit(solution)/shard_map/ppermute | solution.py:299
  145.1 25.8 %collective-permute-start.9 = (bf16[6,96,384]{2,1,0:T(8,128)(2,1)S(1)}, bf16[6,96,384]{2,1,0:T(8,128)(2,1)S(1)}, u32[]{:S(2)}, u32[]{:S(2)}) collective-permute-start(bf16[6,96,384]{2,1,0:T(8,128)(2,1)S(1)} %get-tuple-element.26), channel_id=1, source_target_pairs={{0,3},{1,0},{2,1},{3,2},{4,7},{5,4},{6,5},{7,6},{8,11},{9,8},{10,9... | collective-permute-start | bytes 1327112 | tf_op jit(solution)/shard_map/ppermute | solution.py:299
  145.4 1.0 copy-start.10
  168.1 8.0 %collective-permute-start.4 = (bf16[2,96,384]{2,1,0:T(8,128)(2,1)S(1)}, bf16[2,96,384]{2,1,0:T(8,128)(2,1)S(1)}, u32[]{:S(2)}, u32[]{:S(2)}) collective-permute-start(bf16[2,96,384]{2,1,0:T(8,128)(2,1)S(1)} %get-tuple-element.21), channel_id=1, source_target_pairs={{0,1},{1,2},{2,3},{3,0},{4,5},{5,6},{6,7},{7,4},{8,9},{9,10},{10,1... | collective-permute-start | bytes 442376 | tf_op jit(solution)/shard_map/ppermute | solution.py:299
  169.6 7.9 %collective-permute-start.5 = (bf16[2,96,384]{2,1,0:T(8,128)(2,1)S(1)}, bf16[2,96,384]{2,1,0:T(8,128)(2,1)S(1)}, u32[]{:S(2)}, u32[]{:S(2)}) collective-permute-start(bf16[2,96,384]{2,1,0:T(8,128)(2,1)S(1)} %get-tuple-element.22), channel_id=1, source_target_pairs={{0,2},{1,3},{2,0},{3,1},{4,6},{5,7},{6,4},{7,5},{8,10},{9,11},{10,... | collective-permute-start | bytes 442376 | tf_op jit(solution)/shard_map/ppermute | solution.py:299
  170.8 7.3 %collective-permute-start.6 = (bf16[2,96,384]{2,1,0:T(8,128)(2,1)S(1)}, bf16[2,96,384]{2,1,0:T(8,128)(2,1)S(1)}, u32[]{:S(2)}, u32[]{:S(2)}) collective-permute-start(bf16[2,96,384]{2,1,0:T(8,128)(2,1)S(1)} %get-tuple-element.23), channel_id=1, source_target_pairs={{0,3},{1,0},{2,1},{3,2},{4,7},{5,4},{6,5},{7,6},{8,11},{9,8},{10,9... | collective-permute-start | bytes 442376 | tf_op jit(solution)/shard_map/ppermute | solution.py:299
